TPU v7x, 32 devices: a whole 2x2x4 slice. The times are simulated.
32 devices in a mesh: dp: 32 (over z, y, x, core).
Axes of the slice: x: 2, y: 2, z: 4, core: 2. Of those that a mesh axis runs over, the one named last changes fastest.
Arguments:
- inputs: bfloat16 [64, 1024, 512], P('dp'), may hold values from -6 to 6
- lengths: int32 [64], P('dp'), may hold values from 128 to 1024, as said below
- memory: bfloat16 [20, 512], P(None, 'dp'), may hold values from -6 to 6
- query_weight: bfloat16 [512, 512], P('dp'), may hold values from -0.25 to 0.25
- query_bias: bfloat16 [512], P('dp'), may hold values from -3 to 3
- key_weight: bfloat16 [512, 512], P('dp'), may hold values from -0.25 to 0.25
- value_weight: bfloat16 [512, 512], P('dp'), may hold values from -0.25 to 0.25
- value_bias: bfloat16 [512], P('dp'), may hold values from -3 to 3
- output_weight: bfloat16 [512, 512], P('dp'), may hold values from -0.5 to 0.5
- output_bias: bfloat16 [512], P('dp'), may hold values from -3 to 3
- first_gain: bfloat16 [512], P('dp'), may hold values from 0.099609375 to 1.8984375
- first_shift: bfloat16 [512], P('dp'), may hold values from -1.75 to 1.75
- up_weight: bfloat16 [512, 2048], P('dp'), may hold values from -0.25 to 0.25
- up_bias: bfloat16 [2048], P('dp'), may hold values from -3 to 3
- down_weight: bfloat16 [2048, 512], P('dp'), may hold values from -0.125 to 0.125
- down_bias: bfloat16 [512], P('dp'), may hold values from -3 to 3
- second_gain: bfloat16 [512], P('dp'), may hold values from 0.099609375 to 1.8984375
- second_shift: bfloat16 [512], P('dp'), may hold values from -1.75 to 1.75
- cotangent: bfloat16 [64, 1024, 512], P('dp'), may hold values from -6 to 6
Outputs:
- layer_out: bfloat16 [64, 1024, 512], P('dp')
- input_grad: bfloat16 [64, 1024, 512], P('dp')
- memory_grad: float32 [20, 512], P(None, 'dp')
- query_weight_grad: float32 [512, 512], P('dp')
- query_bias_grad: float32 [512], P('dp')
- key_weight_grad: float32 [512, 512], P('dp')
- value_weight_grad: float32 [512, 512], P('dp')
- value_bias_grad: float32 [512], P('dp')
- output_weight_grad: float32 [512, 512], P('dp')
- output_bias_grad: float32 [512], P('dp')
- first_gain_grad: float32 [512], P('dp')
- first_shift_grad: float32 [512], P('dp')
- up_weight_grad: float32 [512, 2048], P('dp')
- up_bias_grad: float32 [2048], P('dp')
- down_weight_grad: float32 [2048, 512], P('dp')
- down_bias_grad: float32 [512], P('dp')
- second_gain_grad: float32 [512], P('dp')
- second_shift_grad: float32 [512], P('dp')
Inputs may be any that keep to these rules, and one draw needn't show every extreme that they name: `lengths`: the number of real tokens of each sequence; later slots are padding that no query attends to, memory tokens are always visible, and some sequence has all 1024 tokens real.
All inputs are finite; a program needn't handle non-finite values.
Results may differ from a plain program's by a relative error of at most 0.013.
Values may be sent and summed in bfloat16 or wider, within the bound.
A program may use at most 256 MiB of HBM per device.

v0:
```python
import jax
import jax.numpy as jnp
from jax import lax
from jax.sharding import PartitionSpec as P

HEADS = 8
HEAD_DIM = 64


EPSILON = 1e-05


def norm_forward(value, gain, shift):
    center = value - jnp.mean(value, -1, keepdims=True)
    inverse = lax.rsqrt(jnp.mean(center * center, -1, keepdims=True) + EPSILON)
    normed = center * inverse
    return (normed * gain + shift, normed, inverse)


def norm_backward(grad, normed, inverse, gain):
    scaled = grad * gain
    value_grad = inverse * (
        scaled
        - jnp.mean(scaled, -1, keepdims=True)
        - normed * jnp.mean(scaled * normed, -1, keepdims=True)
    )
    return (value_grad, jnp.sum(grad * normed, 0), jnp.sum(grad, 0))


def matmul(left, right):
    return jnp.dot(left, right, preferred_element_type=jnp.float32)


def outer_sum(left, right):
    return jnp.einsum("ti,tj->ij", left, right, preferred_element_type=jnp.float32)


def back_mul(grad, weight):
    return jnp.einsum("tj,ij->ti", grad, weight, preferred_element_type=jnp.float32)


def block_scores(query_block, all_keys, visible):
    scores = jnp.einsum("qhd,khd->hqk", query_block, all_keys, preferred_element_type=jnp.float32)
    return jnp.where(visible[None, None, :], scores, -1e30)


def attend_sequence(item, mem_keys, mem_values):
    queries, keyed, valued, length = item
    rows, width = queries.shape
    all_keys = jnp.concatenate([mem_keys, keyed], 0).reshape(-1, HEADS, width // HEADS)
    all_values = jnp.concatenate([mem_values, valued], 0).reshape(-1, HEADS, width // HEADS)
    visible = jnp.arange(all_keys.shape[0]) < mem_keys.shape[0] + length
    block = min(512, rows)
    pieces = []
    stats = []
    for start in range(0, rows, block):
        query_block = queries[start : start + block].reshape(block, HEADS, width // HEADS)
        scores = block_scores(query_block, all_keys, visible)
        top = jnp.max(scores, -1, keepdims=True)
        expo = jnp.exp(scores - top)
        total = jnp.sum(expo, -1, keepdims=True)
        probs = expo / total
        stats.append((top + jnp.log(total))[..., 0])
        mixed = jnp.einsum(
            "hqk,khd->qhd",
            probs.astype(jnp.bfloat16),
            all_values,
            preferred_element_type=jnp.float32,
        )
        pieces.append(mixed.reshape(block, width).astype(jnp.bfloat16))
    return (jnp.concatenate(pieces, 0), jnp.concatenate(stats, 1))


def attend_backward(item, mem_keys, mem_values):
    queries, keyed, valued, length, stats, out_grad = item
    rows, width = queries.shape
    head_dim = width // HEADS
    all_keys = jnp.concatenate([mem_keys, keyed], 0).reshape(-1, HEADS, head_dim)
    all_values = jnp.concatenate([mem_values, valued], 0).reshape(-1, HEADS, head_dim)
    key_count = all_keys.shape[0]
    visible = jnp.arange(key_count) < mem_keys.shape[0] + length
    block = min(512, rows)
    key_grad = jnp.zeros((key_count, HEADS, head_dim), jnp.float32)
    value_grad = jnp.zeros((key_count, HEADS, head_dim), jnp.float32)
    query_grads = []
    for start in range(0, rows, block):
        query_block = queries[start : start + block].reshape(block, HEADS, head_dim)
        grad_block = out_grad[start : start + block].reshape(block, HEADS, head_dim)
        scores = block_scores(query_block, all_keys, visible)
        probs = jnp.exp(scores - stats[:, start : start + block, None])
        weights_low = probs.astype(jnp.bfloat16)
        prob_grad = jnp.einsum(
            "qhd,khd->hqk", grad_block, all_values, preferred_element_type=jnp.float32
        )
        centred = probs * (prob_grad - jnp.sum(prob_grad * probs, -1, keepdims=True))
        score_grad = centred.astype(jnp.bfloat16)
        query_grads.append(
            jnp.einsum("hqk,khd->qhd", score_grad, all_keys, preferred_element_type=jnp.float32)
            .reshape(block, width)
            .astype(jnp.bfloat16)
        )
        key_grad = key_grad + jnp.einsum(
            "hqk,qhd->khd", score_grad, query_block, preferred_element_type=jnp.float32
        )
        value_grad = value_grad + jnp.einsum(
            "hqk,qhd->khd", weights_low, grad_block, preferred_element_type=jnp.float32
        )
    key_grad = key_grad.reshape(key_count, width).astype(jnp.bfloat16)
    value_grad = value_grad.reshape(key_count, width).astype(jnp.bfloat16)
    mem_rows = mem_keys.shape[0]
    return (
        jnp.concatenate(query_grads, 0),
        key_grad[mem_rows:],
        value_grad[mem_rows:],
        key_grad[:mem_rows],
        value_grad[:mem_rows],
    )


def project(flat, memory, query_weight, query_bias, key_weight, value_weight, value_bias, scale):
    queries = ((matmul(flat, query_weight) + query_bias.astype(jnp.float32)) * scale).astype(
        jnp.bfloat16
    )
    keyed = matmul(flat, key_weight).astype(jnp.bfloat16)
    valued = (matmul(flat, value_weight) + value_bias.astype(jnp.float32)).astype(jnp.bfloat16)
    mem_keys = matmul(memory, key_weight).astype(jnp.bfloat16)
    mem_values = (matmul(memory, value_weight) + value_bias.astype(jnp.float32)).astype(
        jnp.bfloat16
    )
    return (queries, keyed, valued, mem_keys, mem_values)


def feed_forward(hidden, up_weight, up_bias, down_weight, down_bias, second_gain, second_shift):
    hidden_low = hidden.astype(jnp.bfloat16)
    inner = matmul(hidden_low, up_weight) + up_bias.astype(jnp.float32)
    acted = jax.nn.gelu(inner).astype(jnp.bfloat16)
    outer = matmul(acted, down_weight) + down_bias.astype(jnp.float32)
    result, normed, inverse = norm_forward(
        hidden + outer, second_gain.astype(jnp.float32), second_shift.astype(jnp.float32)
    )
    return (result, normed, inverse, hidden_low, inner, acted)


def on_device(
    inputs,
    lengths,
    memory,
    query_weight,
    query_bias,
    key_weight,
    value_weight,
    value_bias,
    output_weight,
    output_bias,
    first_gain,
    first_shift,
    up_weight,
    up_bias,
    down_weight,
    down_bias,
    second_gain,
    second_shift,
    cotangent,
):
    seqs, length, width = inputs.shape
    scale = HEAD_DIM ** (-0.5)
    full = (
        lax.all_gather(memory, "dp", axis=1, tiled=True),
        lax.all_gather(query_weight, "dp", axis=0, tiled=True),
        lax.all_gather(query_bias, "dp", axis=0, tiled=True),
        lax.all_gather(key_weight, "dp", axis=0, tiled=True),
        lax.all_gather(value_weight, "dp", axis=0, tiled=True),
        lax.all_gather(value_bias, "dp", axis=0, tiled=True),
        lax.all_gather(output_weight, "dp", axis=0, tiled=True),
        lax.all_gather(output_bias, "dp", axis=0, tiled=True),
        lax.all_gather(first_gain, "dp", axis=0, tiled=True),
        lax.all_gather(first_shift, "dp", axis=0, tiled=True),
        lax.all_gather(up_weight, "dp", axis=0, tiled=True),
        lax.all_gather(up_bias, "dp", axis=0, tiled=True),
        lax.all_gather(down_weight, "dp", axis=0, tiled=True),
        lax.all_gather(down_bias, "dp", axis=0, tiled=True),
        lax.all_gather(second_gain, "dp", axis=0, tiled=True),
        lax.all_gather(second_shift, "dp", axis=0, tiled=True),
    )
    (
        mem_full,
        wq_full,
        bq_full,
        wk_full,
        wv_full,
        bv_full,
        wo_full,
        bo_full,
        ga_full,
        sa_full,
        wu_full,
        bu_full,
        wd_full,
        bd_full,
        gb_full,
        sb_full,
    ) = full
    flat = inputs.reshape(seqs * length, width)
    queries, keyed, valued, mem_keys, mem_values = project(
        flat, mem_full, wq_full, bq_full, wk_full, wv_full, bv_full, scale
    )
    attended, stats = lax.map(
        lambda item: attend_sequence(item, mem_keys, mem_values),
        (
            queries.reshape(seqs, length, width),
            keyed.reshape(seqs, length, width),
            valued.reshape(seqs, length, width),
            lengths,
        ),
    )
    attended = attended.reshape(seqs * length, width)
    branch = matmul(attended, wo_full) + bo_full.astype(jnp.float32)
    hidden, first_normed, first_inverse = norm_forward(
        flat.astype(jnp.float32) + branch, ga_full.astype(jnp.float32), sa_full.astype(jnp.float32)
    )
    result = feed_forward(hidden, wu_full, bu_full, wd_full, bd_full, gb_full, sb_full)[0]
    layer_out = result.astype(jnp.bfloat16).reshape(seqs, length, width)
    again = (
        lax.all_gather(memory, "dp", axis=1, tiled=True),
        lax.all_gather(query_weight, "dp", axis=0, tiled=True),
        lax.all_gather(query_bias, "dp", axis=0, tiled=True),
        lax.all_gather(key_weight, "dp", axis=0, tiled=True),
        lax.all_gather(value_weight, "dp", axis=0, tiled=True),
        lax.all_gather(value_bias, "dp", axis=0, tiled=True),
        lax.all_gather(output_weight, "dp", axis=0, tiled=True),
        lax.all_gather(output_bias, "dp", axis=0, tiled=True),
        lax.all_gather(first_gain, "dp", axis=0, tiled=True),
        lax.all_gather(first_shift, "dp", axis=0, tiled=True),
        lax.all_gather(up_weight, "dp", axis=0, tiled=True),
        lax.all_gather(up_bias, "dp", axis=0, tiled=True),
        lax.all_gather(down_weight, "dp", axis=0, tiled=True),
        lax.all_gather(down_bias, "dp", axis=0, tiled=True),
        lax.all_gather(second_gain, "dp", axis=0, tiled=True),
        lax.all_gather(second_shift, "dp", axis=0, tiled=True),
    )
    (
        mem_full,
        wq_full,
        bq_full,
        wk_full,
        wv_full,
        bv_full,
        wo_full,
        bo_full,
        ga_full,
        sa_full,
        wu_full,
        bu_full,
        wd_full,
        bd_full,
        gb_full,
        sb_full,
    ) = again
    grad_out = cotangent.reshape(seqs * length, width).astype(jnp.float32)
    _, second_normed, second_inverse, hidden_low, inner, acted = feed_forward(
        hidden, wu_full, bu_full, wd_full, bd_full, gb_full, sb_full
    )
    res_grad, second_gain_grad, second_shift_grad = norm_backward(
        grad_out, second_normed, second_inverse, gb_full.astype(jnp.float32)
    )
    outer_grad = res_grad.astype(jnp.bfloat16)
    down_weight_grad = outer_sum(acted, outer_grad)
    down_bias_grad = jnp.sum(outer_grad.astype(jnp.float32), 0)
    acted_grad = back_mul(outer_grad, wd_full)
    _, gelu_pull = jax.vjp(jax.nn.gelu, inner)
    inner_grad = gelu_pull(acted_grad)[0].astype(jnp.bfloat16)
    up_weight_grad = outer_sum(hidden_low, inner_grad)
    up_bias_grad = jnp.sum(inner_grad.astype(jnp.float32), 0)
    hidden_grad = res_grad + back_mul(inner_grad, wu_full)
    first_grad, first_gain_grad, first_shift_grad = norm_backward(
        hidden_grad, first_normed, first_inverse, ga_full.astype(jnp.float32)
    )
    branch_grad = first_grad.astype(jnp.bfloat16)
    output_weight_grad = outer_sum(attended, branch_grad)
    output_bias_grad = jnp.sum(branch_grad.astype(jnp.float32), 0)
    attended_grad = back_mul(branch_grad, wo_full).astype(jnp.bfloat16)
    queries, keyed, valued, mem_keys, mem_values = project(
        flat, mem_full, wq_full, bq_full, wk_full, wv_full, bv_full, scale
    )
    query_grad, key_grad, value_grad, mem_key_grad, mem_value_grad = lax.map(
        lambda item: attend_backward(item, mem_keys, mem_values),
        (
            queries.reshape(seqs, length, width),
            keyed.reshape(seqs, length, width),
            valued.reshape(seqs, length, width),
            lengths,
            stats,
            attended_grad.reshape(seqs, length, width),
        ),
    )
    query_grad = query_grad.reshape(seqs * length, width)
    key_grad = key_grad.reshape(seqs * length, width)
    value_grad = value_grad.reshape(seqs * length, width)
    query_weight_grad = outer_sum(flat, query_grad) * scale
    query_bias_grad = jnp.sum(query_grad.astype(jnp.float32), 0) * scale
    key_weight_grad = outer_sum(flat, key_grad) + jnp.einsum(
        "smj,mi->ij", mem_key_grad, mem_full, preferred_element_type=jnp.float32
    )
    value_weight_grad = outer_sum(flat, value_grad) + jnp.einsum(
        "smj,mi->ij", mem_value_grad, mem_full, preferred_element_type=jnp.float32
    )
    value_bias_grad = jnp.sum(value_grad.astype(jnp.float32), 0) + jnp.sum(
        mem_value_grad.astype(jnp.float32), (0, 1)
    )
    memory_grad = jnp.einsum(
        "smj,ij->mi", mem_key_grad, wk_full, preferred_element_type=jnp.float32
    ) + jnp.einsum("smj,ij->mi", mem_value_grad, wv_full, preferred_element_type=jnp.float32)
    input_grad = (
        first_grad
        + back_mul(query_grad, wq_full) * scale
        + back_mul(key_grad, wk_full)
        + back_mul(value_grad, wv_full)
    )
    input_grad = input_grad.astype(jnp.bfloat16).reshape(seqs, length, width)
    summed = (
        lax.psum_scatter(memory_grad, "dp", scatter_dimension=1, tiled=True),
        lax.psum_scatter(query_weight_grad, "dp", scatter_dimension=0, tiled=True),
        lax.psum_scatter(query_bias_grad, "dp", scatter_dimension=0, tiled=True),
        lax.psum_scatter(key_weight_grad, "dp", scatter_dimension=0, tiled=True),
        lax.psum_scatter(value_weight_grad, "dp", scatter_dimension=0, tiled=True),
        lax.psum_scatter(value_bias_grad, "dp", scatter_dimension=0, tiled=True),
        lax.psum_scatter(output_weight_grad, "dp", scatter_dimension=0, tiled=True),
        lax.psum_scatter(output_bias_grad, "dp", scatter_dimension=0, tiled=True),
        lax.psum_scatter(first_gain_grad, "dp", scatter_dimension=0, tiled=True),
        lax.psum_scatter(first_shift_grad, "dp", scatter_dimension=0, tiled=True),
        lax.psum_scatter(up_weight_grad, "dp", scatter_dimension=0, tiled=True),
        lax.psum_scatter(up_bias_grad, "dp", scatter_dimension=0, tiled=True),
        lax.psum_scatter(down_weight_grad, "dp", scatter_dimension=0, tiled=True),
        lax.psum_scatter(down_bias_grad, "dp", scatter_dimension=0, tiled=True),
        lax.psum_scatter(second_gain_grad, "dp", scatter_dimension=0, tiled=True),
        lax.psum_scatter(second_shift_grad, "dp", scatter_dimension=0, tiled=True),
    )
    return (
        layer_out,
        input_grad,
        summed[0],
        summed[1],
        summed[2],
        summed[3],
        summed[4],
        summed[5],
        summed[6],
        summed[7],
        summed[8],
        summed[9],
        summed[10],
        summed[11],
        summed[12],
        summed[13],
        summed[14],
        summed[15],
    )


def solution(mesh):
    in_specs = (
        P("dp", None, None),
        P("dp"),
        P(None, "dp"),
        P("dp", None),
        P("dp"),
        P("dp", None),
        P("dp", None),
        P("dp"),
        P("dp", None),
        P("dp"),
        P("dp"),
        P("dp"),
        P("dp", None),
        P("dp"),
        P("dp", None),
        P("dp"),
        P("dp"),
        P("dp"),
        P("dp", None, None),
    )
    out_specs = (
        P("dp", None, None),
        P("dp", None, None),
        P(None, "dp"),
        P("dp", None),
        P("dp"),
        P("dp", None),
        P("dp", None),
        P("dp"),
        P("dp", None),
        P("dp"),
        P("dp"),
        P("dp"),
        P("dp", None),
        P("dp"),
        P("dp", None),
        P("dp"),
        P("dp"),
        P("dp"),
    )
    return jax.shard_map(
        on_device, mesh=mesh, in_specs=in_specs, out_specs=out_specs, check_vma=False
    )
```

profile of v0, /device:TPU:0, one launch (start us, length us, event | category | flops | bytes accessed | tf_op | source)
XLA Modules:
  0.0 1635.3 jit_solution(3070826220830270797)
XLA Ops:
  16.4 42.2 %all-reduce.19 = (bf16[512]{0:T(512)(128)(2,1)S(1)}, bf16[512]{0:T(512)(128)(2,1)S(1)}, bf16[512]{0:T(512)(128)(2,1)}, bf16[512]{0:T(512)(128)(2,1)}, bf16[512]{...) all-reduce(bf16[512]{0:T(512)(128)(2,1)S(1)} %dynamic-update-slice,, ...), channel_id=1, replica_groups=mesh['dp'=32] {'dp'}, use_global_device_ids=true, to_apply=%add | all-reduce | flops 6144 | bytes 24576
  58.6 41.3 %all_gather.61 = bf16[20,512]{0,1:T(8,128)(2,1)S(1)} all-gather(bf16[20,16]{0,1:T(8,128)(2,1)} %param.25), channel_id=1, replica_groups=mesh['dp'=32] {'dp'}, dimensions={1}, use_global_device_ids=true | all-gather | bytes 21120 | tf_op jit(solution)/shard_map/all_gather | solution.py:168
  99.9 38.8 %all_gather.66 = bf16[512,512]{1,0:T(8,128)(2,1)S(1)} all-gather(bf16[16,512]{1,0:T(8,128)(2,1)} %param.28), channel_id=1, replica_groups=mesh['dp'=32] {'dp'}, dimensions={0}, use_global_device_ids=true | all-gather | bytes 540672 | tf_op jit(solution)/shard_map/all_gather | solution.py:171
  138.8 39.7 %all_gather.62 = bf16[512,512]{1,0:T(8,128)(2,1)S(1)} all-gather(bf16[16,512]{1,0:T(8,128)(2,1)} %param.29), channel_id=1, replica_groups=mesh['dp'=32] {'dp'}, dimensions={0}, use_global_device_ids=true | all-gather | bytes 540672 | tf_op jit(solution)/shard_map/all_gather | solution.py:172
  184.8 38.1 %all_gather.64 = bf16[512,512]{1,0:T(8,128)(2,1)S(1)} all-gather(bf16[16,512]{1,0:T(8,128)(2,1)S(1)} %copy-done.42), channel_id=1, replica_groups=mesh['dp'=32] {'dp'}, dimensions={0}, use_global_device_ids=true | all-gather | bytes 540672 | tf_op jit(solution)/shard_map/all_gather | solution.py:169
  222.9 4.4 multiply_convert_fusion.3
  227.2 3.9 copy.71
  233.7 4.0 copy.73
  237.7 115.9 %while.30 = (s32[]{:T(128)}, bf16[2,1024,512]{2,1,0:T(8,128)(2,1)}, f32[2,8,1024]{2,1,0:T(8,128)}, bf16[20,512]{0,1:T(8,128)(2,1)S(1)}, bf16[2,1024,512]{1,2,0:T...) while((s32[]{:T(128)}, bf16[2,1024,512]{2,1,0:T(8,128)(2,1)}, ...), condition=%wide.region_5.6_spmd, body=%wide.region_0.5_spmd.sunk | while | flops 2260468736 | bytes 121916656 | solution.py:207
  242.5 8.1 fusion.165
  250.6 8.2 fusion.166
  258.8 9.1 fusion.167
  268.0 8.1 fusion.162
  276.1 8.2 fusion.163
  284.3 9.1 fusion.164
  300.1 8.1 fusion.165
  308.3 8.2 fusion.166
  316.5 9.1 fusion.167
  325.6 8.1 fusion.162
  333.8 8.2 fusion.163
  342.0 9.1 fusion.164
  353.9 3.1 convert_reduce_fusion.1
  357.0 39.5 %all_gather.67 = bf16[512,512]{1,0:T(8,128)(2,1)S(1)} all-gather(bf16[16,512]{1,0:T(8,128)(2,1)S(1)} %copy-done.43), channel_id=1, replica_groups=mesh['dp'=32] {'dp'}, dimensions={0}, use_global_device_ids=true | all-gather | bytes 540672 | tf_op jit(solution)/shard_map/all_gather | solution.py:174
  396.5 3.7 fusion.69
  403.1 13.3 fusion.63
  416.4 11.9 fusion.70
  432.4 3.9 convert_reduce_fusion.2
  436.3 20.6 %convert_reduce_fusion = (f32[2048]{0:T(1024)}, bf16[2048,2048]{1,0:T(8,128)(2,1)}) fusion(f32[2048,2048]{1,0:T(8,128)} %fusion.63, f32[2048]{0:T(1024)S(1)} %convert_element_type.200, bf16[2048,512]{1,0:T(8,128)(2,1)} %all-gather.5.cloned.1.call-done, f32[2048,512]{1,0:T(8,128)S(1)} %get-tuple-element.347), kind=kOutput, calls=%fused_computation.80 | convolution fusion | flops 4392482816 | bytes 31473664 | tf_op jit(solution)/shard_map/tj,ij->ti/dot_general | solution.py:39
  457.0 9.1 multiply_reduce_fusion.2
  473.3 206.0 %while.31 = (s32[]{:T(128)}, bf16[2,1024,512]{1,2,0:T(8,128)(2,1)}, bf16[2,1024,512]{1,2,0:T(8,128)(2,1)}, bf16[2,1024,512]{1,2,0:T(8,128)(2,1)}, bf16[2,20,512]...) while((s32[]{:T(128)}, bf16[2,1024,512]{1,2,0:T(8,128)(2,1)}, ...), condition=%wide.region_17.18_spmd, body=%wide.region_14.17_spmd.sunk | while | flops 5559567360 | bytes 445792192 | solution.py:285
  481.7 8.2 fusion.185
  489.8 4.5 fusion.184
  494.3 5.9 copy-done
  500.2 5.1 fusion.186
  505.3 9.6 fusion.187
  515.6 11.3 multiply_reduce_fusion.10
  526.9 11.7 multiply_convert_fusion.9
  543.1 11.3 multiply_reduce_fusion.9
  554.5 11.7 multiply_convert_fusion.8
  584.4 8.2 fusion.185
  592.6 4.5 fusion.184
  597.0 5.9 copy-done
  602.9 5.1 fusion.186
  608.0 9.6 fusion.187
  618.3 11.3 multiply_reduce_fusion.10
  629.6 11.7 multiply_convert_fusion.9
  645.9 11.3 multiply_reduce_fusion.9
  657.2 11.7 multiply_convert_fusion.8
  685.1 4.5 fusion.55
  689.7 3.5 convolution_bitcast_fusion.1
  694.9 3.6 fusion.51
  704.5 13.8 fusion.58
  719.0 11.4 fusion.61
  733.4 4.0 copy.81
  737.4 4.0 copy.83
  745.4 37.2 %all-reduce.18 = (f32[512]{0:T(512)S(1)}, f32[512]{0:T(512)S(1)}, f32[512]{0:T(512)S(1)}, f32[512]{0:T(512)S(1)}, f32[512]{0:T(512)S(1)}, /*index=5*/f32[2048]{0...) all-reduce(f32[512]{0:T(512)S(1)} %broadcast_multiply_fusion.5, ...), channel_id=4, replica_groups=mesh['dp'=32] {'dp'}, use_global_device_ids=true, to_apply=%region_23.24.clone | all-reduce | flops 6144 | bytes 49152
  793.8 3.1 add_convert_fusion
  796.8 18.4 %reduce-scatter.14.cloned.1.call-done = f32[20,16]{0,1:T(8,128)} async-done(((f32[20,512]{0,1:T(8,128)}), f32[20,16]{0,1:T(8,128)}) %reduce-scatter.14.cloned.1.call-update) | async-done | bytes 1296 | tf_op jit(solution)/shard_map/reduce_scatter | solution.py:321
  815.2 133.5 %reduce-scatter.16.cloned.1.call-done = f32[16,512]{1,0:T(8,128)} async-done(((f32[512,512]{1,0:T(8,128)}), f32[16,512]{1,0:T(8,128)}) %reduce-scatter.16.cloned.1.call-update) | async-done | bytes 32784 | tf_op jit(solution)/shard_map/reduce_scatter | solution.py:327
  948.7 133.5 %reduce-scatter.24.cloned.1.call-done = f32[16,512]{1,0:T(8,128)} async-done(((f32[512,512]{1,0:T(8,128)}), f32[16,512]{1,0:T(8,128)}) %reduce-scatter.24.cloned.1.call-update) | async-done | bytes 32784
  1082.2 133.5 %reduce-scatter.22.cloned.1.call-done = f32[16,512]{1,0:T(8,128)} async-done(((f32[512,512]{1,0:T(8,128)}), f32[16,512]{1,0:T(8,128)}) %reduce-scatter.22.cloned.1.call-update) | async-done | bytes 32784
  1215.7 133.6 %reduce-scatter.26.cloned.1.call-done = f32[16,512]{1,0:T(8,128)} async-done(((f32[512,512]{1,0:T(8,128)}), f32[16,512]{1,0:T(8,128)}) %reduce-scatter.26.cloned.1.call-update) | async-done | bytes 32784
  1349.3 139.6 %reduce-scatter.20.cloned.1.call-done = f32[64,512]{1,0:T(8,128)} async-done(((f32[2048,512]{1,0:T(8,128)}), f32[64,512]{1,0:T(8,128)}) %reduce-scatter.20.cloned.1.call-update) | async-done | bytes 131088 | tf_op jit(solution)/shard_map/reduce_scatter | solution.py:333
  1488.9 139.7 %reduce-scatter.18.cloned.1.call-done = f32[16,2048]{1,0:T(8,128)} async-done(((f32[512,2048]{1,0:T(8,128)}), f32[16,2048]{1,0:T(8,128)}) %reduce-scatter.18.cloned.1.call-update) | async-done | bytes 131088 | tf_op jit(solution)/shard_map/reduce_scatter | solution.py:331
  (338 shorter events, 120.8 us)
Async XLA Ops:
  7.2 395.9 %all-gather.3.cloned.1.call-start = ((), (), s32[]{:S(2)}) async-start(), calls=%async_computation.7 | async-start | bytes 2162688 | tf_op jit(solution)/shard_map/all_gather | solution.py:178
  7.9 408.5 %all-gather.5.cloned.1.call-start = ((), (), s32[]{:S(2)}) async-start(), calls=%async_computation.8 | async-start | bytes 2162688 | tf_op jit(solution)/shard_map/all_gather | solution.py:180
  8.7 806.5 %reduce-scatter.14.cloned.1.call-start = ((), (), s32[]{:S(2)}) async-start(), calls=%async_computation.9 | async-start | bytes 270336 | tf_op jit(solution)/shard_map/reduce_scatter | solution.py:321
  99.9 78.7 %copy-start.27 = (bf16[20,512]{0,1:T(8,128)(2,1)}, bf16[20,512]{0,1:T(8,128)(2,1)S(1)}, u32[]{:S(2)}) copy-start(bf16[20,512]{0,1:T(8,128)(2,1)S(1)} %all_gather.61) | copy-start | bytes 61444
  138.8 43.1 %copy-start.17 = (bf16[512,512]{1,0:T(8,128)(2,1)}, bf16[512,512]{1,0:T(8,128)(2,1)S(1)}, u32[]{:S(2)}) copy-start(bf16[512,512]{1,0:T(8,128)(2,1)S(1)} %all_gather.66) | copy-start | bytes 1572868
  178.5 3.5 copy-start.19
  178.9 3.0 copy-start.64
  222.9 4.4 copy-start.30
  231.2 6.5 copy-start.66
  237.7 116.0 %copy-start.63 = (bf16[512]{0:T(512)(128)(2,1)S(1)}, bf16[512]{0:T(512)(128)(2,1)}, u32[]{:S(2)}) copy-start(bf16[512]{0:T(512)(128)(2,1)} %get-tuple-element.342) | copy-start | bytes 3076
  237.7 116.1 %copy-start.62 = (bf16[512]{0:T(512)(128)(2,1)S(1)}, bf16[512]{0:T(512)(128)(2,1)}, u32[]{:S(2)}) copy-start(bf16[512]{0:T(512)(128)(2,1)} %get-tuple-element.341) | copy-start | bytes 3076
  237.7 116.1 %copy-start.61 = (bf16[512]{0:T(512)(128)(2,1)S(1)}, bf16[512]{0:T(512)(128)(2,1)}, u32[]{:S(2)}) copy-start(bf16[512]{0:T(512)(128)(2,1)} %get-tuple-element.345) | copy-start | bytes 3076
  237.7 116.1 %copy-start.60 = (bf16[512]{0:T(512)(128)(2,1)S(1)}, bf16[512]{0:T(512)(128)(2,1)}, u32[]{:S(2)}) copy-start(bf16[512]{0:T(512)(128)(2,1)} %get-tuple-element.339) | copy-start | bytes 3076
  237.7 116.1 %copy-start.59 = (bf16[512]{0:T(512)(128)(2,1)S(1)}, bf16[512]{0:T(512)(128)(2,1)}, u32[]{:S(2)}) copy-start(bf16[512]{0:T(512)(128)(2,1)} %get-tuple-element.340) | copy-start | bytes 3076
  237.7 116.1 %copy-start.58 = (bf16[512]{0:T(512)(128)(2,1)S(1)}, bf16[512]{0:T(512)(128)(2,1)}, u32[]{:S(2)}) copy-start(bf16[512]{0:T(512)(128)(2,1)} %get-tuple-element.344) | copy-start | bytes 3076
  237.7 116.1 %copy-start.53 = (bf16[2048]{0:T(1024)(128)(2,1)S(1)}, bf16[2048]{0:T(1024)(128)(2,1)}, u32[]{:S(2)}) copy-start(bf16[2048]{0:T(1024)(128)(2,1)} %get-tuple-element.343) | copy-start | bytes 12292
  237.7 119.3 %copy-start.43 = (bf16[16,512]{1,0:T(8,128)(2,1)S(1)}, bf16[16,512]{1,0:T(8,128)(2,1)}, u32[]{:S(2)}) copy-start(bf16[16,512]{1,0:T(8,128)(2,1)} %param.31) | copy-start | bytes 49156
  353.7 112.4 %copy-start.47 = (f32[512]{0:T(512)}, f32[512]{0:T(512)S(1)}, u32[]{:S(2)}) copy-start(f32[512]{0:T(512)S(1)} %convert_element_type.197) | copy-start | bytes 6148
  353.7 62.6 %copy-start.56 = (f32[512]{0:T(512)}, f32[512]{0:T(512)S(1)}, u32[]{:S(2)}) copy-start(f32[512]{0:T(512)S(1)} %convert_element_type.198) | copy-start | bytes 6148
  353.9 82.5 %copy-start.50 = (f32[2048]{0:T(1024)}, f32[2048]{0:T(1024)S(1)}, u32[]{:S(2)}) copy-start(f32[2048]{0:T(1024)S(1)} %convert_element_type.200) | copy-start | bytes 24580
  400.2 65.9 %copy-start.38 = (f32[2048]{0:T(1024)}, f32[2048]{0:T(1024)S(1)}, u32[]{:S(2)}) copy-start(f32[2048]{0:T(1024)S(1)} %broadcast_multiply_fusion.4) | copy-start | bytes 24580
  403.1 63.1 %copy-start.40 = (f32[2048]{0:T(1024)}, f32[2048]{0:T(1024)S(1)}, u32[]{:S(2)}) copy-start(f32[2048]{0:T(1024)S(1)} %add_rsqrt_fusion.1) | copy-start | bytes 24580
  436.3 20.7 %copy-start.26 = (f32[2048,512]{1,0:T(8,128)}, f32[2048,512]{1,0:T(8,128)S(1)}, u32[]{:S(2)}) copy-start(f32[2048,512]{1,0:T(8,128)S(1)} %get-tuple-element.347) | copy-start | bytes 12582916
  436.3 20.7 %copy-start.13 = (f32[2048,512]{1,0:T(8,128)S(1)}, f32[2048,512]{1,0:T(8,128)}, u32[]{:S(2)}) copy-start(f32[2048,512]{1,0:T(8,128)} %copy-done.12) | copy-start | bytes 12582916
  436.3 20.7 %copy-start.65 = (bf16[512,2048]{1,0:T(8,128)(2,1)S(1)}, bf16[512,2048]{1,0:T(8,128)(2,1)}, u32[]{:S(2)}) copy-start(bf16[512,2048]{1,0:T(8,128)(2,1)} %all-gather.3.cloned.1.call-done) | copy-start | bytes 6291460
  473.5 3.4 copy-start.14
  473.5 4.7 copy-start.10
  481.6 8.2 copy-start.2
  481.7 8.2 copy-start.4
  494.3 5.9 copy-start
  505.3 10.3 copy-start.6
  514.9 12.0 copy-start.7
  554.5 11.7 copy-start.3
  569.1 2.9 copy-start.32
  571.2 5.0 copy-start.15
  576.2 3.4 copy-start.14
  576.2 4.7 copy-start.10
  584.4 8.2 copy-start.2
  584.4 8.2 copy-start.4
  597.0 5.9 copy-start
  608.0 10.3 copy-start.6
  617.6 12.0 copy-start.7
  657.2 11.7 copy-start.3
  671.8 2.9 copy-start.32
  673.9 5.0 copy-start.15
  679.3 5.7 copy-start.29
  685.0 263.7 %reduce-scatter.16.cloned.1.call-start = ((), (), s32[]{:S(2)}) async-start(), calls=%async_computation.10 | async-start | bytes 1081344 | tf_op jit(solution)/shard_map/reduce_scatter | solution.py:327
  689.6 3.6 copy-start.28
  689.6 392.6 %reduce-scatter.24.cloned.1.call-start = ((), (), s32[]{:S(2)}) async-start(), calls=%async_computation.14 | async-start | bytes 1081344
  694.8 520.9 %reduce-scatter.22.cloned.1.call-start = ((), (), s32[]{:S(2)}) async-start(), calls=%async_computation.13 | async-start | bytes 1081344
  694.9 5.0 copy-start.23
  699.9 649.4 %reduce-scatter.26.cloned.1.call-start = ((), (), s32[]{:S(2)}) async-start(), calls=%async_computation.15 | async-start | bytes 1081344
  704.5 784.5 %reduce-scatter.20.cloned.1.call-start = ((), (), s32[]{:S(2)}) async-start(), calls=%async_computation.12 | async-start | bytes 4325376 | tf_op jit(solution)/shard_map/reduce_scatter | solution.py:333
  718.4 910.2 %reduce-scatter.18.cloned.1.call-start = ((), (), s32[]{:S(2)}) async-start(), calls=%async_computation.11 | async-start | bytes 4325376 | tf_op jit(solution)/shard_map/reduce_scatter | solution.py:331
  737.3 8.0 copy-start.44
  737.3 8.0 copy-start.45
  737.3 8.0 copy-start.46
  737.3 8.0 copy-start.49
  737.3 8.0 copy-start.52
  737.3 8.0 copy-start.54
  737.3 8.0 copy-start.55
  737.4 50.5 %copy-start.31 = (bf16[512,512]{1,0:T(8,128)(2,1)S(1)}, bf16[512,512]{1,0:T(8,128)(2,1)}, u32[]{:S(2)}) copy-start(bf16[512,512]{1,0:T(8,128)(2,1)} %copy-done.30) | copy-start | bytes 1572868
  787.9 2.9 copy-start.18
  790.8 2.9 copy-start.20
  (35 other events, 70.6 us)
Sparse Core Ops, SparseCore 0:
  10.9 59.0 all-gather.2
  72.9 55.8 all-gather.4
  685.1 130.0 reduce-scatter.13
  818.0 130.7 reduce-scatter.15
  951.4 130.7 reduce-scatter.23
  1084.9 130.7 reduce-scatter.21
  1218.5 130.7 reduce-scatter.25
  1352.2 136.6 reduce-scatter.19
  1491.9 136.6 reduce-scatter.17
where the time goes:
time: 1640 us
  waiting for transfers between devices  833 us (51%)
  matrix products  311 us (19%)
  blocking collectives  277 us (17%)
  other arithmetic  101 us (6%)
  local copies, waits for them, and re-layouts  93 us (6%)
    unnamed x12, waiting for transfers between devices  402 us
    reduce_scatter x1, waiting for transfers between devices, on_device(): lax.psum_scatter(up_weight_grad, 'dp', scatter_dimension=0, tiled=True)  140 us
    reduce_scatter x1, waiting for transfers between devices, on_device(): lax.psum_scatter(down_weight_grad, 'dp', scatter_dimension=0, tiled=True)  140 us
    reduce_scatter x1, waiting for transfers between devices, on_device(): lax.psum_scatter(output_weight_grad, 'dp', scatter_dimension=0, tiled=True)  134 us
    unnamed x2, blocking collectives  79.5 us
    dot_general x8, matrix products, block_scores(): jnp.einsum('qhd,khd->hqk', query_block, all_keys, preferred_element_type=...  57.8 us
    convert_element_type x4, other arithmetic, attend_backward(): score_grad = centred.astype(jnp.bfloat16)  46.8 us
    dot_general x4, matrix products, attend_backward(): jnp.einsum('qhd,khd->hqk', grad_block, all_values, preferred_element_type...  45.4 us
  transfers between devices with their start and end apart: 9, of which 7 were waited for; matrix products, arithmetic and copies ran while one was open for 14% of the time, Pallas kernels for 0%

commit v1 on v0

v1 whole, which is shorter than its diff:
```python
import functools

import jax
import jax.numpy as jnp
from jax import lax
from jax.experimental import pallas as pl
from jax.experimental.pallas import tpu as pltpu
from jax.sharding import PartitionSpec as P

HEADS = 8
HEAD_DIM = 64
EPSILON = 1e-05
LOG2E = 1.4426950408889634
LN2 = 0.6931471805599453
GELU_A = 0.7978845608028654
GELU_B = GELU_A * 0.044715
HIDE = -1e30
KEY_PAD = 32

f32 = jnp.float32
bf16 = jnp.bfloat16
VMEM = pltpu.VMEM
MESH = pl.DeviceIdType.MESH
NN = (((1,), (0,)), ((), ()))
NT = (((1,), (1,)), ((), ()))
TN = (((0,), (0,)), ((), ()))


def dg(left, right, dims):
    return lax.dot_general(left, right, dims, preferred_element_type=f32)


def col_sum(value):
    return jnp.sum(value, 0, keepdims=True)


class Cube:
    def __init__(self, count, sub):
        self.count, self.sub = count, sub
        self.nb = count.bit_length() - 1
        device = lax.axis_index("dp")
        self.device = device
        me = device // sub
        self.bits = [(me // (2**b)) % 2 for b in range(self.nb)]
        self.msb_first = tuple(range(self.nb - 1, -1, -1))

    def partner(self, b):
        return (self.device + (1 - 2 * self.bits[b]) * (2**b * self.sub),)

    def barrier(self):
        sem = pltpu.get_barrier_semaphore()
        for b in range(self.nb):
            pl.semaphore_signal(sem, inc=1, device_id=self.partner(b), device_id_type=MESH)
        pl.semaphore_wait(sem, self.nb)

    def own(self):
        return tuple(self.bits[b] for b in self.msb_first)


def orders(nb):
    if nb >= 4:
        far = list(range(nb - 1, 2, -1))
        return (far + [1, 2, 0], far + [2, 1, 0])
    return (list(range(nb - 1, -1, -1)),) * 2


def gather_copy(cube, ref, order, step, rows, lanes, send, recv):
    b = order[step]
    done = set(order[:step])
    idx = tuple(slice(None) if c in done else cube.bits[c] for c in cube.msb_first)
    view = ref.at[idx + (rows, lanes)]
    return pltpu.make_async_remote_copy(
        src_ref=view,
        dst_ref=view,
        send_sem=send,
        recv_sem=recv,
        device_id=cube.partner(b),
        device_id_type=MESH,
    )


class Scatter:
    def __init__(self, cube, source, lanes, order, bufs, send, recv):
        self.cube, self.source, self.lanes, self.order = cube, source, lanes, order
        self.bufs, self.send, self.recv = bufs, send, recv

    def _half(self, step, mine):
        cube, b = self.cube, self.order[step]
        left = [c for c in cube.msb_first if c not in self.order[:step]]
        bit = cube.bits[b] if mine else 1 - cube.bits[b]
        idx = tuple(bit if c == b else slice(None) for c in left)
        if step == 0:
            return self.source, idx + (slice(None), self.lanes)
        return self.bufs[step - 1], idx

    def copy(self, step):
        ref, idx = self._half(step, False)
        return pltpu.make_async_remote_copy(
            src_ref=ref.at[idx],
            dst_ref=self.bufs[step],
            send_sem=self.send.at[step],
            recv_sem=self.recv.at[step],
            device_id=self.cube.partner(self.order[step]),
            device_id_type=MESH,
        )

    def add(self, step, f32_result=False):
        ref, idx = self._half(step, True)
        into = self.bufs[step]
        free = self.cube.nb - 1 - step
        if f32_result:
            return into[...].astype(f32) + ref[idx].astype(f32)
        at = self.cube.bits[self.order[step]]
        left = [c for c in self.cube.msb_first if c not in self.order[:step]]
        where = left.index(self.order[step])
        for flat in range(2**free):
            sub = tuple((flat >> (free - 1 - k)) & 1 for k in range(free))
            full = sub[:where] + (at,) + sub[where:]
            if step == 0:
                full = full + (slice(None), self.lanes)
            into[sub] = (into[sub].astype(f32) + ref[full].astype(f32)).astype(into.dtype)
        return None


def attend_kernel(
    count, sub, mem_rows,
    len_ref, x_ref, wq_ref, wk_ref, wv_ref, wo_ref, wu_ref, wd_ref, small_ref,
    q_o, k_o, v_o, qt_o, att_o, g1, g2, vec_o, ub_o, mem_o,
    gs, ksel, vt_s, score_a, score_b, top_a, top_b,
    local, send1, recv1, send2, recv2, send3, recv3,
):
    cube = Cube(count, sub)
    nb = cube.nb
    seqs, length, width = x_ref.shape
    keys = k_o.shape[1]
    mem_pad = keys - length
    r = wq_ref.shape[0]
    ff = wu_ref.shape[1]
    cols = ff // width
    fr = wd_ref.shape[0]
    own = cube.own()
    ways = orders(nb)
    half = width // 2
    halves = (slice(0, half), slice(half, width))
    whole = (slice(None), slice(None))
    for j, ref in enumerate((wq_ref, wk_ref, wv_ref)):
        g1[own + (slice(j * r, j * r + r), slice(None))] = ref[...]
    gs[own + whole] = small_ref[...]
    parts = [(wo_ref, slice(0, r))]
    parts += [
        (wu_ref.at[:, c * width : (c + 1) * width], slice(r + c * r, r + c * r + r))
        for c in range(cols)
    ]
    parts += [(wd_ref, slice(r + cols * r, r + cols * r + fr))]
    moves = [
        pltpu.make_async_copy(ref, g2.at[own + (rows, slice(None))], local.at[j])
        for j, (ref, rows) in enumerate(parts)
    ]
    for move in moves:
        move.start()
    cube.barrier()

    def first(step):
        copies = [
            gather_copy(
                cube, g1, ways[k], step, slice(None), halves[k], send1.at[k, step], recv1.at[k, step]
            )
            for k in range(2)
        ]
        return copies + [
            gather_copy(
                cube, gs, ways[0], step, slice(None), slice(None), send3.at[step], recv3.at[step]
            )
        ]

    def second(step):
        return [
            gather_copy(
                cube, g2, ways[k], step, slice(None), halves[k], send2.at[k, step], recv2.at[k, step]
            )
            for k in range(2)
        ]

    for step in range(nb):
        copies = first(step)
        for copy in copies:
            copy.start()
        if step == 0:
            for move in moves:
                move.wait()
        if step == nb - 1:
            for copy in second(0):
                copy.start()
        for copy in copies:
            copy.wait()

    lane = lax.broadcasted_iota(jnp.int32, (1, 128), 1)
    groups = width // 128
    per = 128 // r
    upper = [jnp.zeros((16, 128), f32) for _ in range(groups)]
    lower = [jnp.zeros((16, 128), f32) for _ in range(groups)]
    vecs = [jnp.zeros((16, 128), f32) for _ in range(groups)]
    ups = [jnp.zeros((16, 128), f32) for _ in range(ff // 128)]
    for i in range(count):
        at = tuple((i >> b) & 1 for b in cube.msb_first)
        block = gs[at + whole].astype(f32)
        to = (i % per) * r
        g = i // per
        here = (lane >= to) & (lane < to + r)
        upper[g] = upper[g] + jnp.where(here, pltpu.roll(block, to % 128, 1), 0.0)
        lower[g] = lower[g] + jnp.where(here, pltpu.roll(block, (to - r) % 128, 1), 0.0)
        vecs[g] = vecs[g] + jnp.where(here, pltpu.roll(block, (to - 2 * r) % 128, 1), 0.0)
        to = (i * fr) % 128
        g = (i * fr) // 128
        here = (lane >= to) & (lane < to + fr)
        ups[g] = ups[g] + jnp.where(here, pltpu.roll(block, (to - 3 * r) % 128, 1), 0.0)
    for g in range(groups):
        at = slice(128 * g, 128 * g + 128)
        mem_o[0:16, at] = upper[g].astype(bf16)
        mem_o[16:32, at] = lower[g].astype(bf16)
        vec_o[:, at] = vecs[g]
    for g in range(ff // 128):
        ub_o[:, 128 * g : 128 * g + 128] = ups[g][0:1, :]

    def weight(j):
        return g1[(slice(None),) * nb + (slice(j * r, j * r + r), slice(None))].reshape(width, width)

    bq = vec_o[0:1, :]
    bv = vec_o[1:2, :]

    def put_keys(s, rows, kk, vv, bias):
        kb = kk.astype(bf16)
        vb = vv.astype(bf16)
        k_o[s, rows, :] = kb
        v_o[s, rows, :] = vb
        for h in range(HEADS):
            p, o = h // 2, 64 * (1 - h % 2)
            pattern = jnp.where(
                lane == o, bias, jnp.where((lane > o) & (lane <= o + 3), 1.0, 0.0)
            ).astype(bf16)
            mine = (lane < 64) if h % 2 == 0 else (lane >= 64)
            ksel[s, h, rows, :] = jnp.where(mine, kb[:, 128 * p : 128 * p + 128], pattern)
        vt = vb.T
        for h in range(HEADS):
            vt_s[s, h, 0:64, rows] = vt[64 * h : 64 * h + 64, :]

    top_row = lax.broadcasted_iota(jnp.int32, (16, keys), 0)
    ones = jnp.where(top_row == 0, 1.0, 0.0).astype(bf16)
    for s in range(seqs):
        for h in range(HEADS):
            vt_s[s, h, 64:80, :] = ones
    mem = mem_o[...]
    mem_keys = dg(mem, weight(1), NN)
    mem_values = dg(mem, weight(2), NN) + bv
    mem_row = lax.broadcasted_iota(jnp.int32, (mem_pad, 1), 0)
    for s in range(seqs):
        put_keys(
            s, slice(length, keys), mem_keys, mem_values, jnp.where(mem_row < mem_rows, 0.0, HIDE)
        )
    tile = 512
    tiles = length // tile
    aux = jnp.where(lax.broadcasted_iota(jnp.int32, (64, tile), 0) == 0, 1.0, 0.0).astype(bf16)

    @pl.loop(0, seqs * tiles)
    def _(i):
        s = i // tiles
        start = pl.multiple_of((i % tiles) * tile, tile)
        rows = pl.ds(start, tile)
        xt = x_ref[s, rows, :]
        qb = ((dg(xt, weight(0), NN) + bq) * (LOG2E * HEAD_DIM**-0.5)).astype(bf16)
        q_o[s, rows, :] = qb
        qt = qb.T
        for h in range(HEADS):
            e = h % 2
            qt_o[s, h, 64 * e : 64 * e + 64, rows] = qt[64 * h : 64 * h + 64, :]
            qt_o[s, h, 64 * (1 - e) : 64 * (1 - e) + 64, rows] = aux
        row = lax.broadcasted_iota(jnp.int32, (tile, 1), 0) + start
        put_keys(
            s,
            rows,
            dg(xt, weight(1), NN),
            dg(xt, weight(2), NN) + bv,
            jnp.where(row < len_ref[s], 0.0, HIDE),
        )

    block = score_a.shape[1]
    per_head = length // block
    blocks = seqs * HEADS * per_head

    def place(i):
        s = i // (HEADS * per_head)
        h = (i // per_head) % HEADS
        return s, h, pl.ds(pl.multiple_of((i % per_head) * block, block), block)

    def scores(i, score, top):
        s, h, at = place(i)
        value = dg(ksel[s, h], qt_o[s, h, :, at], NN)
        score[...] = value
        top[...] = jnp.max(value, 0, keepdims=True)

    def mix(i, score, top):
        s, h, at = place(i)
        peak = top[...]
        probs = jnp.exp2(score[...] - peak).astype(bf16)
        mixed = dg(vt_s[s, h], probs, NN)
        total = mixed[64:65, :]
        att_o[s, h, :, at] = (mixed[0:64, :] / total).astype(bf16)
        stat = peak + jnp.log2(total)
        hi = stat.astype(bf16).astype(f32)
        mid = (stat - hi).astype(bf16).astype(f32)
        low = stat - hi - mid
        row = lax.broadcasted_iota(jnp.int32, (16, block), 0)
        extra = jnp.where(
            row == 0,
            1.0,
            jnp.where(row == 1, -hi, jnp.where(row == 2, -mid, jnp.where(row == 3, -low, 0.0))),
        )
        o = pl.multiple_of(64 * (1 - h % 2), 64)
        qt_o[s, h, pl.ds(o, 16), at] = extra.astype(bf16)

    scores(0, score_a, top_a)
    turns = blocks // 2

    @pl.loop(0, turns)
    def _(j):
        for step in range(1, nb):

            @pl.when(j == (step * turns) // nb)
            def _():
                for copy in second(step - 1):
                    copy.wait()
                for copy in second(step):
                    copy.start()

        scores(2 * j + 1, score_b, top_b)
        mix(2 * j, score_a, top_a)
        scores(jnp.minimum(2 * j + 2, blocks - 1), score_a, top_a)
        mix(2 * j + 1, score_b, top_b)

    for copy in second(nb - 1):
        copy.wait()


def attend_call(count, sub, lengths, x, wq, wk, wv, wo, wu, wd, small, mem_rows):
    seqs, length, width = x.shape
    r, ff, fr = wq.shape[0], wu.shape[1], wd.shape[0]
    rows2 = r + (ff // width) * r + fr
    keys = length + KEY_PAD
    nb = count.bit_length() - 1
    cube = (2,) * nb
    block = min(512, length)
    shape = jax.ShapeDtypeStruct
    vm = pl.BlockSpec(memory_space=VMEM)
    dma = pltpu.SemaphoreType.DMA
    return pl.pallas_call(
        functools.partial(attend_kernel, count, sub, mem_rows),
        out_shape=(
            shape((seqs, length, width), bf16),
            shape((seqs, keys, width), bf16),
            shape((seqs, keys, width), bf16),
            shape((seqs, HEADS, 128, length), bf16),
            shape((seqs, HEADS, HEAD_DIM, length), bf16),
            shape(cube + (3 * r, width), bf16),
            shape(cube + (rows2, width), bf16),
            shape((16, width), f32),
            shape((1, ff), f32),
            shape((KEY_PAD, width), bf16),
        ),
        in_specs=[pl.BlockSpec(memory_space=pltpu.SMEM)] + [vm] * 8,
        out_specs=[vm] * 6 + [pl.BlockSpec(memory_space=pl.ANY)] + [vm] * 3,
        scratch_shapes=[
            VMEM(cube + (16, 128), bf16),
            VMEM((seqs, HEADS, keys, 128), bf16),
            VMEM((seqs, HEADS, 80, keys), bf16),
            VMEM((keys, block), f32),
            VMEM((keys, block), f32),
            VMEM((1, block), f32),
            VMEM((1, block), f32),
            dma((2 + ff // width,)),
            dma((2, nb)),
            dma((2, nb)),
            dma((2, nb)),
            dma((2, nb)),
            dma((nb,)),
            dma((nb,)),
        ],
        compiler_params=pltpu.CompilerParams(
            collective_id=0, has_side_effects=True, vmem_limit_bytes=60 * 2**20
        ),
        name="attend",
    )(lengths, x, wq, wk, wv, wo, wu, wd, small)


def norm_forward(value, gain, shift):
    center = value - jnp.mean(value, -1, keepdims=True)
    inverse = lax.rsqrt(jnp.mean(center * center, -1, keepdims=True) + EPSILON)
    normed = center * inverse
    return normed * gain + shift, normed, inverse


def norm_backward(grad, normed, inverse, gain):
    scaled = grad * gain
    return inverse * (
        scaled
        - jnp.mean(scaled, -1, keepdims=True)
        - normed * jnp.mean(scaled * normed, -1, keepdims=True)
    )


def feed_kernel(
    r, fr, steps,
    x_ref, att_ref, dy_ref, g2, vec, ub,
    out_o, res_o, datt_o, part_o, gvec, gub,
    slope_s, act_s, gwo, gwu, gwd,
):
    i = pl.program_id(0)
    rows, width = x_ref.shape[1:]
    count = g2.shape[0]
    cols = g2.shape[1] // r - 1 - fr // r
    per = width // fr

    @pl.when(i == 0)
    def _():
        for ref in (gwo, gwu, gwd, gvec, gub):
            ref[...] = jnp.zeros_like(ref)

    bo, ga, sa, bd, gb, sb = [vec[j : j + 1, :] for j in range(2, 8)]

    def wo():
        return g2[:, 0:r, :].reshape(width, width)

    def wu(c):
        return g2[:, r + c * r : r + c * r + r, :].reshape(width, width)

    def wd(c):
        return g2[c * per : (c + 1) * per, r + cols * r :, :].reshape(width, width)

    att = att_ref[0]
    hidden, normed1, inverse1 = norm_forward(x_ref[0].astype(f32) + dg(att, wo(), TN) + bo, ga, sa)
    low = hidden.astype(bf16)
    outer = hidden + bd
    for c in range(cols):
        at = slice(c * width, (c + 1) * width)
        u = dg(low, wu(c), NN) + ub[:, at]
        u2 = u * u
        t = jnp.tanh(u * (GELU_A + GELU_B * u2))
        hu = 0.5 * u
        act = (hu + hu * t).astype(bf16)
        act_s[c] = act
        slope_s[c] = (
            (0.5 + 0.5 * t) + (hu * (1.0 - t * t)) * (GELU_A + 3.0 * GELU_B * u2)
        ).astype(bf16)
        outer = outer + dg(act, wd(c), NN)
    out, normed2, inverse2 = norm_forward(outer, gb, sb)
    out_o[0] = out.astype(bf16)
    dy = dy_ref[0].astype(f32)
    gvec[6:7, :] += col_sum(dy * normed2)
    gvec[7:8, :] += col_sum(dy)
    d_res2 = norm_backward(dy, normed2, inverse2, gb)
    d_outer = d_res2.astype(bf16)
    gvec[5:6, :] += col_sum(d_outer.astype(f32))
    d_hidden = d_res2
    for c in range(cols):
        at = slice(c * width, (c + 1) * width)
        d_act = dg(d_outer, wd(c), NT)
        d_inner = (d_act * slope_s[c].astype(f32)).astype(bf16)
        gwd[at, :] += dg(act_s[c], d_outer, TN)
        gwu[:, at] += dg(low, d_inner, TN)
        gub[:, at] += col_sum(d_inner.astype(f32))
        d_hidden = d_hidden + dg(d_inner, wu(c), NT)
    gvec[3:4, :] += col_sum(d_hidden * normed1)
    gvec[4:5, :] += col_sum(d_hidden)
    d_res1 = norm_backward(d_hidden, normed1, inverse1, ga)
    res_o[0] = d_res1
    d_branch = d_res1.astype(bf16)
    gvec[2:3, :] += col_sum(d_branch.astype(f32))
    gwo[...] += dg(att, d_branch, NN)
    datt_o[0] = dg(d_branch, wo(), NT).astype(bf16)

    @pl.when(i == steps - 1)
    def _():
        part_o[:, 0:r, :] = gwo[...].astype(bf16).reshape(count, r, width)
        for c in range(cols):
            part_o[:, r + c * r : r + c * r + r, :] = (
                gwu[:, c * width : (c + 1) * width].astype(bf16).reshape(count, r, width)
            )
        part_o[:, r + cols * r :, :] = gwd[...].astype(bf16).reshape(count, fr, width)


def feed_call(x, att, dy, g2, vec, ub, r, fr):
    seqs, length, width = x.shape
    ff = ub.shape[1]
    tile = min(512, length)
    tiles = length // tile
    shape = jax.ShapeDtypeStruct
    rows = pl.BlockSpec((1, tile, width), lambda i: (i // tiles, i % tiles, 0))

    def full(a):
        return pl.BlockSpec(a.shape, lambda i: (0,) * len(a.shape))

    outs = (
        shape((seqs, length, width), bf16),
        shape((seqs, length, width), f32),
        shape((seqs, length, width), bf16),
        shape(g2.shape, bf16),
        shape((8, width), f32),
        shape((1, ff), f32),
    )
    return pl.pallas_call(
        functools.partial(feed_kernel, r, fr, seqs * tiles),
        grid=(seqs * tiles,),
        out_shape=outs,
        in_specs=[
            rows,
            pl.BlockSpec((1, width, tile), lambda i: (i // tiles, 0, i % tiles)),
            rows,
            full(g2),
            full(vec),
            full(ub),
        ],
        out_specs=[rows, rows, rows] + [full(a) for a in outs[3:]],
        scratch_shapes=[
            VMEM((ff // width, tile, width), bf16),
            VMEM((ff // width, tile, width), bf16),
            VMEM((width, width), f32),
            VMEM((width, ff), f32),
            VMEM((ff, width), f32),
        ],
        compiler_params=pltpu.CompilerParams(vmem_limit_bytes=60 * 2**20),
        name="feed",
    )(x, att, dy, g2, vec, ub)


def pull_kernel(
    count, sub, mem_rows, r, fr,
    len_ref, x_ref, mem_ref, q_ref, k_ref, v_ref, qt_ref, att_ref, da_ref, res_ref, g1, part1,
    gvec_ref, gub_ref,
    dx_o, gwq_o, gwk_o, gwv_o, gwo_o, gwu_o, gwd_o, small_o,
    ksel, vsel, kt, dot_s, p_a, d_a, p_b, d_b, dq_s, dk_s, dv_s, dqt,
    dv_0, dv_1, dk_0, dk_1, part2, small_s, *rest,
):
    cube = Cube(count, sub)
    nb = cube.nb
    bufs = [rest[k * nb : (k + 1) * nb] for k in range(5)]
    send, recv = rest[5 * nb :]
    seqs, length, width = x_ref.shape
    keys = k_ref.shape[1]
    ff = gub_ref.shape[1]
    cols = ff // width
    half = width // 2
    halves = (slice(0, half), slice(half, width))
    ways = [list(reversed(order)) for order in orders(nb)]
    feeds = [
        Scatter(cube, part1, halves[k], ways[k], bufs[k], send.at[k], recv.at[k]) for k in range(2)
    ]
    heads = [
        Scatter(cube, part2, halves[k], ways[k], bufs[2 + k], send.at[2 + k], recv.at[2 + k])
        for k in range(2)
    ]
    smalls = [Scatter(cube, small_s, slice(None), ways[0], bufs[4], send.at[4], recv.at[4])]

    def start(group, step):
        for part in group:
            part.copy(step).start()

    def finish(group, step):
        for part in group:
            part.copy(step).wait()
        if step < nb - 1:
            for part in group:
                part.add(step)

    cube.barrier()
    start(feeds, 0)

    lane = lax.broadcasted_iota(jnp.int32, (1, 128), 1)
    key_row = lax.broadcasted_iota(jnp.int32, (keys, 1), 0)
    block = p_a.shape[1]
    per_head = length // block
    dv_t, dk_t = (dv_0, dv_1), (dk_0, dk_1)
    temp = ((p_a, d_a), (p_b, d_b))

    def pair(j):
        s = j // (HEADS // 2)
        p = j % (HEADS // 2)
        at = pl.ds(pl.multiple_of(128 * p, 128), 128)
        kp = k_ref[s, :, at]
        vp = v_ref[s, :, at]
        kt[...] = kp.T
        da = da_ref[s, :, at]
        dat = da.T
        seen = (key_row < len_ref[s]) | ((key_row >= length) & (key_row < length + mem_rows))
        bias = jnp.where(seen, 0.0, HIDE)
        for e in range(2):
            o = 64 * (1 - e)
            mine = (lane < 64) if e == 0 else (lane >= 64)
            pattern = jnp.where(
                lane == o, bias, jnp.where((lane > o) & (lane <= o + 3), 1.0, 0.0)
            ).astype(bf16)
            ksel[e] = jnp.where(mine, kp, pattern)
            vsel[e] = jnp.where(
                mine, vp, jnp.where((lane >= o) & (lane < o + 2), 1.0, 0.0).astype(bf16)
            )
            dt = dat[64 * e : 64 * e + 64, :]
            delta = col_sum(dt.astype(f32) * att_ref[s, 2 * p + e].astype(f32))
            hi = delta.astype(bf16).astype(f32)
            row = lax.broadcasted_iota(jnp.int32, (64, length), 0)
            dot_s[e, 64 * e : 64 * e + 64, :] = dt
            dot_s[e, o : o + 64, :] = jnp.where(
                row == 0, -hi, jnp.where(row == 1, hi - delta, 0.0)
            ).astype(bf16)

        def probs(b):
            e, c = b // per_head, b % per_head
            cut = slice(c * block, (c + 1) * block)
            prob = jnp.exp2(dg(ksel[e], qt_ref[s, 2 * p + e, :, cut], NN))
            grad = dg(vsel[e], dot_s[e, :, cut], NN)
            temp[b % 2][0][...] = prob.astype(bf16)
            temp[b % 2][1][...] = (prob * grad).astype(bf16)

        def pulls(b):
            e, c = b // per_head, b % per_head
            cut = slice(c * block, (c + 1) * block)
            prob, grad = temp[b % 2]
            dv = dg(prob[...], da[cut, :], NN)
            dk = dg(grad[...], q_ref[s, cut, at], NN)
            dqt[64 * e : 64 * e + 64, cut] = dg(kt[64 * e : 64 * e + 64, :], grad[...], NN)
            if c == 0:
                dv_t[e][...] = dv
                dk_t[e][...] = dk
            else:
                dv_t[e][...] += dv
                dk_t[e][...] += dk

        probs(0)
        for b in range(2 * per_head):
            if b + 1 < 2 * per_head:
                probs(b + 1)
            pulls(b)
        even = lane < 64
        dv_s[s, :, at] = jnp.where(even, dv_0[...], dv_1[...]).astype(bf16)
        dk_s[s, :, at] = (jnp.where(even, dk_0[...], dk_1[...]) * LN2).astype(bf16)
        dq_s[s, :, at] = dqt[...].T.astype(bf16)

    turns = seqs * (HEADS // 2)

    @pl.loop(0, turns)
    def _(j):
        for step in range(nb - 1):

            @pl.when(j == ((step + 1) * turns) // nb)
            def _():
                finish(feeds, step)
                start(feeds, step + 1)

        pair(j)

    def weight(j):
        return g1[(slice(None),) * nb + (slice(j * r, j * r + r), slice(None))].reshape(width, width)

    scale = HEAD_DIM**-0.5
    mem = mem_ref[...]
    tail = slice(length, keys)
    sums = []
    for j, ref in enumerate((dq_s, dk_s, dv_s)):
        total = 0.0
        for s in range(seqs):
            total = total + dg(x_ref[s], ref[s, 0:length, :], TN)
            if j:
                total = total + dg(mem, ref[s, tail, :], TN)
        if j == 0:
            total = total * scale
        cuts = (slice(None),) * nb + (slice(j * r, j * r + r), slice(None))
        part2[cuts] = total.astype(bf16).reshape((2,) * nb + (r, width))
    start(heads, 0)
    bq = sum(col_sum(dq_s[s].astype(f32)) for s in range(seqs)) * scale
    bv = sum(col_sum(dv_s[s].astype(f32)) for s in range(seqs))
    gmem = sum(
        dg(dk_s[s, tail, :], weight(1), NT) + dg(dv_s[s, tail, :], weight(2), NT)
        for s in range(seqs)
    )
    vec_row = lax.broadcasted_iota(jnp.int32, (8, width), 0)
    vecs = jnp.where(vec_row == 0, bq, jnp.where(vec_row == 1, bv, gvec_ref[...]))
    per = 128 // r
    row8 = lax.broadcasted_iota(jnp.int32, (8, 128), 0)
    for i in range(count):
        at = tuple((i >> b) & 1 for b in cube.msb_first)
        g, off = i // per, (i % per) * r
        cut = slice(128 * g, 128 * g + 128)
        up = gub_ref[:, 128 * (i * fr // 128) : 128 * (i * fr // 128) + 128]
        up = jnp.where(row8 == 0, jnp.broadcast_to(up, (8, 128)), 0.0)
        up = pltpu.roll(up, (3 * r - (i * fr) % 128) % 128, 1)
        for k in range(2):
            top = pltpu.roll(gmem[8 * k : 8 * k + 8, cut], -off % 128, 1)
            block8 = jnp.where(lane < r, top, 0.0)
            if k == 0:
                low = pltpu.roll(gmem[16:24, cut], (r - off) % 128, 1)
                vec = pltpu.roll(vecs[:, cut], (2 * r - off) % 128, 1)
                block8 = jnp.where((lane >= r) & (lane < 2 * r), low, block8)
                block8 = jnp.where((lane >= 2 * r) & (lane < 3 * r), vec, block8)
                block8 = jnp.where((lane >= 3 * r) & (lane < 3 * r + fr), up, block8)
            small_s[at + (slice(8 * k, 8 * k + 8), slice(None))] = block8
    start(smalls, 0)

    tile = 512
    tiles = length // tile

    def inputs(i):
        s, rows = i // tiles, pl.ds((i % tiles) * tile, tile)
        dx = res_ref[s, rows, :] + dg(dq_s[s, rows, :], weight(0), NT) * scale
        dx = dx + dg(dk_s[s, rows, :], weight(1), NT) + dg(dv_s[s, rows, :], weight(2), NT)
        dx_o[s, rows, :] = dx.astype(bf16)

    finish(feeds, nb - 1)
    for k in range(2):
        total = feeds[k].add(nb - 1, True)
        gwo_o[:, halves[k]] = total[0:r, :]
        for c in range(cols):
            lo = c * width + halves[k].start
            gwu_o[:, lo : lo + half] = total[r + c * r : r + c * r + r, :]
        gwd_o[:, halves[k]] = total[r + cols * r :, :]
    todo = list(range(seqs * tiles))
    for step in range(nb):
        if todo:
            inputs(todo.pop(0))
        finish(heads + smalls, step)
        if step + 1 < nb:
            start(heads + smalls, step + 1)
    for i in todo:
        inputs(i)
    for k in range(2):
        total = heads[k].add(nb - 1, True)
        for j, ref in enumerate((gwq_o, gwk_o, gwv_o)):
            ref[:, halves[k]] = total[j * r : j * r + r, :]
    small_o[...] = smalls[0].add(nb - 1, True)


def pull_call(count, sub, mem_rows, r, fr, lengths, x, mem, q, k, v, qt, att, da, res, g1, part1, gvec, gub):
    seqs, length, width = x.shape
    keys = k.shape[1]
    ff = gub.shape[1]
    rows2 = part1.shape[-2]
    nb = count.bit_length() - 1
    cube = (2,) * nb
    block = min(512, length)
    half = width // 2
    shape = jax.ShapeDtypeStruct
    vm = pl.BlockSpec(memory_space=VMEM)

    def steps(tail, dtype):
        return [VMEM((2,) * (nb - 1 - step) + tail, dtype) for step in range(nb)]

    return pl.pallas_call(
        functools.partial(pull_kernel, count, sub, mem_rows, r, fr),
        out_shape=(
            shape((seqs, length, width), bf16),
            shape((r, width), f32),
            shape((r, width), f32),
            shape((r, width), f32),
            shape((r, width), f32),
            shape((r, ff), f32),
            shape((fr, width), f32),
            shape((16, 128), f32),
        ),
        in_specs=[pl.BlockSpec(memory_space=pltpu.SMEM)] + [vm] * 13,
        out_specs=[vm] * 8,
        scratch_shapes=[
            VMEM((2, keys, 128), bf16),
            VMEM((2, keys, 128), bf16),
            VMEM((128, keys), bf16),
            VMEM((2, 128, length), bf16),
        ]
        + [VMEM((keys, block), bf16)] * 4
        + [
            VMEM((seqs, length, width), bf16),
            VMEM((seqs, keys, width), bf16),
            VMEM((seqs, keys, width), bf16),
            VMEM((128, length), f32),
        ]
        + [VMEM((keys, 128), f32)] * 4
        + [VMEM(cube + (3 * r, width), bf16), VMEM(cube + (16, 128), f32)]
        + steps((rows2, half), bf16) * 2
        + steps((3 * r, half), bf16) * 2
        + steps((16, 128), f32)
        + [pltpu.SemaphoreType.DMA((5, nb)), pltpu.SemaphoreType.DMA((5, nb))],
        compiler_params=pltpu.CompilerParams(
            collective_id=1, has_side_effects=True, vmem_limit_bytes=60 * 2**20
        ),
        name="pull",
    )(lengths, x, mem, q, k, v, qt, att, da, res, g1, part1, gvec, gub)


DIMS = (1, 0, 0, 0, 0, 0, 0, 0, 0, 0, 0, 0, 0, 0, 0, 0)


def on_device(devices, inputs, lengths, *rest):
    params, cotangent = rest[:-1], rest[-1]
    width = inputs.shape[2]
    count = min(devices, width // 16)
    sub = devices // count
    sets = [list(range(g * sub, (g + 1) * sub)) for g in range(count)]
    if sub > 1:
        params = tuple(
            lax.all_gather(a, "dp", axis=d, tiled=True, axis_index_groups=sets)
            for a, d in zip(params, DIMS, strict=True)
        )
    (memory, wq, bq, wk, wv, bv, wo, bo, ga, sa, wu, bu, wd, bd, gb, sb) = params
    r, fr = wq.shape[0], wd.shape[0]
    mem_rows = memory.shape[0]

    def fill(a, lanes):
        return jnp.pad(a, ((0, 16 - a.shape[0]), (0, lanes - a.shape[1])))

    vecs = jnp.stack([bq, bv, bo, ga, sa, bd, gb, sb])
    small = jnp.concatenate(
        [memory[0:16], fill(memory[16:], r), fill(vecs, r), fill(bu[None], 128 - 3 * r)], 1
    )
    q, k, v, qt, att, g1, g2, vec, ub, mem = attend_call(
        count, sub, lengths, inputs, wq, wk, wv, wo, wu, wd, small, mem_rows
    )
    seqs, length = inputs.shape[:2]
    layer_out, res, datt, part1, gvec, gub = feed_call(
        inputs,
        att.reshape(seqs, width, length),
        cotangent,
        g2.reshape((count,) + g2.shape[-2:]),
        vec,
        ub,
        r,
        fr,
    )
    dx, gwq, gwk, gwv, gwo, gwu, gwd, tiny = pull_call(
        count, sub, mem_rows, r, fr, lengths, inputs, mem, q, k, v, qt, att, datt, res, g1,
        part1.reshape(g2.shape), gvec, gub,
    )
    gmem = jnp.concatenate([tiny[:, 0:r], tiny[0 : mem_rows - 16, r : 2 * r]], 0)
    gbq, gbv, gbo, gga, gsa, gbd, ggb, gsb = [tiny[j, 2 * r : 3 * r] for j in range(8)]
    gbu = tiny[0, 3 * r : 3 * r + fr]
    grads = (gmem, gwq, gbq, gwk, gwv, gbv, gwo, gbo, gga, gsa, gwu, gbu, gwd, gbd, ggb, gsb)
    if sub > 1:
        grads = tuple(
            lax.psum_scatter(a, "dp", scatter_dimension=d, tiled=True, axis_index_groups=sets)
            for a, d in zip(grads, DIMS, strict=True)
        )
    return (layer_out, dx) + grads


def solution(mesh):
    rows, row, mem = P("dp", None), P("dp"), P(None, "dp")
    full = P("dp", None, None)
    params = (mem, rows, row, rows, rows, row, rows, row, row, row, rows, row, rows, row, row, row)
    return jax.shard_map(
        functools.partial(on_device, mesh.shape["dp"]),
        mesh=mesh,
        in_specs=(full, P("dp")) + params + (full,),
        out_specs=(full, full) + params,
        check_vma=False,
    )
```

time: 1640 us -> 239 us (0.15)
  waiting for transfers between devices: 833 us -> 0 us
  matrix products: 311 us -> 0 us
  blocking collectives: 277 us -> 0 us
  Pallas kernels: 0 us -> 222 us
  other arithmetic: 101 us -> 2.03 us
  local copies, waits for them, and re-layouts: 93 us -> 13.6 us
    reduce_scatter x4 -> x0, waiting for transfers between devices: 431 us -> none  [the longest x1 140 us: on_device(): lax.psum_scatter(up_weight_grad, 'dp', scatter_dimension=0, tiled=True)]
    unnamed x12 -> x0, waiting for transfers between devices: 402 us -> none
    dot_general x52 -> x0, matrix products: 311 us -> none  [the longest x8 57.8 us: block_scores(): jnp.einsum('qhd,khd->hqk', query_block, all_keys, preferred_element_type=...]
    pallas_call x0 -> x3, Pallas kernels: none -> 222 us  [the longest x1 90.2 us: pull_call(): pl.pallas_call(functools.partial(pull_kernel, count, sub, mem_rows, r, fr...]
    all_gather x5 -> x0, blocking collectives: 197 us -> none  [the longest x1 41.3 us: on_device(): lax.all_gather(memory, 'dp', axis=1, tiled=True)]
    unnamed x2 -> x0, blocking collectives: 79.5 us -> none
    reduce_sum x14 -> x0, other arithmetic: 52.4 us -> none  [the longest x4 32.8 us: attend_sequence(): total = jnp.sum(expo, -1, keepdims=True)]
    convert_element_type x13 -> x0, other arithmetic: 46.8 us -> none  [the longest x4 46.8 us: attend_backward(): score_grad = centred.astype(jnp.bfloat16)]
  transfers between devices with their start and end apart: 9 -> 0, of which waited for: 7 -> 0; matrix products, arithmetic and copies ran while one was open for 14% -> 0% of each run, Pallas kernels for 0% -> 0%
where the time goes in v1:
time: 239 us
  Pallas kernels  222 us (93%)
  local copies, waits for them, and re-layouts  13.6 us (6%)
    pallas_call x1, Pallas kernels, pull_call(): pl.pallas_call(functools.partial(pull_kernel, count, sub, mem_rows, r, fr...  90.2 us
    pallas_call x1, Pallas kernels, attend_call(): pl.pallas_call(functools.partial(attend_kernel, count, sub, mem_rows), ou...  81.1 us
    pallas_call x1, Pallas kernels, feed_call(): pl.pallas_call(functools.partial(feed_kernel, r, fr, seqs * tiles), grid=...  51 us
    unnamed x22, local copies, waits for them, and re-layouts  8.42 us

profile of v1, /device:TPU:0, one launch (start us, length us, event | category | flops | bytes accessed | tf_op | source)
XLA Modules:
  0.0 238.7 jit_solution(5765540730572524744)
XLA Ops:
  0.7 0.8 stack.35
  1.5 0.8 copy.40
  2.2 0.8 slice.40
  3.0 0.1 copy.41
  3.1 1.3 fusion.6.small_ref
  4.4 81.1 %attend.1 = (bf16[2,1024,512]{2,1,0:T(8,128)(2,1)}, bf16[2,1056,512]{2,1,0:T(8,128)(2,1)}, bf16[2,1056,512]{2,1,0:T(8,128)(2,1)}, bf16[2,8,128,1024]{3,2,1,0:T(8...) custom-call(s32[2]{0:T(128)} %len_ref.3, ...), custom_call_target="tpu_custom_call" | custom-call | tf_op jit(solution)/shard_map/attend/pallas_call | solution.py:355
  85.5 51.0 %feed.1 = (bf16[2,1024,512]{2,1,0:T(8,128)(2,1)}, f32[2,1024,512]{2,1,0:T(8,128)}, bf16[2,1024,512]{2,1,0:T(8,128)(2,1)}, bf16[32,144,512]{2,1,0:T(8,128)(2,1)}, f32[8,512]{1,0:T(8,128)}, /*index=5*/f32[1,2048]{1,0:T(1,128)}) custom-call(bf16[2,1024,512]{2,1,0:T(8,128)(2,1)} %x_ref.5, bf16[2,512,1024]{2,1,0:T(8,128)(2,1)} %bitcast.32, ...), custom_call_target="tpu_custom_call" | custom-call | tf_op jit(solution)/shard_map/feed/pallas_call | solution.py:509
  136.6 90.2 %pull.1 = (bf16[2,1024,512]{2,1,0:T(8,128)(2,1)}, f32[16,512]{1,0:T(8,128)}, f32[16,512]{1,0:T(8,128)}, f32[16,512]{1,0:T(8,128)}, f32[16,512]{1,0:T(8,128)}, /*...) custom-call(s32[2]{0:T(128)} %len_ref.3, bf16[2,1024,512]{2,1,0:T(8,128)(2,1)} %x_ref.5, ...), custom_call_target="tpu_custom_call" | custom-call | tf_op jit(solution)/shard_map/pull/pallas_call | solution.py:753
  226.8 1.3 slice_bitcast_fusion.3
  228.1 0.8 slice.42
  228.8 1.6 slice_bitcast_fusion
  230.4 0.7 pad_maximum_fusion
  231.1 0.7 copy.39
  231.8 0.0 copy-start.5
  231.8 0.0 copy-start.4
  231.8 0.0 copy-start.3
  231.8 0.0 copy-start.2
  231.8 0.0 copy-start.1
  231.8 0.0 copy-start
  231.8 3.1 %copy.49 = bf16[2,1024,512]{2,1,0:T(8,128)(2,1)} copy(bf16[2,1024,512]{2,1,0:T(8,128)(2,1)} %get-tuple-element.111) | data formatting | bytes 4194304
  234.9 0.0 copy-done.5
  234.9 0.6 copy.50
  235.5 0.0 copy-done.4
  235.5 0.6 copy.51
  236.1 0.0 copy-done.3
  236.1 0.6 copy.52
  236.7 0.0 copy-done.2
  236.7 0.6 copy.53
  237.4 0.0 copy-done.1
  237.4 0.7 copy.54
  238.0 0.0 copy-done
  238.0 0.7 copy.55
Async XLA Ops:
  231.8 3.1 %copy-start.5 = (f32[16,512]{1,0:T(8,128)S(1)}, f32[16,512]{1,0:T(8,128)}, u32[]{:S(2)}) copy-start(f32[16,512]{1,0:T(8,128)} %get-tuple-element.113) | copy-start | bytes 98308
  231.8 3.7 %copy-start.4 = (f32[16,512]{1,0:T(8,128)S(1)}, f32[16,512]{1,0:T(8,128)}, u32[]{:S(2)}) copy-start(f32[16,512]{1,0:T(8,128)} %get-tuple-element.115) | copy-start | bytes 98308
  231.8 4.4 %copy-start.3 = (f32[16,512]{1,0:T(8,128)S(1)}, f32[16,512]{1,0:T(8,128)}, u32[]{:S(2)}) copy-start(f32[16,512]{1,0:T(8,128)} %get-tuple-element.116) | copy-start | bytes 98308
  231.8 5.0 %copy-start.2 = (f32[16,512]{1,0:T(8,128)S(1)}, f32[16,512]{1,0:T(8,128)}, u32[]{:S(2)}) copy-start(f32[16,512]{1,0:T(8,128)} %get-tuple-element.118) | copy-start | bytes 98308
  231.8 5.6 %copy-start.1 = (f32[16,2048]{1,0:T(8,128)S(1)}, f32[16,2048]{1,0:T(8,128)}, u32[]{:S(2)}) copy-start(f32[16,2048]{1,0:T(8,128)} %get-tuple-element.122) | copy-start | bytes 393220
  231.8 6.2 %copy-start = (f32[64,512]{1,0:T(8,128)S(1)}, f32[64,512]{1,0:T(8,128)}, u32[]{:S(2)}) copy-start(f32[64,512]{1,0:T(8,128)} %get-tuple-element.124) | copy-start | bytes 393220

commit v2 on v1

v2 whole, which is shorter than its diff:
```python
import functools

import jax
import jax.numpy as jnp
from jax import lax
from jax.experimental import pallas as pl
from jax.experimental.pallas import tpu as pltpu
from jax.sharding import PartitionSpec as P

HEADS = 8
HEAD_DIM = 64
EPSILON = 1e-05
LOG2E = 1.4426950408889634
LN2 = 0.6931471805599453
GELU_A = 0.7978845608028654
GELU_B = GELU_A * 0.044715
HIDE = -1e30
VEC = 20
KEY_PAD = 32

f32 = jnp.float32
bf16 = jnp.bfloat16
VMEM = pltpu.VMEM
MESH = pl.DeviceIdType.MESH
NN = (((1,), (0,)), ((), ()))
NT = (((1,), (1,)), ((), ()))
TN = (((0,), (0,)), ((), ()))


def dg(left, right, dims):
    return lax.dot_general(left, right, dims, preferred_element_type=f32)


def col_sum(value):
    return jnp.sum(value, 0, keepdims=True)


class Cube:
    def __init__(self, count, sub):
        self.count, self.sub = count, sub
        self.nb = count.bit_length() - 1
        device = lax.axis_index("dp")
        self.device = device
        me = device // sub
        self.bits = [(me // (2**b)) % 2 for b in range(self.nb)]
        self.msb_first = tuple(range(self.nb - 1, -1, -1))

    def partner(self, flips):
        to = self.device
        for b in flips:
            to = to + (1 - 2 * self.bits[b]) * (2**b * self.sub)
        return (to,)

    def barrier(self, routes):
        groups = sorted({flips for route in routes for group in route for flips in masks(group)})
        sem = pltpu.get_barrier_semaphore()
        for flips in groups:
            pl.semaphore_signal(sem, inc=1, device_id=self.partner(flips), device_id_type=MESH)
        pl.semaphore_wait(sem, len(groups))

    def own(self):
        return tuple(self.bits[b] for b in self.msb_first)


def masks(group):
    return [
        tuple(b for k, b in enumerate(group) if (m >> k) & 1) for m in range(1, 2 ** len(group))
    ]


def routes(nb):
    if nb >= 4:
        far = list(range(nb - 1, 2, -1))
        groups = [tuple(far[k : k + 2]) for k in range(0, len(far), 2)]
        return (groups + [(1,), (2,), (0,)], groups + [(2,), (1,), (0,)])
    return ([(b,) for b in range(nb - 1, -1, -1)],) * 2


def most(route):
    return max(2 ** len(group) - 1 for group in route)


def gather_copies(cube, ref, route, step, lanes, send, recv):
    done = {b for group in route[:step] for b in group}
    idx = tuple(slice(None) if c in done else cube.bits[c] for c in cube.msb_first)
    view = ref.at[idx + (slice(None), lanes)]
    return [
        pltpu.make_async_remote_copy(
            src_ref=view,
            dst_ref=view,
            send_sem=send.at[step, k],
            recv_sem=recv.at[step, k],
            device_id=cube.partner(flips),
            device_id_type=MESH,
        )
        for k, flips in enumerate(masks(route[step]))
    ]


class Scatter:
    def __init__(self, cube, source, lanes, route, bufs, send, recv):
        self.cube, self.source, self.lanes, self.route = cube, source, lanes, route
        self.bufs, self.send, self.recv = bufs, send, recv
        self.steps = len(route)

    def _piece(self, step, flips, rest=None):
        cube = self.cube
        gone = {b for group in self.route[:step] for b in group}
        left = [c for c in cube.msb_first if c not in gone]
        rest = iter(rest) if rest is not None else None
        idx = ()
        for c in left:
            if c in self.route[step]:
                idx += (1 - cube.bits[c] if c in flips else cube.bits[c],)
            else:
                idx += (slice(None) if rest is None else next(rest),)
        if step == 0:
            return self.source, idx + (slice(None), self.lanes)
        return self.bufs[step - 1].at[0], idx

    def copies(self, step):
        out = []
        for k, flips in enumerate(masks(self.route[step])):
            ref, idx = self._piece(step, flips)
            out.append(
                pltpu.make_async_remote_copy(
                    src_ref=ref.at[idx],
                    dst_ref=self.bufs[step].at[k],
                    send_sem=self.send.at[step, k],
                    recv_sem=self.recv.at[step, k],
                    device_id=self.cube.partner(flips),
                    device_id_type=MESH,
                )
            )
        return out

    def total(self, step, rest=None):
        ref, idx = self._piece(step, (), rest)
        value = ref[idx].astype(f32)
        for k in range(2 ** len(self.route[step]) - 1):
            value = value + self.bufs[step][(k,) + tuple(rest or ())].astype(f32)
        return value

    def add(self, step):
        free = self.cube.nb - sum(len(group) for group in self.route[: step + 1])
        into = self.bufs[step]
        for flat in range(2**free):
            rest = tuple((flat >> (free - 1 - k)) & 1 for k in range(free))
            into[(0,) + rest] = self.total(step, rest).astype(into.dtype)


def scatter_bufs(nb, route, tail, dtype):
    bufs, left = [], nb
    for group in route:
        left -= len(group)
        bufs.append(VMEM((2 ** len(group) - 1,) + (2,) * left + tail, dtype))
    return bufs


def attend_kernel(
    count, sub, mem_rows,
    len_ref, x_any, wq_ref, wk_ref, wv_ref, wo_ref, wu_ref, wd_ref, memt_ref, ub_ref, *rest,
):
    vec_refs, rest = rest[:8], rest[8:]
    (
    q_any, k_any, v_any, qt_any, att_any, g1_any, g2, vec_o, ub_o, mem_o,
    x_ref, q_o, k_o, v_o, qt_o, att_o, g1,
    gs, ksel, vt_s, score_a, score_b, top_a, top_b,
    flat_s, wide_s,
    local, x_sem, out_sem, head_sem, send1, recv1, send2, recv2, send3, recv3,
    ) = rest
    cube = Cube(count, sub)
    nb = cube.nb
    seqs, length, width = x_ref.shape
    keys = k_o.shape[2]
    mem_pad = keys - length
    r = wq_ref.shape[0]
    ff = wu_ref.shape[1]
    cols = ff // width
    fr = wd_ref.shape[0]
    own = cube.own()
    ways = routes(nb)
    steps = len(ways[0])
    half = width // 2
    halves = (slice(0, half), slice(half, width))
    whole = (slice(None), slice(None))
    x_load = pltpu.make_async_copy(x_any, x_ref, x_sem)
    x_load.start()
    for j, ref in enumerate((wq_ref, wk_ref, wv_ref)):
        g1[own + (slice(j * r, j * r + r), slice(None))] = ref[...]
    wide_s[...] = jnp.zeros_like(wide_s)
    flat_s[...] = jnp.zeros_like(flat_s)
    for j, ref in enumerate(vec_refs):
        wide_s[VEC + j : VEC + j + 1, 0:r] = ref[...].astype(f32)
    flat_s[0:r, 0:mem_rows] = memt_ref[...].astype(f32)
    flat_s[0:1, 64 : 64 + fr] = ub_ref[...].astype(f32)
    gs[own + whole] = (flat_s[...] + wide_s[...].T[0:16, :]).astype(bf16)
    parts = [(wo_ref, slice(0, r))]
    parts += [
        (wu_ref.at[:, c * width : (c + 1) * width], slice(r + c * r, r + c * r + r))
        for c in range(cols)
    ]
    parts += [(wd_ref, slice(r + cols * r, r + cols * r + fr))]
    moves = [
        pltpu.make_async_copy(ref, g2.at[own + (rows, slice(None))], local.at[j])
        for j, (ref, rows) in enumerate(parts)
    ]
    for move in moves:
        move.start()
    cube.barrier(ways)

    def first(step):
        copies = []
        for k in range(2):
            copies += gather_copies(cube, g1, ways[k], step, halves[k], send1.at[k], recv1.at[k])
        return copies + gather_copies(cube, gs, ways[0], step, slice(None), send3, recv3)

    chunks = 4
    chunk = width // chunks

    def second(c, step):
        lanes = slice(c * chunk, (c + 1) * chunk)
        return gather_copies(cube, g2, ways[c % 2], step, lanes, send2.at[c], recv2.at[c])

    def advance(c, step):
        if step > 0:
            for copy in second(c, step - 1):
                copy.wait()
        if step < steps:
            for copy in second(c, step):
                copy.start()

    for step in range(steps):
        copies = first(step)
        for copy in copies:
            copy.start()
        if step == 0:
            for move in moves:
                move.wait()
        for copy in copies:
            copy.wait()
        for slot, c, part in ((0, 0, 0), (1, 1, 0), (2, 0, 1), (2, 1, 1), (2, 2, 0)):
            if step == slot:
                advance(c, part)
    g1_out = pltpu.make_async_copy(g1, g1_any, out_sem.at[0])
    g1_out.start()
    x_load.wait()

    lane = lax.broadcasted_iota(jnp.int32, (1, 128), 1)
    every = gs[...].astype(f32).reshape(width, 128).T
    mem_o[0:16, :] = every[0:16, :].astype(bf16)
    rest_row = lax.broadcasted_iota(jnp.int32, (16, width), 0)
    mem_o[16:32, :] = jnp.where(rest_row < mem_rows - 16, every[16:32, :], 0.0).astype(bf16)
    vec_o[...] = every[VEC : VEC + 8, :]
    ups = [jnp.zeros((16, 128), f32) for _ in range(ff // 128)]
    for i in range(count):
        at = tuple((i >> b) & 1 for b in cube.msb_first)
        to = (i * fr) % 128
        here = (lane >= to) & (lane < to + fr)
        rolled = pltpu.roll(gs[at + whole].astype(f32), (to - 64) % 128, 1)
        ups[i * fr // 128] = ups[i * fr // 128] + jnp.where(here, rolled, 0.0)
    for g in range(ff // 128):
        ub_o[:, 128 * g : 128 * g + 128] = ups[g][0:1, :]

    def weight(j):
        return g1[(slice(None),) * nb + (slice(j * r, j * r + r), slice(None))].reshape(width, width)

    bq = vec_o[0:1, :]
    bv = vec_o[1:2, :]

    def put_keys(s, rows, kk, vv, bias):
        kb = kk.astype(bf16)
        vb = vv.astype(bf16)
        for p in range(HEADS // 2):
            k_o[s, p, rows, :] = kb[:, 128 * p : 128 * p + 128]
            v_o[s, p, rows, :] = vb[:, 128 * p : 128 * p + 128]
        for h in range(HEADS):
            p, o = h // 2, 64 * (1 - h % 2)
            pattern = jnp.where(
                lane == o, bias, jnp.where((lane > o) & (lane <= o + 3), 1.0, 0.0)
            ).astype(bf16)
            mine = (lane < 64) if h % 2 == 0 else (lane >= 64)
            ksel[s, h, rows, :] = jnp.where(mine, kb[:, 128 * p : 128 * p + 128], pattern)
        vt = vb.T
        for h in range(HEADS):
            vt_s[s, h, 0:64, rows] = vt[64 * h : 64 * h + 64, :]

    top_row = lax.broadcasted_iota(jnp.int32, (16, keys), 0)
    ones = jnp.where(top_row == 0, 1.0, 0.0).astype(bf16)
    for s in range(seqs):
        for h in range(HEADS):
            vt_s[s, h, 64:80, :] = ones
    mem = mem_o[...]
    mem_keys = dg(mem, weight(1), NN)
    mem_values = dg(mem, weight(2), NN) + bv
    mem_row = lax.broadcasted_iota(jnp.int32, (mem_pad, 1), 0)
    for s in range(seqs):
        put_keys(
            s, slice(length, keys), mem_keys, mem_values, jnp.where(mem_row < mem_rows, 0.0, HIDE)
        )
    tile = 512
    tiles = length // tile
    aux = jnp.where(lax.broadcasted_iota(jnp.int32, (64, tile), 0) == 0, 1.0, 0.0).astype(bf16)

    @pl.loop(0, seqs * tiles)
    def _(i):
        for slot, c, step in ((0, 3, 0), (2, 0, 2), (2, 1, 2), (3, 2, 1)):

            @pl.when(i == slot)
            def _():
                advance(c, step)

        s = i // tiles
        start = pl.multiple_of((i % tiles) * tile, tile)
        rows = pl.ds(start, tile)
        xt = x_ref[s, rows, :]
        qb = ((dg(xt, weight(0), NN) + bq) * (LOG2E * HEAD_DIM**-0.5)).astype(bf16)
        for p in range(HEADS // 2):
            q_o[s, p, rows, :] = qb[:, 128 * p : 128 * p + 128]
        qt = qb.T
        for h in range(HEADS):
            e = h % 2
            qt_o[s, h, 64 * e : 64 * e + 64, rows] = qt[64 * h : 64 * h + 64, :]
            qt_o[s, h, 64 * (1 - e) : 64 * (1 - e) + 64, rows] = aux
        row = lax.broadcasted_iota(jnp.int32, (tile, 1), 0) + start
        put_keys(
            s,
            rows,
            dg(xt, weight(1), NN),
            dg(xt, weight(2), NN) + bv,
            jnp.where(row < len_ref[s], 0.0, HIDE),
        )

    block = score_a.shape[1]
    per_head = length // block
    blocks = seqs * HEADS * per_head

    def place(i):
        s = i // (HEADS * per_head)
        h = (i // per_head) % HEADS
        return s, h, pl.ds(pl.multiple_of((i % per_head) * block, block), block)

    def scores(i, score, top):
        s, h, at = place(i)
        value = dg(ksel[s, h], qt_o[s, h, :, at], NN)
        score[...] = value
        top[...] = jnp.max(value, 0, keepdims=True)

    def mix(i, score, top):
        s, h, at = place(i)
        peak = top[...]
        probs = jnp.exp2(score[...] - peak).astype(bf16)
        mixed = dg(vt_s[s, h], probs, NN)
        total = mixed[64:65, :]
        att_o[s, h, :, at] = (mixed[0:64, :] / total).astype(bf16)
        stat = peak + jnp.log2(total)
        hi = stat.astype(bf16).astype(f32)
        mid = (stat - hi).astype(bf16).astype(f32)
        low = stat - hi - mid
        row = lax.broadcasted_iota(jnp.int32, (16, block), 0)
        extra = jnp.where(
            row == 0,
            1.0,
            jnp.where(row == 1, -hi, jnp.where(row == 2, -mid, jnp.where(row == 3, -low, 0.0))),
        )
        o = pl.multiple_of(64 * (1 - h % 2), 64)
        qt_o[s, h, pl.ds(o, 16), at] = extra.astype(bf16)

    outs = [
        pltpu.make_async_copy(src, dst, out_sem.at[1 + n])
        for n, (src, dst) in enumerate(((q_o, q_any), (k_o, k_any), (v_o, v_any)))
    ]
    for out in outs:
        out.start()
    scores(0, score_a, top_a)
    turns = blocks // 2
    heads_a_turn = max(1, 2 // per_head)

    def head_outs(j):
        s, h = j // HEADS, j % HEADS
        return [
            pltpu.make_async_copy(qt_o.at[s, h], qt_any.at[s, h], head_sem.at[j, 0]),
            pltpu.make_async_copy(att_o.at[s, h], att_any.at[s, h], head_sem.at[j, 1]),
        ]

    plan = ((0, 3, 1), (3, 0, 3), (4, 1, 3), (4, 2, 2), (5, 3, 2), (10, 2, 3), (11, 3, 3))

    @pl.loop(0, turns)
    def _(j):
        for slot, c, step in plan:

            @pl.when(j == (slot * turns) // 16)
            def _():
                advance(c, step)

        scores(2 * j + 1, score_b, top_b)
        mix(2 * j, score_a, top_a)
        scores(jnp.minimum(2 * j + 2, blocks - 1), score_a, top_a)
        mix(2 * j + 1, score_b, top_b)
        for k in range(heads_a_turn):
            for out in head_outs(j * heads_a_turn + k):
                out.start()

    for c in range(chunks):
        advance(c, steps)
    for out in outs + [g1_out]:
        out.wait()

    @pl.loop(0, seqs * HEADS)
    def _(j):
        for out in head_outs(j):
            out.wait()


def attend_call(count, sub, lengths, x, wq, wk, wv, wo, wu, wd, memt, ub, vecs, mem_rows):
    seqs, length, width = x.shape
    r, ff, fr = wq.shape[0], wu.shape[1], wd.shape[0]
    rows2 = r + (ff // width) * r + fr
    keys = length + KEY_PAD
    nb = count.bit_length() - 1
    cube = (2,) * nb
    way = routes(nb)[0]
    links = (len(way), most(way))
    block = min(512, length)
    pairs = HEADS // 2
    shape = jax.ShapeDtypeStruct
    vm = pl.BlockSpec(memory_space=VMEM)
    hbm = pl.BlockSpec(memory_space=pl.ANY)
    dma = pltpu.SemaphoreType.DMA
    kept = (
        shape((seqs, pairs, length, 128), bf16),
        shape((seqs, pairs, keys, 128), bf16),
        shape((seqs, pairs, keys, 128), bf16),
        shape((seqs, HEADS, 128, length), bf16),
        shape((seqs, HEADS, HEAD_DIM, length), bf16),
        shape(cube + (3 * r, width), bf16),
    )
    return pl.pallas_call(
        functools.partial(attend_kernel, count, sub, mem_rows),
        out_shape=kept
        + (
            shape(cube + (rows2, width), bf16),
            shape((8, width), f32),
            shape((1, ff), f32),
            shape((KEY_PAD, width), bf16),
        ),
        in_specs=[pl.BlockSpec(memory_space=pltpu.SMEM), hbm] + [vm] * 16,
        out_specs=[hbm] * 7 + [vm] * 3,
        scratch_shapes=[VMEM(x.shape, bf16)]
        + [VMEM(a.shape, bf16) for a in kept]
        + [
            VMEM(cube + (16, 128), bf16),
            VMEM((seqs, HEADS, keys, 128), bf16),
            VMEM((seqs, HEADS, 80, keys), bf16),
            VMEM((keys, block), f32),
            VMEM((keys, block), f32),
            VMEM((1, block), f32),
            VMEM((1, block), f32),
            VMEM((16, 128), f32),
            VMEM((128, 128), f32),
            dma((2 + ff // width,)),
            dma,
            dma((4,)),
            dma((seqs * HEADS, 2)),
            dma((2,) + links),
            dma((2,) + links),
            dma((4,) + links),
            dma((4,) + links),
            dma(links),
            dma(links),
        ],
        compiler_params=pltpu.CompilerParams(
            collective_id=0, has_side_effects=True, vmem_limit_bytes=60 * 2**20
        ),
        name="attend",
    )(lengths, x, wq, wk, wv, wo, wu, wd, memt, ub, *vecs)


def norm_forward(value, gain, shift):
    center = value - jnp.mean(value, -1, keepdims=True)
    inverse = lax.rsqrt(jnp.mean(center * center, -1, keepdims=True) + EPSILON)
    normed = center * inverse
    return normed * gain + shift, normed, inverse


def norm_backward(grad, normed, inverse, gain):
    scaled = grad * gain
    return inverse * (
        scaled
        - jnp.mean(scaled, -1, keepdims=True)
        - normed * jnp.mean(scaled * normed, -1, keepdims=True)
    )


def feed_kernel(
    r, fr, steps,
    x_ref, att_ref, dy_ref, g2, vec, ub,
    out_o, res_o, datt_o, part_o, gvec, gub,
    slope_s, act_s, gwo, gwu, gwd,
):
    i = pl.program_id(0)
    rows, width = x_ref.shape[1:]
    count = g2.shape[0]
    cols = g2.shape[1] // r - 1 - fr // r
    per = width // fr

    @pl.when(i == 0)
    def _():
        for ref in (gwo, gwu, gwd, gvec, gub):
            ref[...] = jnp.zeros_like(ref)

    bo, ga, sa, bd, gb, sb = [vec[j : j + 1, :] for j in range(2, 8)]

    def wo():
        return g2[:, 0:r, :].reshape(width, width)

    def wu(c):
        return g2[:, r + c * r : r + c * r + r, :].reshape(width, width)

    def wd(c):
        return g2[c * per : (c + 1) * per, r + cols * r :, :].reshape(width, width)

    att = att_ref[0]
    hidden, normed1, inverse1 = norm_forward(x_ref[0].astype(f32) + dg(att, wo(), TN) + bo, ga, sa)
    low = hidden.astype(bf16)
    outer = hidden + bd
    for c in range(cols):
        at = slice(c * width, (c + 1) * width)
        u = dg(low, wu(c), NN) + ub[:, at]
        u2 = u * u
        t = jnp.tanh(u * (GELU_A + GELU_B * u2))
        hu = 0.5 * u
        act = (hu + hu * t).astype(bf16)
        act_s[c] = act
        slope_s[c] = (
            (0.5 + 0.5 * t) + (hu * (1.0 - t * t)) * (GELU_A + 3.0 * GELU_B * u2)
        ).astype(bf16)
        outer = outer + dg(act, wd(c), NN)
    out, normed2, inverse2 = norm_forward(outer, gb, sb)
    out_o[0] = out.astype(bf16)
    dy = dy_ref[0].astype(f32)
    gvec[6:7, :] += col_sum(dy * normed2)
    gvec[7:8, :] += col_sum(dy)
    d_res2 = norm_backward(dy, normed2, inverse2, gb)
    d_outer = d_res2.astype(bf16)
    gvec[5:6, :] += col_sum(d_outer.astype(f32))
    d_hidden = d_res2
    for c in range(cols):
        at = slice(c * width, (c + 1) * width)
        d_act = dg(d_outer, wd(c), NT)
        d_inner = (d_act * slope_s[c].astype(f32)).astype(bf16)
        gwd[at, :] += dg(act_s[c], d_outer, TN)
        gwu[:, at] += dg(low, d_inner, TN)
        gub[:, at] += col_sum(d_inner.astype(f32))
        d_hidden = d_hidden + dg(d_inner, wu(c), NT)
    gvec[3:4, :] += col_sum(d_hidden * normed1)
    gvec[4:5, :] += col_sum(d_hidden)
    d_res1 = norm_backward(d_hidden, normed1, inverse1, ga)
    res_o[0] = d_res1
    d_branch = d_res1.astype(bf16)
    gvec[2:3, :] += col_sum(d_branch.astype(f32))
    gwo[...] += dg(att, d_branch, NN)
    d_att = dg(d_branch, wo(), NT).astype(bf16)
    for p in range(width // 128):
        datt_o[0, p] = d_att[:, 128 * p : 128 * p + 128]

    @pl.when(i == steps - 1)
    def _():
        part_o[:, 0:r, :] = gwo[...].astype(bf16).reshape(count, r, width)
        for c in range(cols):
            part_o[:, r + c * r : r + c * r + r, :] = (
                gwu[:, c * width : (c + 1) * width].astype(bf16).reshape(count, r, width)
            )
        part_o[:, r + cols * r :, :] = gwd[...].astype(bf16).reshape(count, fr, width)


def feed_call(x, att, dy, g2, vec, ub, r, fr):
    seqs, length, width = x.shape
    ff = ub.shape[1]
    tile = min(512, length)
    tiles = length // tile
    shape = jax.ShapeDtypeStruct
    rows = pl.BlockSpec((1, tile, width), lambda i: (i // tiles, i % tiles, 0))

    def full(a):
        return pl.BlockSpec(a.shape, lambda i: (0,) * len(a.shape))

    outs = (
        shape((seqs, length, width), bf16),
        shape((seqs, length, width), f32),
        shape((seqs, width // 128, length, 128), bf16),
        shape(g2.shape, bf16),
        shape((8, width), f32),
        shape((1, ff), f32),
    )
    return pl.pallas_call(
        functools.partial(feed_kernel, r, fr, seqs * tiles),
        grid=(seqs * tiles,),
        out_shape=outs,
        in_specs=[
            rows,
            pl.BlockSpec((1, width, tile), lambda i: (i // tiles, 0, i % tiles)),
            rows,
            full(g2),
            full(vec),
            full(ub),
        ],
        out_specs=[
            rows,
            rows,
            pl.BlockSpec((1, width // 128, tile, 128), lambda i: (i // tiles, 0, i % tiles, 0)),
        ]
        + [full(a) for a in outs[3:]],
        scratch_shapes=[
            VMEM((ff // width, tile, width), bf16),
            VMEM((ff // width, tile, width), bf16),
            VMEM((width, width), f32),
            VMEM((width, ff), f32),
            VMEM((ff, width), f32),
        ],
        compiler_params=pltpu.CompilerParams(vmem_limit_bytes=60 * 2**20),
        name="feed",
    )(x, att, dy, g2, vec, ub)


def pull_kernel(
    count, sub, mem_rows, r, fr,
    len_ref, x_any, mem_ref, q_any, k_any, v_any, qt_any, att_any, da_any, res_any, g1_any, part1,
    gvec_ref, gub_ref,
    dx_any, sums_o, small_o,
    x_ref, q_ref, k_ref, v_ref, qt_ref, att_ref, da_ref, res_ref, g1, dx_o,
    ksel, vsel, kt, dot_s, p_a, d_a, p_b, d_b, dq_s, dk_s, dv_s, dqt,
    dv_0, dv_1, dk_0, dk_1, part2, small_s, *rest,
):
    cube = Cube(count, sub)
    nb = cube.nb
    ways = [list(reversed(route)) for route in routes(nb)]
    steps = len(ways[0])
    bufs = [rest[k * steps : (k + 1) * steps] for k in range(5)]
    send, recv, load_sem, late_sem, out_sem = rest[5 * steps :]
    seqs, length, width = x_ref.shape
    keys = k_ref.shape[2]
    ff = gub_ref.shape[1]
    cols = ff // width
    half = width // 2
    halves = (slice(0, half), slice(half, width))
    pairs = HEADS // 2
    feeds = [
        Scatter(cube, part1, halves[k], ways[k], bufs[k], send.at[k], recv.at[k]) for k in range(2)
    ]
    heads = [
        Scatter(cube, part2, halves[k], ways[k], bufs[2 + k], send.at[2 + k], recv.at[2 + k])
        for k in range(2)
    ]
    smalls = Scatter(cube, small_s, slice(None), ways[0], bufs[4], send.at[4], recv.at[4])

    def start(group, step):
        for part in group:
            for copy in part.copies(step):
                copy.start()

    def finish(group, step):
        for part in group:
            for copy in part.copies(step):
                copy.wait()
        if step < steps - 1:
            for part in group:
                part.add(step)

    def loads(j):
        p, s = j // seqs, j % seqs
        own = ((q_any, q_ref), (k_any, k_ref), (v_any, v_ref), (da_any, da_ref))
        out = [
            pltpu.make_async_copy(a.at[s, p], b.at[s, p], load_sem.at[j, n])
            for n, (a, b) in enumerate(own)
        ]
        both = pl.ds(2 * p, 2)
        return out + [
            pltpu.make_async_copy(a.at[s, both], b.at[s, both], load_sem.at[j, 4 + n])
            for n, (a, b) in enumerate(((qt_any, qt_ref), (att_any, att_ref)))
        ]

    late = [
        pltpu.make_async_copy(a, b, late_sem.at[n])
        for n, (a, b) in enumerate(((x_any, x_ref), (g1_any, g1), (res_any, res_ref)))
    ]

    @pl.loop(0, seqs * pairs)
    def _(j):
        for load in loads(j):
            load.start()

    for load in late:
        load.start()
    cube.barrier(ways)
    start(feeds, 0)

    lane = lax.broadcasted_iota(jnp.int32, (1, 128), 1)
    key_row = lax.broadcasted_iota(jnp.int32, (keys, 1), 0)
    block = p_a.shape[1]
    per_head = length // block
    dv_t, dk_t = (dv_0, dv_1), (dk_0, dk_1)
    temp = ((p_a, d_a), (p_b, d_b))

    def pair(j):
        p, s = j // seqs, j % seqs
        at = pl.ds(pl.multiple_of(128 * p, 128), 128)
        kp = k_ref[s, p]
        vp = v_ref[s, p]
        kt[...] = kp.T
        da = da_ref[s, p]
        dat = da.T
        seen = (key_row < len_ref[s]) | ((key_row >= length) & (key_row < length + mem_rows))
        bias = jnp.where(seen, 0.0, HIDE)
        for e in range(2):
            o = 64 * (1 - e)
            mine = (lane < 64) if e == 0 else (lane >= 64)
            pattern = jnp.where(
                lane == o, bias, jnp.where((lane > o) & (lane <= o + 3), 1.0, 0.0)
            ).astype(bf16)
            ksel[e] = jnp.where(mine, kp, pattern)
            vsel[e] = jnp.where(
                mine, vp, jnp.where((lane >= o) & (lane < o + 2), 1.0, 0.0).astype(bf16)
            )
            dt = dat[64 * e : 64 * e + 64, :]
            delta = col_sum(dt.astype(f32) * att_ref[s, 2 * p + e].astype(f32))
            hi = delta.astype(bf16).astype(f32)
            row = lax.broadcasted_iota(jnp.int32, (64, length), 0)
            dot_s[e, 64 * e : 64 * e + 64, :] = dt
            dot_s[e, o : o + 64, :] = jnp.where(
                row == 0, -hi, jnp.where(row == 1, hi - delta, 0.0)
            ).astype(bf16)

        def probs(b):
            e, c = b // per_head, b % per_head
            cut = slice(c * block, (c + 1) * block)
            prob = jnp.exp2(dg(ksel[e], qt_ref[s, 2 * p + e, :, cut], NN))
            grad = dg(vsel[e], dot_s[e, :, cut], NN)
            temp[b % 2][0][...] = prob.astype(bf16)
            temp[b % 2][1][...] = (prob * grad).astype(bf16)

        def pulls(b):
            e, c = b // per_head, b % per_head
            cut = slice(c * block, (c + 1) * block)
            prob, grad = temp[b % 2]
            dv = dg(prob[...], da[cut, :], NN)
            dk = dg(grad[...], q_ref[s, p, cut, :], NN)
            dqt[64 * e : 64 * e + 64, cut] = dg(kt[64 * e : 64 * e + 64, :], grad[...], NN)
            if c == 0:
                dv_t[e][...] = dv
                dk_t[e][...] = dk
            else:
                dv_t[e][...] += dv
                dk_t[e][...] += dk

        probs(0)
        for b in range(2 * per_head):
            if b + 1 < 2 * per_head:
                probs(b + 1)
            pulls(b)
        even = lane < 64
        dv_s[s, :, at] = jnp.where(even, dv_0[...], dv_1[...]).astype(bf16)
        dk_s[s, :, at] = (jnp.where(even, dk_0[...], dk_1[...]) * LN2).astype(bf16)
        dq_s[s, :, at] = dqt[...].T.astype(bf16)

    def weight(j):
        return g1[(slice(None),) * nb + (slice(j * r, j * r + r), slice(None))].reshape(width, width)

    scale = HEAD_DIM**-0.5
    tail = slice(length, keys)

    def terms(k):
        mem = mem_ref[...]
        for j, ref in enumerate((dq_s, dk_s, dv_s)):
            total = 0.0
            for s in range(seqs):
                total = total + dg(x_ref[s], ref[s, 0:length, halves[k]], TN)
                if j:
                    total = total + dg(mem, ref[s, tail, halves[k]], TN)
            if j == 0:
                total = total * scale
            cuts = (slice(None),) * nb + (slice(j * r, j * r + r), halves[k])
            part2[cuts] = total.astype(bf16).reshape((2,) * nb + (r, half))

    turns = seqs * pairs

    @pl.loop(0, turns)
    def _(j):
        for load in loads(j):
            load.wait()

        for slot, step in ((1, 0), (3, 1), (4, 2)):

            @pl.when(j == (slot * turns) // 8)
            def _():
                finish(feeds, step)
                start(feeds, step + 1)

        @pl.when(j == turns // 2)
        def _():
            for load in late:
                load.wait()
            terms(0)
            start(heads[:1], 0)

        for slot, step in ((5, 0), (6, 1), (7, 2)):

            @pl.when(j == (slot * turns) // 8)
            def _():
                finish(heads[:1], step)
                start(heads[:1], step + 1)

        pair(j)

    terms(1)
    start(heads[1:], 0)
    bq = sum(col_sum(dq_s[s].astype(f32)) for s in range(seqs)) * scale
    bv = sum(col_sum(dv_s[s].astype(f32)) for s in range(seqs))
    gmem = sum(
        dg(dk_s[s, tail, :], weight(1), NT) + dg(dv_s[s, tail, :], weight(2), NT)
        for s in range(seqs)
    )
    vec_row = lax.broadcasted_iota(jnp.int32, (8, width), 0)
    vecs = jnp.where(vec_row == 0, bq, jnp.where(vec_row == 1, bv, gvec_ref[...]))
    flat = jnp.concatenate(
        [
            gmem[0:16, :],
            jnp.concatenate([gmem[16:20, :], vecs[0:4, :]], 0),
            jnp.concatenate([vecs[4:8, :], jnp.zeros((4, width), f32)], 0),
            jnp.zeros((96, width), f32),
        ],
        0,
    )
    small_s[...] = flat.T.reshape((2,) * nb + (16, 128))
    for i in range(count):
        at = tuple((i >> b) & 1 for b in cube.msb_first)
        off = (i * fr) % 128
        up = jnp.broadcast_to(gub_ref[:, i * fr - off : i * fr - off + 128], (8, 128))
        up = pltpu.roll(up, (64 - off) % 128, 1)
        small_s[at + (slice(0, 1), slice(64, 64 + fr))] = up[0:1, 64 : 64 + fr]
    start([smalls], 0)
    tile = 512
    tiles = length // tile

    def inputs(i):
        s, rows = i // tiles, pl.ds((i % tiles) * tile, tile)
        dx = res_ref[s, rows, :] + dg(dq_s[s, rows, :], weight(0), NT) * scale
        dx = dx + dg(dk_s[s, rows, :], weight(1), NT) + dg(dv_s[s, rows, :], weight(2), NT)
        dx_o[s, rows, :] = dx.astype(bf16)
        out = pltpu.make_async_copy(dx_o.at[s, rows], dx_any.at[s, rows], out_sem.at[i])
        out.start()
        return out

    def total(part, lo, hi, k):
        value = part.total(steps - 1)
        sums_o[lo:hi, halves[k]] = value

    todo = list(range(seqs * tiles))
    outs = []
    group = heads[1:] + [smalls]
    for step in range(steps):
        if todo:
            outs.append(inputs(todo.pop(0)))
        if step == steps - 2:
            finish(feeds, steps - 1)
            for k in range(2):
                total(feeds[k], 3 * r, sums_o.shape[0], k)
            finish(heads[:1], steps - 1)
            total(heads[0], 0, 3 * r, 0)
        finish(group, step)
        if step + 1 < steps:
            start(group, step + 1)
    for i in todo:
        outs.append(inputs(i))
    total(heads[1], 0, 3 * r, 1)
    small_o[...] = smalls.total(steps - 1)
    for out in outs:
        out.wait()


def pull_call(count, sub, mem_rows, r, fr, lengths, x, mem, q, k, v, qt, att, da, res, g1, part1, gvec, gub):
    seqs, length, width = x.shape
    keys = k.shape[2]
    rows2 = part1.shape[-2]
    nb = count.bit_length() - 1
    cube = (2,) * nb
    way = list(reversed(routes(nb)[0]))
    links = (len(way), most(way))
    block = min(512, length)
    half = width // 2
    turns = seqs * (HEADS // 2)
    shape = jax.ShapeDtypeStruct
    vm = pl.BlockSpec(memory_space=VMEM)
    hbm = pl.BlockSpec(memory_space=pl.ANY)
    dma = pltpu.SemaphoreType.DMA
    return pl.pallas_call(
        functools.partial(pull_kernel, count, sub, mem_rows, r, fr),
        out_shape=(
            shape((seqs, length, width), bf16),
            shape((3 * r + rows2, width), f32),
            shape((16, 128), f32),
        ),
        in_specs=[pl.BlockSpec(memory_space=pltpu.SMEM), hbm, vm] + [hbm] * 8 + [vm] * 3,
        out_specs=[hbm, vm, vm],
        scratch_shapes=[VMEM(a.shape, a.dtype) for a in (x, q, k, v, qt, att, da, res, g1, x)]
        + [
            VMEM((2, keys, 128), bf16),
            VMEM((2, keys, 128), bf16),
            VMEM((128, keys), bf16),
            VMEM((2, 128, length), bf16),
        ]
        + [VMEM((keys, block), bf16)] * 4
        + [
            VMEM((seqs, length, width), bf16),
            VMEM((seqs, keys, width), bf16),
            VMEM((seqs, keys, width), bf16),
            VMEM((128, length), f32),
        ]
        + [VMEM((keys, 128), f32)] * 4
        + [VMEM(cube + (3 * r, width), bf16), VMEM(cube + (16, 128), f32)]
        + scatter_bufs(nb, way, (rows2, half), bf16) * 2
        + scatter_bufs(nb, way, (3 * r, half), bf16) * 2
        + scatter_bufs(nb, way, (16, 128), f32)
        + [dma((5,) + links)] * 2
        + [dma((turns, 6)), dma((3,)), dma((seqs * (length // 512),))],
        compiler_params=pltpu.CompilerParams(
            collective_id=1, has_side_effects=True, vmem_limit_bytes=62 * 2**20
        ),
        name="pull",
    )(lengths, x, mem, q, k, v, qt, att, da, res, g1, part1, gvec, gub)


def results_kernel(r, fr, mem_rows, dx_ref, sums, small, dx_o, *outs):
    outs, sem = outs[:-1], outs[-1]
    move = pltpu.make_async_copy(dx_ref, dx_o, sem)
    move.start()
    gq, gk, gv, go, gu, gd, gm, gb = outs[:8]
    vecs = outs[8:]
    width = gq.shape[1]
    cols = gu.shape[1] // width
    for n, ref in enumerate((gq, gk, gv, go)):
        ref[...] = sums[n * r : (n + 1) * r, :]
    for c in range(cols):
        gu[:, c * width : (c + 1) * width] = sums[(4 + c) * r : (5 + c) * r, :]
    gd[...] = sums[(4 + cols) * r :, :]
    value = small[...]
    gm[...] = value[0:r, 0:mem_rows]
    turned = jnp.concatenate([value, jnp.zeros((112, 128), f32)], 0).T
    for n, ref in enumerate(vecs):
        ref[...] = turned[VEC + n : VEC + n + 1, 0:r]
    gb[...] = value[0:1, 64 : 64 + fr]
    move.wait()


def results_call(r, fr, mem_rows, ff, dx, sums, small):
    width = sums.shape[1]
    shape = jax.ShapeDtypeStruct
    vm = pl.BlockSpec(memory_space=VMEM)
    hbm = pl.BlockSpec(memory_space=pl.ANY)
    mats = [(r, width)] * 4 + [(r, ff), (fr, width), (r, mem_rows), (1, fr)] + [(1, r)] * 8
    return pl.pallas_call(
        functools.partial(results_kernel, r, fr, mem_rows),
        out_shape=(shape(dx.shape, dx.dtype),) + tuple(shape(m, f32) for m in mats),
        in_specs=[vm, vm, vm],
        out_specs=[hbm] + [vm] * len(mats),
        scratch_shapes=[pltpu.SemaphoreType.DMA],
        name="results",
    )(dx, sums, small)


DIMS = (1, 0, 0, 0, 0, 0, 0, 0, 0, 0, 0, 0, 0, 0, 0, 0)


def on_device(devices, inputs, lengths, *rest):
    params, cotangent = rest[:-1], rest[-1]
    width = inputs.shape[2]
    count = min(devices, width // 16)
    sub = devices // count
    sets = [list(range(g * sub, (g + 1) * sub)) for g in range(count)]
    if sub > 1:
        params = tuple(
            lax.all_gather(a, "dp", axis=d, tiled=True, axis_index_groups=sets)
            for a, d in zip(params, DIMS, strict=True)
        )
    (memory, wq, bq, wk, wv, bv, wo, bo, ga, sa, wu, bu, wd, bd, gb, sb) = params
    r, fr = wq.shape[0], wd.shape[0]
    mem_rows = memory.shape[0]

    vecs = [a.reshape(1, r) for a in (bq, bv, bo, ga, sa, bd, gb, sb)]
    q, k, v, qt, att, g1, g2, vec, ub, mem = attend_call(
        count, sub, lengths, inputs, wq, wk, wv, wo, wu, wd, memory.T, bu.reshape(1, fr), vecs, mem_rows
    )
    seqs, length = inputs.shape[:2]
    layer_out, res, datt, part1, gvec, gub = feed_call(
        inputs,
        att.reshape(seqs, width, length),
        cotangent,
        g2.reshape((count,) + g2.shape[-2:]),
        vec,
        ub,
        r,
        fr,
    )
    dx, sums, tiny = pull_call(
        count, sub, mem_rows, r, fr, lengths, inputs, mem, q, k, v, qt, att, datt, res, g1,
        part1.reshape(g2.shape), gvec, gub,
    )
    dx, gwq, gwk, gwv, gwo, gwu, gwd, gmem, gbu, *vecs = results_call(
        r, fr, mem_rows, wu.shape[1], dx, sums, tiny
    )
    gmem = gmem.T
    gbu = gbu.reshape(fr)
    gbq, gbv, gbo, gga, gsa, gbd, ggb, gsb = [a.reshape(r) for a in vecs]
    grads = (gmem, gwq, gbq, gwk, gwv, gbv, gwo, gbo, gga, gsa, gwu, gbu, gwd, gbd, ggb, gsb)
    if sub > 1:
        grads = tuple(
            lax.psum_scatter(a, "dp", scatter_dimension=d, tiled=True, axis_index_groups=sets)
            for a, d in zip(grads, DIMS, strict=True)
        )
    return (layer_out, dx) + grads


def solution(mesh):
    rows, row, mem = P("dp", None), P("dp"), P(None, "dp")
    full = P("dp", None, None)
    params = (mem, rows, row, rows, rows, row, rows, row, row, row, rows, row, rows, row, row, row)
    return jax.shard_map(
        functools.partial(on_device, mesh.shape["dp"]),
        mesh=mesh,
        in_specs=(full, P("dp")) + params + (full,),
        out_specs=(full, full) + params,
        check_vma=False,
    )
```

time: 239 us -> 199 us (0.83)
  Pallas kernels: 222 us -> 198 us
  local copies, waits for them, and re-layouts: 13.6 us -> 0 us
    pallas_call x1, Pallas kernels: 81.1 us -> 63 us  [attend_call(): pl.pallas_call(functools.partial(attend_kernel, count, sub, mem_rows), ou...]
    pallas_call x1, Pallas kernels: 90.2 us -> 80 us  [pull_call(): pl.pallas_call(functools.partial(pull_kernel, count, sub, mem_rows, r, fr...]
    unnamed x22 -> x0, local copies, waits for them, and re-layouts: 8.42 us -> none
    pallas_call x0 -> x1, Pallas kernels: none -> 3.85 us  [results_call(): pl.pallas_call(functools.partial(results_kernel, r, fr, mem_rows), out_sh...]
    squeeze x2 -> x0, local copies, waits for them, and re-layouts: 2.84 us -> none  [the longest x1 1.58 us: on_device(): tiny[j, 2 * r:3 * r]]
where the time goes in v2:
time: 199 us
  Pallas kernels  198 us (99%)
    pallas_call x1, Pallas kernels, pull_call(): pl.pallas_call(functools.partial(pull_kernel, count, sub, mem_rows, r, fr...  80 us
    pallas_call x1, Pallas kernels, attend_call(): pl.pallas_call(functools.partial(attend_kernel, count, sub, mem_rows), ou...  63 us
    pallas_call x1, Pallas kernels, feed_call(): pl.pallas_call(functools.partial(feed_kernel, r, fr, seqs * tiles), grid=...  51.1 us

profile of v2, /device:TPU:0, one launch (start us, length us, event | category | flops | bytes accessed | tf_op | source)
XLA Modules:
  0.0 198.8 jit_solution(13006097066132151914)
XLA Ops:
  0.7 63.0 %attend.1 = (bf16[2,4,1024,128]{3,2,1,0:T(8,128)(2,1)}, bf16[2,4,1056,128]{3,2,1,0:T(8,128)(2,1)}, bf16[2,4,1056,128]{3,2,1,0:T(8,128)(2,1)}, bf16[2,8,128,1024]...) custom-call(s32[2]{0:T(128)} %len_ref.3, ...), custom_call_target="tpu_custom_call" | custom-call | tf_op jit(solution)/shard_map/attend/pallas_call | solution.py:438
  63.7 51.1 %feed.1 = (bf16[2,1024,512]{2,1,0:T(8,128)(2,1)}, f32[2,1024,512]{2,1,0:T(8,128)}, bf16[2,4,1024,128]{3,2,1,0:T(8,128)(2,1)}, bf16[32,144,512]{2,1,0:T(8,128)(2,...) custom-call(bf16[2,1024,512]{2,1,0:T(8,128)(2,1)} %x_any.3, bf16[2,512,1024]{2,1,0:T(8,128)(2,1)} %bitcast.23, ...), custom_call_target="tpu_custom_call" | custom-call | tf_op jit(solution)/shard_map/feed/pallas_call | solution.py:596
  114.7 80.0 %pull.1 = (bf16[2,1024,512]{2,1,0:T(8,128)(2,1)}, f32[192,512]{1,0:T(8,128)}, f32[16,128]{1,0:T(8,128)}) custom-call(s32[2]{0:T(128)} %len_ref.3, bf16[2,1024,512]{2,1,0:T(8,128)(2,1)} %x_any.3, bf16[32,512]{1,0:T(8,128)(2,1)} %get-tuple-element.59.mem_ref, bf16[2,4,1024,128]{3,2,1,0:T(8,128)(2,1)} %get-tuple-element.60.q_any, ...), custom_call_target="tpu_custom_call" | custom-call | tf_op jit(solution)/shard_map/pull/pallas_call | solution.py:896
  194.8 3.8 %results.1 = (bf16[2,1024,512]{2,1,0:T(8,128)(2,1)}, f32[16,512]{1,0:T(8,128)}, f32[16,512]{1,0:T(8,128)}, f32[16,512]{1,0:T(8,128)}, f32[16,512]{1,0:T(8,128)},...) custom-call(bf16[2,1024,512]{2,1,0:T(8,128)(2,1)} %get-tuple-element, ...), custom_call_target="tpu_custom_call" | custom-call | tf_op jit(solution)/shard_map/results/pallas_call | solution.py:961

commit v3 on v2

--- a/solution.py
+++ b/solution.py
@@ -163,16 +163,16 @@
 ):
     vec_refs, rest = rest[:8], rest[8:]
     (
-    q_any, k_any, v_any, qt_any, att_any, g1_any, g2, vec_o, ub_o, mem_o,
-    x_ref, q_o, k_o, v_o, qt_o, att_o, g1,
-    gs, ksel, vt_s, score_a, score_b, top_a, top_b,
+    q_any, k_any, v_any, att_any, inv_any, g1_any, prob_any, g2, vec_o, ub_o, mem_o,
+    x_ref, q_o, k_o, v_o, att_o, inv_o, g1,
+    qt_o, gs, ksel, vt_s, score_a, score_b, prob_s, top_a, top_b,
     flat_s, wide_s,
-    local, x_sem, out_sem, head_sem, send1, recv1, send2, recv2, send3, recv3,
+    local, x_sem, out_sem, head_sem, prob_sem, send1, recv1, send2, recv2, send3, recv3,
     ) = rest
     cube = Cube(count, sub)
     nb = cube.nb
     seqs, length, width = x_ref.shape
-    keys = k_o.shape[2]
+    keys = v_o.shape[2]
     mem_pad = keys - length
     r = wq_ref.shape[0]
     ff = wu_ref.shape[1]
@@ -271,14 +271,13 @@
     def put_keys(s, rows, kk, vv, bias):
         kb = kk.astype(bf16)
         vb = vv.astype(bf16)
+        kt = kb.T
         for p in range(HEADS // 2):
-            k_o[s, p, rows, :] = kb[:, 128 * p : 128 * p + 128]
+            k_o[s, p, :, rows] = kt[128 * p : 128 * p + 128, :]
             v_o[s, p, rows, :] = vb[:, 128 * p : 128 * p + 128]
         for h in range(HEADS):
             p, o = h // 2, 64 * (1 - h % 2)
-            pattern = jnp.where(
-                lane == o, bias, jnp.where((lane > o) & (lane <= o + 3), 1.0, 0.0)
-            ).astype(bf16)
+            pattern = jnp.where(lane == o, bias, 0.0).astype(bf16)
             mine = (lane < 64) if h % 2 == 0 else (lane >= 64)
             ksel[s, h, rows, :] = jnp.where(mine, kb[:, 128 * p : 128 * p + 128], pattern)
         vt = vb.T
@@ -315,9 +314,9 @@
         rows = pl.ds(start, tile)
         xt = x_ref[s, rows, :]
         qb = ((dg(xt, weight(0), NN) + bq) * (LOG2E * HEAD_DIM**-0.5)).astype(bf16)
+        qt = qb.T
         for p in range(HEADS // 2):
-            q_o[s, p, rows, :] = qb[:, 128 * p : 128 * p + 128]
-        qt = qb.T
+            q_o[s, p, :, rows] = qt[128 * p : 128 * p + 128, :]
         for h in range(HEADS):
             e = h % 2
             qt_o[s, h, 64 * e : 64 * e + 64, rows] = qt[64 * h : 64 * h + 64, :]
@@ -340,31 +339,42 @@
         h = (i // per_head) % HEADS
         return s, h, pl.ds(pl.multiple_of((i % per_head) * block, block), block)
 
-    def scores(i, score, top):
-        s, h, at = place(i)
-        value = dg(ksel[s, h], qt_o[s, h, :, at], NN)
-        score[...] = value
-        top[...] = jnp.max(value, 0, keepdims=True)
-
-    def mix(i, score, top):
-        s, h, at = place(i)
-        peak = top[...]
-        probs = jnp.exp2(score[...] - peak).astype(bf16)
-        mixed = dg(vt_s[s, h], probs, NN)
-        total = mixed[64:65, :]
-        att_o[s, h, :, at] = (mixed[0:64, :] / total).astype(bf16)
-        stat = peak + jnp.log2(total)
-        hi = stat.astype(bf16).astype(f32)
-        mid = (stat - hi).astype(bf16).astype(f32)
-        low = stat - hi - mid
-        row = lax.broadcasted_iota(jnp.int32, (16, block), 0)
-        extra = jnp.where(
-            row == 0,
-            1.0,
-            jnp.where(row == 1, -hi, jnp.where(row == 2, -mid, jnp.where(row == 3, -low, 0.0))),
+    cuts = [slice(c, c + 256) for c in range(0, length - 256, 256)] + [slice(length - 256, keys)]
+
+    def turn(i, now, then):
+        if i is not None:
+            score, top, slot = now
+            s, h, at = place(i)
+            peak = top[...]
+            mixed = 0.0
+        if then is not None:
+            next_i, next_score, next_top = then
+            next_s, next_h, next_at = place(next_i)
+            column = qt_o[next_s, next_h, :, next_at]
+            high = None
+        for cut in cuts:
+            if then is not None:
+                value = dg(ksel[next_s, next_h, cut, :], column, NN)
+                next_score[cut, :] = value
+                part = jnp.max(value.reshape(-1, 8, block), 0)
+                high = part if high is None else jnp.maximum(high, part)
+            if i is not None:
+                weights = jnp.exp2(score[cut, :] - peak).astype(bf16)
+                prob_s[slot + (cut, slice(None))] = weights
+                mixed = mixed + dg(vt_s[s, h, :, cut], weights, NN)
+        if then is not None:
+            next_top[...] = jnp.max(high, 0, keepdims=True)
+        if i is not None:
+            prob_out(i, slot).start()
+            inverse = 1.0 / mixed[64:65, :]
+            att_o[s, h, :, at] = (mixed[0:64, :] * inverse).astype(bf16)
+            inv_o[s, h, :, at] = inverse
+
+    def prob_out(i, slot):
+        s, h, _ = place(i)
+        return pltpu.make_async_copy(
+            prob_s.at[slot], prob_any.at[s, h, i % per_head], prob_sem.at[slot]
         )
-        o = pl.multiple_of(64 * (1 - h % 2), 64)
-        qt_o[s, h, pl.ds(o, 16), at] = extra.astype(bf16)
 
     outs = [
         pltpu.make_async_copy(src, dst, out_sem.at[1 + n])
@@ -372,15 +382,15 @@
     ]
     for out in outs:
         out.start()
-    scores(0, score_a, top_a)
+    turn(None, None, (0, score_a, top_a))
     turns = blocks // 2
     heads_a_turn = max(1, 2 // per_head)
 
     def head_outs(j):
         s, h = j // HEADS, j % HEADS
         return [
-            pltpu.make_async_copy(qt_o.at[s, h], qt_any.at[s, h], head_sem.at[j, 0]),
-            pltpu.make_async_copy(att_o.at[s, h], att_any.at[s, h], head_sem.at[j, 1]),
+            pltpu.make_async_copy(att_o.at[s, h], att_any.at[s, h], head_sem.at[j, 0]),
+            pltpu.make_async_copy(inv_o.at[s, h], inv_any.at[s, h], head_sem.at[j, 1]),
         ]
 
     plan = ((0, 3, 1), (3, 0, 3), (4, 1, 3), (4, 2, 2), (5, 3, 2), (10, 2, 3), (11, 3, 3))
@@ -393,16 +403,25 @@
             def _():
                 advance(c, step)
 
-        scores(2 * j + 1, score_b, top_b)
-        mix(2 * j, score_a, top_a)
-        scores(jnp.minimum(2 * j + 2, blocks - 1), score_a, top_a)
-        mix(2 * j + 1, score_b, top_b)
+        odd = j % 2
+
+        @pl.when(j > 1)
+        def _():
+            for k in range(2):
+                prob_out(2 * j - 4 + k, (odd, k)).wait()
+
+        turn(2 * j, (score_a, top_a, (odd, 0)), (2 * j + 1, score_b, top_b))
+        then = jnp.minimum(2 * j + 2, blocks - 1)
+        turn(2 * j + 1, (score_b, top_b, (odd, 1)), (then, score_a, top_a))
         for k in range(heads_a_turn):
             for out in head_outs(j * heads_a_turn + k):
                 out.start()
 
     for c in range(chunks):
         advance(c, steps)
+    for j in range(max(0, turns - 2), turns):
+        for k in range(2):
+            prob_out(2 * j + k, (j % 2, k)).wait()
     for out in outs + [g1_out]:
         out.wait()
 
@@ -428,32 +447,35 @@
     hbm = pl.BlockSpec(memory_space=pl.ANY)
     dma = pltpu.SemaphoreType.DMA
     kept = (
-        shape((seqs, pairs, length, 128), bf16),
+        shape((seqs, pairs, 128, length), bf16),
+        shape((seqs, pairs, 128, keys), bf16),
         shape((seqs, pairs, keys, 128), bf16),
-        shape((seqs, pairs, keys, 128), bf16),
-        shape((seqs, HEADS, 128, length), bf16),
         shape((seqs, HEADS, HEAD_DIM, length), bf16),
+        shape((seqs, HEADS, 1, length), f32),
         shape(cube + (3 * r, width), bf16),
     )
     return pl.pallas_call(
         functools.partial(attend_kernel, count, sub, mem_rows),
         out_shape=kept
         + (
+            shape((seqs, HEADS, length // block, keys, block), bf16),
             shape(cube + (rows2, width), bf16),
             shape((8, width), f32),
             shape((1, ff), f32),
             shape((KEY_PAD, width), bf16),
         ),
         in_specs=[pl.BlockSpec(memory_space=pltpu.SMEM), hbm] + [vm] * 16,
-        out_specs=[hbm] * 7 + [vm] * 3,
+        out_specs=[hbm] * 8 + [vm] * 3,
         scratch_shapes=[VMEM(x.shape, bf16)]
-        + [VMEM(a.shape, bf16) for a in kept]
+        + [VMEM(a.shape, a.dtype) for a in kept]
         + [
+            VMEM((seqs, HEADS, 128, length), bf16),
             VMEM(cube + (16, 128), bf16),
             VMEM((seqs, HEADS, keys, 128), bf16),
             VMEM((seqs, HEADS, 80, keys), bf16),
             VMEM((keys, block), f32),
             VMEM((keys, block), f32),
+            VMEM((2, 2, keys, block), bf16),
             VMEM((1, block), f32),
             VMEM((1, block), f32),
             VMEM((16, 128), f32),
@@ -462,6 +484,7 @@
             dma,
             dma((4,)),
             dma((seqs * HEADS, 2)),
+            dma((2, 2)),
             dma((2,) + links),
             dma((2,) + links),
             dma((4,) + links),
@@ -496,7 +519,7 @@
     r, fr, steps,
     x_ref, att_ref, dy_ref, g2, vec, ub,
     out_o, res_o, datt_o, part_o, gvec, gub,
-    slope_s, act_s, gwo, gwu, gwd,
+    act_s, slope_s, low_s, outer_s, branch_s, gwo, gwu, gwd,
 ):
     i = pl.program_id(0)
     rows, width = x_ref.shape[1:]
@@ -520,49 +543,85 @@
     def wd(c):
         return g2[c * per : (c + 1) * per, r + cols * r :, :].reshape(width, width)
 
-    att = att_ref[0]
-    hidden, normed1, inverse1 = norm_forward(x_ref[0].astype(f32) + dg(att, wo(), TN) + bo, ga, sa)
-    low = hidden.astype(bf16)
-    outer = hidden + bd
+    class Part:
+        def __init__(self, at):
+            self.at = at
+
+        def enter(self):
+            branch = dg(att_ref[0, :, self.at], wo(), TN)
+            value = x_ref[0, self.at, :].astype(f32) + branch + bo
+            hidden, self.normed, self.inverse = norm_forward(value, ga, sa)
+            self.low = hidden.astype(bf16)
+            low_s[self.at, :] = self.low
+            self.outer = hidden + bd
+
+        def forward(self, c):
+            u = dg(self.low, wu(c), NN) + ub[:, c * width : (c + 1) * width]
+            bend = GELU_A + GELU_B * (u * u)
+            gate = 0.5 + 0.5 * jnp.tanh(u * bend)
+            act = u * gate
+            low = act.astype(bf16)
+            act_s[c][self.at, :] = low
+            slope = gate + act * (1.0 - gate) * (6.0 * bend - 4.0 * GELU_A)
+            slope_s[c][self.at, :] = slope.astype(bf16)
+            self.outer = self.outer + dg(low, wd(c), NN)
+
+        def turn(self):
+            out, normed, inverse = norm_forward(self.outer, gb, sb)
+            out_o[0, self.at, :] = out.astype(bf16)
+            dy = dy_ref[0, self.at, :].astype(f32)
+            gvec[6:7, :] += col_sum(dy * normed)
+            gvec[7:8, :] += col_sum(dy)
+            self.d_hidden = norm_backward(dy, normed, inverse, gb)
+            gvec[5:6, :] += col_sum(self.d_hidden)
+            self.d_outer = self.d_hidden.astype(bf16)
+            outer_s[self.at, :] = self.d_outer
+
+        def backward(self, c):
+            d_act = dg(self.d_outer, wd(c), NT)
+            d_inner = d_act * slope_s[c][self.at, :].astype(f32)
+            gub[:, c * width : (c + 1) * width] += col_sum(d_inner)
+            low = d_inner.astype(bf16)
+            slope_s[c][self.at, :] = low
+            self.d_hidden = self.d_hidden + dg(low, wu(c), NT)
+
+        def leave(self):
+            gvec[3:4, :] += col_sum(self.d_hidden * self.normed)
+            gvec[4:5, :] += col_sum(self.d_hidden)
+            d_res1 = norm_backward(self.d_hidden, self.normed, self.inverse, ga)
+            res_o[0, self.at, :] = d_res1
+            gvec[2:3, :] += col_sum(d_res1)
+            d_branch = d_res1.astype(bf16)
+            branch_s[self.at, :] = d_branch
+            d_att = dg(d_branch, wo(), NT).astype(bf16)
+            for p in range(width // 128):
+                datt_o[0, p, self.at, :] = d_att[:, 128 * p : 128 * p + 128]
+
+    half = rows // 2
+    a, b = Part(slice(0, half)), Part(slice(half, rows))
+    a.enter()
+    b.enter()
+    for c in range(cols):
+        a.forward(c)
+    b.forward(0)
+    a.turn()
+    for c in range(1, cols):
+        b.forward(c)
+    a.backward(0)
+    b.turn()
+    for c in range(1, cols):
+        a.backward(c)
+    b.backward(0)
+    a.leave()
+    for c in range(1, cols):
+        b.backward(c)
     for c in range(cols):
         at = slice(c * width, (c + 1) * width)
-        u = dg(low, wu(c), NN) + ub[:, at]
-        u2 = u * u
-        t = jnp.tanh(u * (GELU_A + GELU_B * u2))
-        hu = 0.5 * u
-        act = (hu + hu * t).astype(bf16)
-        act_s[c] = act
-        slope_s[c] = (
-            (0.5 + 0.5 * t) + (hu * (1.0 - t * t)) * (GELU_A + 3.0 * GELU_B * u2)
-        ).astype(bf16)
-        outer = outer + dg(act, wd(c), NN)
-    out, normed2, inverse2 = norm_forward(outer, gb, sb)
-    out_o[0] = out.astype(bf16)
-    dy = dy_ref[0].astype(f32)
-    gvec[6:7, :] += col_sum(dy * normed2)
-    gvec[7:8, :] += col_sum(dy)
-    d_res2 = norm_backward(dy, normed2, inverse2, gb)
-    d_outer = d_res2.astype(bf16)
-    gvec[5:6, :] += col_sum(d_outer.astype(f32))
-    d_hidden = d_res2
-    for c in range(cols):
-        at = slice(c * width, (c + 1) * width)
-        d_act = dg(d_outer, wd(c), NT)
-        d_inner = (d_act * slope_s[c].astype(f32)).astype(bf16)
-        gwd[at, :] += dg(act_s[c], d_outer, TN)
-        gwu[:, at] += dg(low, d_inner, TN)
-        gub[:, at] += col_sum(d_inner.astype(f32))
-        d_hidden = d_hidden + dg(d_inner, wu(c), NT)
-    gvec[3:4, :] += col_sum(d_hidden * normed1)
-    gvec[4:5, :] += col_sum(d_hidden)
-    d_res1 = norm_backward(d_hidden, normed1, inverse1, ga)
-    res_o[0] = d_res1
-    d_branch = d_res1.astype(bf16)
-    gvec[2:3, :] += col_sum(d_branch.astype(f32))
-    gwo[...] += dg(att, d_branch, NN)
-    d_att = dg(d_branch, wo(), NT).astype(bf16)
-    for p in range(width // 128):
-        datt_o[0, p] = d_att[:, 128 * p : 128 * p + 128]
+        gwd[at, :] += dg(act_s[c][...], outer_s[...], TN)
+        gwu[:, at] += dg(low_s[...], slope_s[c][...], TN)
+        if c == 0:
+            b.leave()
+    gwo[...] += dg(att_ref[0], branch_s[...], NN)
 
     @pl.when(i == steps - 1)
     def _():
@@ -612,8 +671,11 @@
         ]
         + [full(a) for a in outs[3:]],
         scratch_shapes=[
-            VMEM((ff // width, tile, width), bf16),
-            VMEM((ff // width, tile, width), bf16),
+            [VMEM((tile, width), bf16)] * (ff // width),
+            [VMEM((tile, width), bf16)] * (ff // width),
+            VMEM((tile, width), bf16),
+            VMEM((tile, width), bf16),
+            VMEM((tile, width), bf16),
             VMEM((width, width), f32),
             VMEM((width, ff), f32),
             VMEM((ff, width), f32),
@@ -625,34 +687,34 @@
 
 def pull_kernel(
     count, sub, mem_rows, r, fr,
-    len_ref, x_any, mem_ref, q_any, k_any, v_any, qt_any, att_any, da_any, res_any, g1_any, part1,
+    x_any, mem_ref, q_any, k_any, v_any, att_any, inv_any, prob_any, da_any, res_any, g1_any, part1,
     gvec_ref, gub_ref,
     dx_any, sums_o, small_o,
-    x_ref, q_ref, k_ref, v_ref, qt_ref, att_ref, da_ref, res_ref, g1, dx_o,
-    ksel, vsel, kt, dot_s, p_a, d_a, p_b, d_b, dq_s, dk_s, dv_s, dqt,
-    dv_0, dv_1, dk_0, dk_1, part2, small_s, *rest,
+    x_ref, q_ref, k_ref, v_ref, att_ref, inv_ref, da_ref, res_ref, g1, dx_o,
+    prob_s, vsel, dot_s, d_a, d_b, pt_s, dt_s, dq_s, dk_s, dv_s, dqt, dkt, dvt, dkm, dvm, part2, small_s, *rest,
 ):
     cube = Cube(count, sub)
     nb = cube.nb
     ways = [list(reversed(route)) for route in routes(nb)]
     steps = len(ways[0])
-    bufs = [rest[k * steps : (k + 1) * steps] for k in range(5)]
-    send, recv, load_sem, late_sem, out_sem = rest[5 * steps :]
+    bufs = [rest[k * steps : (k + 1) * steps] for k in range(8)]
+    send, recv, load_sem, late_sem, out_sem, prob_sem = rest[8 * steps :]
     seqs, length, width = x_ref.shape
-    keys = k_ref.shape[2]
+    keys = v_ref.shape[2]
     ff = gub_ref.shape[1]
     cols = ff // width
     half = width // 2
     halves = (slice(0, half), slice(half, width))
     pairs = HEADS // 2
-    feeds = [
-        Scatter(cube, part1, halves[k], ways[k], bufs[k], send.at[k], recv.at[k]) for k in range(2)
-    ]
-    heads = [
-        Scatter(cube, part2, halves[k], ways[k], bufs[2 + k], send.at[2 + k], recv.at[2 + k])
-        for k in range(2)
-    ]
-    smalls = Scatter(cube, small_s, slice(None), ways[0], bufs[4], send.at[4], recv.at[4])
+    quarter = width // 4
+
+    def scatter(n, source, lo, hi, way):
+        return Scatter(cube, source, slice(lo, hi), ways[way], bufs[n], send.at[n], recv.at[n])
+
+    feeds = [scatter(k, part1, k * quarter, (k + 1) * quarter, k % 2) for k in range(4)]
+    first = [scatter(4, part2, 0, half, 0)]
+    last = [scatter(5 + k, part2, half + k * quarter, half + (k + 1) * quarter, k) for k in range(2)]
+    smalls = scatter(7, small_s, 0, 128, 0)
 
     def start(group, step):
         for part in group:
@@ -677,14 +739,22 @@
         both = pl.ds(2 * p, 2)
         return out + [
             pltpu.make_async_copy(a.at[s, both], b.at[s, both], load_sem.at[j, 4 + n])
-            for n, (a, b) in enumerate(((qt_any, qt_ref), (att_any, att_ref)))
+            for n, (a, b) in enumerate(((att_any, att_ref), (inv_any, inv_ref)))
         ]
+
+    def prob_load(j):
+        p, s = j // seqs, j % seqs
+        return pltpu.make_async_copy(
+            prob_any.at[s, pl.ds(2 * p, 2)], prob_s.at[j % 2], prob_sem.at[j % 2]
+        )
 
     late = [
         pltpu.make_async_copy(a, b, late_sem.at[n])
         for n, (a, b) in enumerate(((x_any, x_ref), (g1_any, g1), (res_any, res_ref)))
     ]
 
+    prob_load(0).start()
+
     @pl.loop(0, seqs * pairs)
     def _(j):
         for load in loads(j):
@@ -696,72 +766,69 @@
     start(feeds, 0)
 
     lane = lax.broadcasted_iota(jnp.int32, (1, 128), 1)
-    key_row = lax.broadcasted_iota(jnp.int32, (keys, 1), 0)
-    block = p_a.shape[1]
+    block = d_a.shape[1]
     per_head = length // block
-    dv_t, dk_t = (dv_0, dv_1), (dk_0, dk_1)
-    temp = ((p_a, d_a), (p_b, d_b))
+    temp = (d_a, d_b)
 
     def pair(j):
         p, s = j // seqs, j % seqs
         at = pl.ds(pl.multiple_of(128 * p, 128), 128)
-        kp = k_ref[s, p]
+        slot = j % 2
         vp = v_ref[s, p]
-        kt[...] = kp.T
-        da = da_ref[s, p]
-        dat = da.T
-        seen = (key_row < len_ref[s]) | ((key_row >= length) & (key_row < length + mem_rows))
-        bias = jnp.where(seen, 0.0, HIDE)
+        dat = da_ref[s, p].T
         for e in range(2):
             o = 64 * (1 - e)
             mine = (lane < 64) if e == 0 else (lane >= 64)
-            pattern = jnp.where(
-                lane == o, bias, jnp.where((lane > o) & (lane <= o + 3), 1.0, 0.0)
-            ).astype(bf16)
-            ksel[e] = jnp.where(mine, kp, pattern)
             vsel[e] = jnp.where(
                 mine, vp, jnp.where((lane >= o) & (lane < o + 2), 1.0, 0.0).astype(bf16)
             )
-            dt = dat[64 * e : 64 * e + 64, :]
-            delta = col_sum(dt.astype(f32) * att_ref[s, 2 * p + e].astype(f32))
+            dt = dat[64 * e : 64 * e + 64, :].astype(f32) * inv_ref[s, 2 * p + e]
+            dot_s[e, 64 * e : 64 * e + 64, :] = dt.astype(bf16)
+            delta = col_sum(dt * att_ref[s, 2 * p + e].astype(f32))
             hi = delta.astype(bf16).astype(f32)
             row = lax.broadcasted_iota(jnp.int32, (64, length), 0)
-            dot_s[e, 64 * e : 64 * e + 64, :] = dt
             dot_s[e, o : o + 64, :] = jnp.where(
                 row == 0, -hi, jnp.where(row == 1, hi - delta, 0.0)
             ).astype(bf16)
 
-        def probs(b):
+        def grads(b):
             e, c = b // per_head, b % per_head
             cut = slice(c * block, (c + 1) * block)
-            prob = jnp.exp2(dg(ksel[e], qt_ref[s, 2 * p + e, :, cut], NN))
             grad = dg(vsel[e], dot_s[e, :, cut], NN)
-            temp[b % 2][0][...] = prob.astype(bf16)
-            temp[b % 2][1][...] = (prob * grad).astype(bf16)
+            temp[b % 2][...] = (prob_s[slot, e, c].astype(f32) * grad).astype(bf16)
+            pt_s[b % 2] = prob_s[slot, e, c, 0:length, :].T
+            dt_s[b % 2] = temp[b % 2][0:length, :].T
 
         def pulls(b):
             e, c = b // per_head, b % per_head
             cut = slice(c * block, (c + 1) * block)
-            prob, grad = temp[b % 2]
-            dv = dg(prob[...], da[cut, :], NN)
-            dk = dg(grad[...], q_ref[s, p, cut, :], NN)
-            dqt[64 * e : 64 * e + 64, cut] = dg(kt[64 * e : 64 * e + 64, :], grad[...], NN)
-            if c == 0:
-                dv_t[e][...] = dv
-                dk_t[e][...] = dk
-            else:
-                dv_t[e][...] += dv
-                dk_t[e][...] += dk
-
-        probs(0)
+            own = slice(64 * e, 64 * e + 64)
+            grad = temp[b % 2]
+            dqt[own, cut] = dg(k_ref[s, p, own, :], grad[...], NN)
+            dots, queries = dot_s[e, own, cut], q_ref[s, p, own, cut]
+            prob = prob_s.at[slot, e, c]
+            news = (
+                (dvt, dg(dots, pt_s[b % 2], NN)),
+                (dkt, dg(queries, dt_s[b % 2], NN)),
+                (dvm, dg(dots, prob[length:keys, :], NT)),
+                (dkm, dg(queries, grad[length:keys, :], NT)),
+            )
+            for ref, new in news:
+                to = slice(0, new.shape[1])
+                if c == 0:
+                    ref[own, to] = new
+                else:
+                    ref[own, to] += new
+
+        grads(0)
         for b in range(2 * per_head):
             if b + 1 < 2 * per_head:
-                probs(b + 1)
+                grads(b + 1)
             pulls(b)
-        even = lane < 64
-        dv_s[s, :, at] = jnp.where(even, dv_0[...], dv_1[...]).astype(bf16)
-        dk_s[s, :, at] = (jnp.where(even, dk_0[...], dk_1[...]) * LN2).astype(bf16)
-        dq_s[s, :, at] = dqt[...].T.astype(bf16)
+        dq_s[s, :, at] = dqt[...].astype(bf16).T
+        for ref, tops, mems, unit in ((dk_s, dkt, dkm, LN2), (dv_s, dvt, dvm, 1.0)):
+            ref[s, 0:length, at] = (tops[...] * unit).astype(bf16).T
+            ref[s, length:keys, at] = ((mems[...] * unit).T)[0 : keys - length, :].astype(bf16)
 
     def weight(j):
         return g1[(slice(None),) * nb + (slice(j * r, j * r + r), slice(None))].reshape(width, width)
@@ -786,34 +853,33 @@
 
     @pl.loop(0, turns)
     def _(j):
-        for load in loads(j):
+        @pl.when(j + 1 < turns)
+        def _():
+            prob_load(j + 1).start()
+
+        for load in loads(j) + [prob_load(j)]:
             load.wait()
 
-        for slot, step in ((1, 0), (3, 1), (4, 2)):
+        plan = ((1, feeds, 0), (3, feeds[:2], 1), (4, feeds[2:], 1), (5, feeds[:2], 2))
+        plan += ((6, feeds[2:], 2), (5, first, 0), (6, first, 1), (7, first, 2))
+        for slot, group, step in plan:
 
             @pl.when(j == (slot * turns) // 8)
             def _():
-                finish(feeds, step)
-                start(feeds, step + 1)
+                finish(group, step)
+                start(group, step + 1)
 
         @pl.when(j == turns // 2)
         def _():
             for load in late:
                 load.wait()
             terms(0)
-            start(heads[:1], 0)
-
-        for slot, step in ((5, 0), (6, 1), (7, 2)):
-
-            @pl.when(j == (slot * turns) // 8)
-            def _():
-                finish(heads[:1], step)
-                start(heads[:1], step + 1)
+            start(first, 0)
 
         pair(j)
 
     terms(1)
-    start(heads[1:], 0)
+    start(last, 0)
     bq = sum(col_sum(dq_s[s].astype(f32)) for s in range(seqs)) * scale
     bv = sum(col_sum(dv_s[s].astype(f32)) for s in range(seqs))
     gmem = sum(
@@ -851,43 +917,42 @@
         out.start()
         return out
 
-    def total(part, lo, hi, k):
-        value = part.total(steps - 1)
-        sums_o[lo:hi, halves[k]] = value
+    def total(part, lo, hi):
+        sums_o[lo:hi, part.lanes] = part.total(steps - 1)
 
     todo = list(range(seqs * tiles))
     outs = []
-    group = heads[1:] + [smalls]
+    group = last + [smalls]
     for step in range(steps):
         if todo:
             outs.append(inputs(todo.pop(0)))
         if step == steps - 2:
-            finish(feeds, steps - 1)
-            for k in range(2):
-                total(feeds[k], 3 * r, sums_o.shape[0], k)
-            finish(heads[:1], steps - 1)
-            total(heads[0], 0, 3 * r, 0)
+            finish(feeds + first, steps - 1)
+            for part in feeds:
+                total(part, 3 * r, sums_o.shape[0])
+            total(first[0], 0, 3 * r)
         finish(group, step)
         if step + 1 < steps:
             start(group, step + 1)
     for i in todo:
         outs.append(inputs(i))
-    total(heads[1], 0, 3 * r, 1)
+    for part in last:
+        total(part, 0, 3 * r)
     small_o[...] = smalls.total(steps - 1)
     for out in outs:
         out.wait()
 
 
-def pull_call(count, sub, mem_rows, r, fr, lengths, x, mem, q, k, v, qt, att, da, res, g1, part1, gvec, gub):
+def pull_call(count, sub, mem_rows, r, fr, x, mem, q, k, v, att, inv, prob, da, res, g1, part1, gvec, gub):
     seqs, length, width = x.shape
-    keys = k.shape[2]
+    keys = v.shape[2]
     rows2 = part1.shape[-2]
     nb = count.bit_length() - 1
     cube = (2,) * nb
     way = list(reversed(routes(nb)[0]))
     links = (len(way), most(way))
-    block = min(512, length)
-    half = width // 2
+    block = prob.shape[4]
+    half, quarter = width // 2, width // 4
     turns = seqs * (HEADS // 2)
     shape = jax.ShapeDtypeStruct
     vm = pl.BlockSpec(memory_space=VMEM)
@@ -900,34 +965,39 @@
             shape((3 * r + rows2, width), f32),
             shape((16, 128), f32),
         ),
-        in_specs=[pl.BlockSpec(memory_space=pltpu.SMEM), hbm, vm] + [hbm] * 8 + [vm] * 3,
+        in_specs=[hbm, vm] + [hbm] * 9 + [vm] * 3,
         out_specs=[hbm, vm, vm],
-        scratch_shapes=[VMEM(a.shape, a.dtype) for a in (x, q, k, v, qt, att, da, res, g1, x)]
+        scratch_shapes=[VMEM(a.shape, a.dtype) for a in (x, q, k, v, att, inv, da, res, g1, x)]
         + [
+            VMEM((2, 2) + prob.shape[2:], bf16),
             VMEM((2, keys, 128), bf16),
-            VMEM((2, keys, 128), bf16),
-            VMEM((128, keys), bf16),
             VMEM((2, 128, length), bf16),
-        ]
-        + [VMEM((keys, block), bf16)] * 4
-        + [
+            VMEM((keys, block), bf16),
+            VMEM((keys, block), bf16),
+            VMEM((2, block, length), bf16),
+            VMEM((2, block, length), bf16),
             VMEM((seqs, length, width), bf16),
             VMEM((seqs, keys, width), bf16),
             VMEM((seqs, keys, width), bf16),
             VMEM((128, length), f32),
+            VMEM((128, length), f32),
+            VMEM((128, length), f32),
+            VMEM((128, KEY_PAD), f32),
+            VMEM((128, KEY_PAD), f32),
+            VMEM(cube + (3 * r, width), bf16),
+            VMEM(cube + (16, 128), f32),
         ]
-        + [VMEM((keys, 128), f32)] * 4
-        + [VMEM(cube + (3 * r, width), bf16), VMEM(cube + (16, 128), f32)]
-        + scatter_bufs(nb, way, (rows2, half), bf16) * 2
-        + scatter_bufs(nb, way, (3 * r, half), bf16) * 2
+        + scatter_bufs(nb, way, (rows2, quarter), bf16) * 4
+        + scatter_bufs(nb, way, (3 * r, half), bf16)
+        + scatter_bufs(nb, way, (3 * r, quarter), bf16) * 2
         + scatter_bufs(nb, way, (16, 128), f32)
-        + [dma((5,) + links)] * 2
-        + [dma((turns, 6)), dma((3,)), dma((seqs * (length // 512),))],
+        + [dma((8,) + links)] * 2
+        + [dma((turns, 6)), dma((3,)), dma((seqs * (length // 512),)), dma((2,))],
         compiler_params=pltpu.CompilerParams(
             collective_id=1, has_side_effects=True, vmem_limit_bytes=62 * 2**20
         ),
         name="pull",
-    )(lengths, x, mem, q, k, v, qt, att, da, res, g1, part1, gvec, gub)
+    )(x, mem, q, k, v, att, inv, prob, da, res, g1, part1, gvec, gub)
 
 
 def results_kernel(r, fr, mem_rows, dx_ref, sums, small, dx_o, *outs):
@@ -987,7 +1057,7 @@
     mem_rows = memory.shape[0]
 
     vecs = [a.reshape(1, r) for a in (bq, bv, bo, ga, sa, bd, gb, sb)]
-    q, k, v, qt, att, g1, g2, vec, ub, mem = attend_call(
+    q, k, v, att, inv, g1, prob, g2, vec, ub, mem = attend_call(
         count, sub, lengths, inputs, wq, wk, wv, wo, wu, wd, memory.T, bu.reshape(1, fr), vecs, mem_rows
     )
     seqs, length = inputs.shape[:2]
@@ -1002,7 +1072,7 @@
         fr,
     )
     dx, sums, tiny = pull_call(
-        count, sub, mem_rows, r, fr, lengths, inputs, mem, q, k, v, qt, att, datt, res, g1,
+        count, sub, mem_rows, r, fr, inputs, mem, q, k, v, att, inv, prob, datt, res, g1,
         part1.reshape(g2.shape), gvec, gub,
     )
     dx, gwq, gwk, gwv, gwo, gwu, gwd, gmem, gbu, *vecs = results_call(

time: 199 us -> 185 us (0.930)
  Pallas kernels: 198 us -> 184 us
    pallas_call x1, Pallas kernels: 80 us -> 68.8 us  [pull_call(): pl.pallas_call(functools.partial(pull_kernel, count, sub, mem_rows, r, fr...]
where the time goes in v3:
time: 185 us
  Pallas kernels  184 us (99%)
    pallas_call x1, Pallas kernels, pull_call(): pl.pallas_call(functools.partial(pull_kernel, count, sub, mem_rows, r, fr...  68.8 us
    pallas_call x1, Pallas kernels, attend_call(): pl.pallas_call(functools.partial(attend_kernel, count, sub, mem_rows), ou...  61.3 us
    pallas_call x1, Pallas kernels, feed_call(): pl.pallas_call(functools.partial(feed_kernel, r, fr, seqs * tiles), grid=...  50.2 us
    pallas_call x1, Pallas kernels, results_call(): pl.pallas_call(functools.partial(results_kernel, r, fr, mem_rows), out_sh...  3.85 us

profile of v3, /device:TPU:0, one launch (start us, length us, event | category | flops | bytes accessed | tf_op | source)
XLA Modules:
  0.0 185.1 jit_solution(8584074562705775978)
XLA Ops:
  0.7 61.3 %attend.1 = (bf16[2,4,128,1024]{3,2,1,0:T(8,128)(2,1)}, bf16[2,4,128,1056]{3,2,1,0:T(8,128)(2,1)}, bf16[2,4,1056,128]{3,2,1,0:T(8,128)(2,1)}, bf16[2,8,64,1024]{...) custom-call(s32[2]{0:T(128)} %len_ref.1, ...), custom_call_target="tpu_custom_call" | custom-call | tf_op jit(solution)/shard_map/attend/pallas_call | solution.py:457
  62.0 50.2 %feed.1 = (bf16[2,1024,512]{2,1,0:T(8,128)(2,1)}, f32[2,1024,512]{2,1,0:T(8,128)}, bf16[2,4,1024,128]{3,2,1,0:T(8,128)(2,1)}, bf16[32,144,512]{2,1,0:T(8,128)(2,...) custom-call(bf16[2,1024,512]{2,1,0:T(8,128)(2,1)} %x_any.3, bf16[2,512,1024]{2,1,0:T(8,128)(2,1)} %bitcast.23, ...), custom_call_target="tpu_custom_call" | custom-call | tf_op jit(solution)/shard_map/feed/pallas_call | solution.py:655
  112.2 68.8 %pull.1 = (bf16[2,1024,512]{2,1,0:T(8,128)(2,1)}, f32[192,512]{1,0:T(8,128)}, f32[16,128]{1,0:T(8,128)}) custom-call(bf16[2,1024,512]{2,1,0:T(8,128)(2,1)} %x_any.3, bf16[32,512]{1,0:T(8,128)(2,1)} %get-tuple-element.60.mem_ref, bf16[2,4,128,1024]{3,2,1,0:T(8,128)(2,1)} %get-tuple-element.61.q_any, bf16[2,4,128,1056]{3,2,1,0:T(8,128)(2,1)} %get-tuple-element.62.k_any, ...), custom_call_target="tpu_custom_call" | custom-call | tf_op jit(solution)/shard_map/pull/pallas_call | solution.py:961
  181.1 3.8 %results.1 = (bf16[2,1024,512]{2,1,0:T(8,128)(2,1)}, f32[16,512]{1,0:T(8,128)}, f32[16,512]{1,0:T(8,128)}, f32[16,512]{1,0:T(8,128)}, f32[16,512]{1,0:T(8,128)},...) custom-call(bf16[2,1024,512]{2,1,0:T(8,128)(2,1)} %get-tuple-element, ...), custom_call_target="tpu_custom_call" | custom-call | tf_op jit(solution)/shard_map/results/pallas_call | solution.py:1031

commit v4 on v3

--- a/solution.py
+++ b/solution.py
@@ -76,14 +76,20 @@
     return ([(b,) for b in range(nb - 1, -1, -1)],) * 2
 
 
+def short(route):
+    if len(route) != 4:
+        return route
+    return [route[0], route[1] + route[2], route[3]]
+
+
 def most(route):
     return max(2 ** len(group) - 1 for group in route)
 
 
-def gather_copies(cube, ref, route, step, lanes, send, recv):
+def gather_copies(cube, ref, route, step, rows, lanes, send, recv):
     done = {b for group in route[:step] for b in group}
     idx = tuple(slice(None) if c in done else cube.bits[c] for c in cube.msb_first)
-    view = ref.at[idx + (slice(None), lanes)]
+    view = ref.at[idx + (rows, lanes)]
     return [
         pltpu.make_async_remote_copy(
             src_ref=view,
@@ -209,18 +215,27 @@
         move.start()
     cube.barrier(ways)
 
-    def first(step):
+    every_row = slice(None)
+
+    def first(j, step):
+        rows = slice(j * r, j * r + r)
         copies = []
         for k in range(2):
-            copies += gather_copies(cube, g1, ways[k], step, halves[k], send1.at[k], recv1.at[k])
-        return copies + gather_copies(cube, gs, ways[0], step, slice(None), send3, recv3)
+            links = (send1.at[2 * j + k], recv1.at[2 * j + k])
+            copies += gather_copies(cube, g1, ways[k], step, rows, halves[k], *links)
+        return copies
+
+    def tiny(step):
+        return gather_copies(cube, gs, ways[0], step, every_row, slice(None), send3, recv3)
 
     chunks = 4
     chunk = width // chunks
 
     def second(c, step):
         lanes = slice(c * chunk, (c + 1) * chunk)
-        return gather_copies(cube, g2, ways[c % 2], step, lanes, send2.at[c], recv2.at[c])
+        return gather_copies(
+            cube, g2, ways[c % 2], step, every_row, lanes, send2.at[c], recv2.at[c]
+        )
 
     def advance(c, step):
         if step > 0:
@@ -230,20 +245,28 @@
             for copy in second(c, step):
                 copy.start()
 
-    for step in range(steps):
-        copies = first(step)
-        for copy in copies:
+    sets = [functools.partial(first, 1), tiny, functools.partial(first, 2), functools.partial(first, 0)]
+    for copies in sets:
+        for copy in copies(0):
             copy.start()
-        if step == 0:
-            for move in moves:
-                move.wait()
-        for copy in copies:
+    for move in moves:
+        move.wait()
+    for step in range(1, steps):
+        for copies in sets:
+            for copy in copies(step - 1):
+                copy.wait()
+            for copy in copies(step):
+                copy.start()
+        if step == 1:
+            for c in range(chunks):
+                advance(c, 0)
+
+    def arrived(n):
+        for copy in sets[n](steps - 1):
             copy.wait()
-        for slot, c, part in ((0, 0, 0), (1, 1, 0), (2, 0, 1), (2, 1, 1), (2, 2, 0)):
-            if step == slot:
-                advance(c, part)
-    g1_out = pltpu.make_async_copy(g1, g1_any, out_sem.at[0])
-    g1_out.start()
+
+    arrived(0)
+    arrived(1)
     x_load.wait()
 
     lane = lax.broadcasted_iota(jnp.int32, (1, 128), 1)
@@ -268,19 +291,22 @@
     bq = vec_o[0:1, :]
     bv = vec_o[1:2, :]
 
-    def put_keys(s, rows, kk, vv, bias):
+    def put_keys(s, rows, kk, bias):
         kb = kk.astype(bf16)
-        vb = vv.astype(bf16)
         kt = kb.T
         for p in range(HEADS // 2):
             k_o[s, p, :, rows] = kt[128 * p : 128 * p + 128, :]
-            v_o[s, p, rows, :] = vb[:, 128 * p : 128 * p + 128]
         for h in range(HEADS):
             p, o = h // 2, 64 * (1 - h % 2)
             pattern = jnp.where(lane == o, bias, 0.0).astype(bf16)
             mine = (lane < 64) if h % 2 == 0 else (lane >= 64)
             ksel[s, h, rows, :] = jnp.where(mine, kb[:, 128 * p : 128 * p + 128], pattern)
+
+    def put_values(s, rows, vv):
+        vb = vv.astype(bf16)
         vt = vb.T
+        for p in range(HEADS // 2):
+            v_o[s, p, rows, :] = vb[:, 128 * p : 128 * p + 128]
         for h in range(HEADS):
             vt_s[s, h, 0:64, rows] = vt[64 * h : 64 * h + 64, :]
 
@@ -291,29 +317,45 @@
             vt_s[s, h, 64:80, :] = ones
     mem = mem_o[...]
     mem_keys = dg(mem, weight(1), NN)
-    mem_values = dg(mem, weight(2), NN) + bv
     mem_row = lax.broadcasted_iota(jnp.int32, (mem_pad, 1), 0)
+    mem_bias = jnp.where(mem_row < mem_rows, 0.0, HIDE)
     for s in range(seqs):
-        put_keys(
-            s, slice(length, keys), mem_keys, mem_values, jnp.where(mem_row < mem_rows, 0.0, HIDE)
-        )
+        put_keys(s, slice(length, keys), mem_keys, mem_bias)
     tile = 512
     tiles = length // tile
     aux = jnp.where(lax.broadcasted_iota(jnp.int32, (64, tile), 0) == 0, 1.0, 0.0).astype(bf16)
 
+    def place_rows(i):
+        start = pl.multiple_of((i % tiles) * tile, tile)
+        return i // tiles, start, pl.ds(start, tile)
+
     @pl.loop(0, seqs * tiles)
     def _(i):
-        for slot, c, step in ((0, 3, 0), (2, 0, 2), (2, 1, 2), (3, 2, 1)):
-
-            @pl.when(i == slot)
-            def _():
-                advance(c, step)
-
-        s = i // tiles
-        start = pl.multiple_of((i % tiles) * tile, tile)
-        rows = pl.ds(start, tile)
-        xt = x_ref[s, rows, :]
-        qb = ((dg(xt, weight(0), NN) + bq) * (LOG2E * HEAD_DIM**-0.5)).astype(bf16)
+        s, start, rows = place_rows(i)
+        row = lax.broadcasted_iota(jnp.int32, (tile, 1), 0) + start
+        bias = jnp.where(row < len_ref[s], 0.0, HIDE)
+        put_keys(s, rows, dg(x_ref[s, rows, :], weight(1), NN), bias)
+
+    arrived(2)
+    mem_values = dg(mem, weight(2), NN) + bv
+    for s in range(seqs):
+        put_values(s, slice(length, keys), mem_values)
+
+    @pl.loop(0, seqs * tiles)
+    def _(i):
+        s, start, rows = place_rows(i)
+        put_values(s, rows, dg(x_ref[s, rows, :], weight(2), NN) + bv)
+
+    arrived(3)
+    advance(0, 1)
+    advance(1, 1)
+    g1_out = pltpu.make_async_copy(g1, g1_any, out_sem.at[0])
+    g1_out.start()
+
+    @pl.loop(0, seqs * tiles)
+    def _(i):
+        s, start, rows = place_rows(i)
+        qb = ((dg(x_ref[s, rows, :], weight(0), NN) + bq) * (LOG2E * HEAD_DIM**-0.5)).astype(bf16)
         qt = qb.T
         for p in range(HEADS // 2):
             q_o[s, p, :, rows] = qt[128 * p : 128 * p + 128, :]
@@ -321,14 +363,6 @@
             e = h % 2
             qt_o[s, h, 64 * e : 64 * e + 64, rows] = qt[64 * h : 64 * h + 64, :]
             qt_o[s, h, 64 * (1 - e) : 64 * (1 - e) + 64, rows] = aux
-        row = lax.broadcasted_iota(jnp.int32, (tile, 1), 0) + start
-        put_keys(
-            s,
-            rows,
-            dg(xt, weight(1), NN),
-            dg(xt, weight(2), NN) + bv,
-            jnp.where(row < len_ref[s], 0.0, HIDE),
-        )
 
     block = score_a.shape[1]
     per_head = length // block
@@ -393,7 +427,8 @@
             pltpu.make_async_copy(inv_o.at[s, h], inv_any.at[s, h], head_sem.at[j, 1]),
         ]
 
-    plan = ((0, 3, 1), (3, 0, 3), (4, 1, 3), (4, 2, 2), (5, 3, 2), (10, 2, 3), (11, 3, 3))
+    plan = ((2, 0, 2), (2, 1, 2), (3, 2, 1), (3, 3, 1), (9, 0, 3), (9, 1, 3), (9, 2, 2), (9, 3, 2))
+    plan += ((15, 2, 3), (15, 3, 3))
 
     @pl.loop(0, turns)
     def _(j):
@@ -485,8 +520,8 @@
             dma((4,)),
             dma((seqs * HEADS, 2)),
             dma((2, 2)),
-            dma((2,) + links),
-            dma((2,) + links),
+            dma((6,) + links),
+            dma((6,) + links),
             dma((4,) + links),
             dma((4,) + links),
             dma(links),
@@ -691,14 +726,18 @@
     gvec_ref, gub_ref,
     dx_any, sums_o, small_o,
     x_ref, q_ref, k_ref, v_ref, att_ref, inv_ref, da_ref, res_ref, g1, dx_o,
-    prob_s, vsel, dot_s, d_a, d_b, pt_s, dt_s, dq_s, dk_s, dv_s, dqt, dkt, dvt, dkm, dvm, part2, small_s, *rest,
+    prob_s, vsel, dot_s, d_a, d_b, pt_s, dt_s, dq_s, dk_s, dv_s, dqt, dkt, dvt, dkm, dvm, turned, terms,
+    vec_s, part2, small_s, *rest,
 ):
     cube = Cube(count, sub)
     nb = cube.nb
     ways = [list(reversed(route)) for route in routes(nb)]
     steps = len(ways[0])
-    bufs = [rest[k * steps : (k + 1) * steps] for k in range(8)]
-    send, recv, load_sem, late_sem, out_sem, prob_sem = rest[8 * steps :]
+    brief = short(ways[0])
+    sizes = [steps] * 7 + [len(brief)] * 2
+    ends = [sum(sizes[: k + 1]) for k in range(len(sizes))]
+    bufs = [rest[end - size : end] for size, end in zip(sizes, ends, strict=True)]
+    send, recv, load_sem, late_sem, out_sem, prob_sem = rest[ends[-1] :]
     seqs, length, width = x_ref.shape
     keys = v_ref.shape[2]
     ff = gub_ref.shape[1]
@@ -709,12 +748,14 @@
     quarter = width // 4
 
     def scatter(n, source, lo, hi, way):
-        return Scatter(cube, source, slice(lo, hi), ways[way], bufs[n], send.at[n], recv.at[n])
-
-    feeds = [scatter(k, part1, k * quarter, (k + 1) * quarter, k % 2) for k in range(4)]
-    first = [scatter(4, part2, 0, half, 0)]
-    last = [scatter(5 + k, part2, half + k * quarter, half + (k + 1) * quarter, k) for k in range(2)]
-    smalls = scatter(7, small_s, 0, 128, 0)
+        return Scatter(cube, source, slice(lo, hi), way, bufs[n], send.at[n], recv.at[n])
+
+    feeds = [scatter(k, part1, k * quarter, (k + 1) * quarter, ways[k % 2]) for k in range(4)]
+    heads = [
+        scatter(4 + p, part2, 128 * p, 128 * p + 128, ways[p % 2] if p < pairs - 1 else brief)
+        for p in range(pairs)
+    ]
+    smalls = scatter(8, small_s, 0, 128, brief)
 
     def start(group, step):
         for part in group:
@@ -725,8 +766,8 @@
         for part in group:
             for copy in part.copies(step):
                 copy.wait()
-        if step < steps - 1:
-            for part in group:
+        for part in group:
+            if step < part.steps - 1:
                 part.add(step)
 
     def loads(j):
@@ -750,8 +791,11 @@
 
     late = [
         pltpu.make_async_copy(a, b, late_sem.at[n])
-        for n, (a, b) in enumerate(((x_any, x_ref), (g1_any, g1), (res_any, res_ref)))
+        for n, (a, b) in enumerate(((g1_any, g1), (res_any, res_ref)))
     ]
+
+    def x_load(s):
+        return pltpu.make_async_copy(x_any.at[s], x_ref.at[s], late_sem.at[2 + s])
 
     prob_load(0).start()
 
@@ -760,9 +804,9 @@
         for load in loads(j):
             load.start()
 
-    for load in late:
+    for load in [x_load(s) for s in range(seqs)] + late:
         load.start()
-    cube.barrier(ways)
+    cube.barrier(ways + [brief])
     start(feeds, 0)
 
     lane = lax.broadcasted_iota(jnp.int32, (1, 128), 1)
@@ -825,29 +869,41 @@
             if b + 1 < 2 * per_head:
                 grads(b + 1)
             pulls(b)
-        dq_s[s, :, at] = dqt[...].astype(bf16).T
-        for ref, tops, mems, unit in ((dk_s, dkt, dkm, LN2), (dv_s, dvt, dvm, 1.0)):
-            ref[s, 0:length, at] = (tops[...] * unit).astype(bf16).T
-            ref[s, length:keys, at] = ((mems[...] * unit).T)[0 : keys - length, :].astype(bf16)
+        units = ((dq_s, dqt, None, 1.0), (dk_s, dkt, dkm, LN2), (dv_s, dvt, dvm, 1.0))
+        news = []
+        for n, (ref, tops, mems, unit) in enumerate(units):
+            low = (tops[...] * unit).astype(bf16)
+            turned[128 * n : 128 * n + 128, :] = low
+            ref[s, 0:length, at] = low.T
+            if mems is not None:
+                low = (mems[...] * unit).astype(bf16)
+                ref[s, length:keys, at] = low.T
+                news.append(dg(low, mem_ref[...], NN))
+        new = dg(turned[...], x_ref[s], NN)
+        add = jnp.where(s == 0, 0.0, 1.0)
+        terms[0:128, :] = terms[0:128, :] * add + new[0:128, :] * HEAD_DIM**-0.5
+        for n in range(2):
+            own = slice(128 * (n + 1), 128 * (n + 2))
+            terms[own, :] = terms[own, :] * add + (new[own, :] + news[n])
+        vec_s[0:1, at] = vec_s[0:1, at] * add + col_sum(dq_s[s, :, at].astype(f32)) * HEAD_DIM**-0.5
+        vec_s[1:2, at] = vec_s[1:2, at] * add + col_sum(dv_s[s, :, at].astype(f32))
+
+        @pl.when(s == seqs - 1)
+        def _():
+            for n in range(3):
+                low = terms[128 * n : 128 * n + 128, :].astype(bf16).T
+                part2[(slice(None),) * nb + (slice(n * r, n * r + r), at)] = low.reshape(
+                    (2,) * nb + (r, 128)
+                )
+
+    terms[...] = jnp.zeros_like(terms)
+    vec_s[...] = jnp.zeros_like(vec_s)
 
     def weight(j):
         return g1[(slice(None),) * nb + (slice(j * r, j * r + r), slice(None))].reshape(width, width)
 
     scale = HEAD_DIM**-0.5
     tail = slice(length, keys)
-
-    def terms(k):
-        mem = mem_ref[...]
-        for j, ref in enumerate((dq_s, dk_s, dv_s)):
-            total = 0.0
-            for s in range(seqs):
-                total = total + dg(x_ref[s], ref[s, 0:length, halves[k]], TN)
-                if j:
-                    total = total + dg(mem, ref[s, tail, halves[k]], TN)
-            if j == 0:
-                total = total * scale
-            cuts = (slice(None),) * nb + (slice(j * r, j * r + r), halves[k])
-            part2[cuts] = total.astype(bf16).reshape((2,) * nb + (r, half))
 
     turns = seqs * pairs
 
@@ -860,34 +916,33 @@
         for load in loads(j) + [prob_load(j)]:
             load.wait()
 
+        for s in range(seqs):
+
+            @pl.when(j == s)
+            def _():
+                x_load(s).wait()
+
         plan = ((1, feeds, 0), (3, feeds[:2], 1), (4, feeds[2:], 1), (5, feeds[:2], 2))
-        plan += ((6, feeds[2:], 2), (5, first, 0), (6, first, 1), (7, first, 2))
+        plan += ((6, feeds[2:], 2), (2, heads[:1], -1), (4, heads[1:2], -1), (6, heads[2:3], -1))
+        plan += ((5, heads[:2], 0), (6, heads[:2], 1), (7, heads[:2], 2), (7, heads[2:3], 0))
         for slot, group, step in plan:
 
             @pl.when(j == (slot * turns) // 8)
             def _():
-                finish(group, step)
+                if step >= 0:
+                    finish(group, step)
                 start(group, step + 1)
 
-        @pl.when(j == turns // 2)
-        def _():
-            for load in late:
-                load.wait()
-            terms(0)
-            start(first, 0)
-
         pair(j)
 
-    terms(1)
-    start(last, 0)
-    bq = sum(col_sum(dq_s[s].astype(f32)) for s in range(seqs)) * scale
-    bv = sum(col_sum(dv_s[s].astype(f32)) for s in range(seqs))
-    gmem = sum(
-        dg(dk_s[s, tail, :], weight(1), NT) + dg(dv_s[s, tail, :], weight(2), NT)
-        for s in range(seqs)
-    )
+    start(heads[3:], 0)
+    for load in late:
+        load.wait()
+    tails = [jnp.concatenate([ref[s, tail, :] for s in range(seqs)], 0) for ref in (dk_s, dv_s)]
+    both = dg(tails[0], weight(1), NT) + dg(tails[1], weight(2), NT)
+    gmem = sum(both[s * (keys - length) : (s + 1) * (keys - length), :] for s in range(seqs))
     vec_row = lax.broadcasted_iota(jnp.int32, (8, width), 0)
-    vecs = jnp.where(vec_row == 0, bq, jnp.where(vec_row == 1, bv, gvec_ref[...]))
+    vecs = jnp.where(vec_row < 2, vec_s[...], gvec_ref[...])
     flat = jnp.concatenate(
         [
             gmem[0:16, :],
@@ -918,27 +973,33 @@
         return out
 
     def total(part, lo, hi):
-        sums_o[lo:hi, part.lanes] = part.total(steps - 1)
+        sums_o[lo:hi, part.lanes] = part.total(part.steps - 1)
 
     todo = list(range(seqs * tiles))
     outs = []
-    group = last + [smalls]
-    for step in range(steps):
+    group = heads[3:] + [smalls]
+    for step in range(len(brief)):
         if todo:
             outs.append(inputs(todo.pop(0)))
-        if step == steps - 2:
-            finish(feeds + first, steps - 1)
+        finish(group, step)
+        if step + 1 < len(brief):
+            start(group, step + 1)
+        if step == 0:
+            finish(heads[2:3], 1)
+            start(heads[2:3], 2)
+            finish(feeds, steps - 1)
             for part in feeds:
                 total(part, 3 * r, sums_o.shape[0])
-            total(first[0], 0, 3 * r)
-        finish(group, step)
-        if step + 1 < steps:
-            start(group, step + 1)
+        if step == 1:
+            finish(heads[2:3], 2)
+            start(heads[2:3], 3)
+            finish(heads[:2], steps - 1)
     for i in todo:
         outs.append(inputs(i))
-    for part in last:
+    finish(heads[2:3], 3)
+    for part in heads:
         total(part, 0, 3 * r)
-    small_o[...] = smalls.total(steps - 1)
+    small_o[...] = smalls.total(smalls.steps - 1)
     for out in outs:
         out.wait()
 
@@ -952,7 +1013,7 @@
     way = list(reversed(routes(nb)[0]))
     links = (len(way), most(way))
     block = prob.shape[4]
-    half, quarter = width // 2, width // 4
+    quarter = width // 4
     turns = seqs * (HEADS // 2)
     shape = jax.ShapeDtypeStruct
     vm = pl.BlockSpec(memory_space=VMEM)
@@ -984,15 +1045,18 @@
             VMEM((128, length), f32),
             VMEM((128, KEY_PAD), f32),
             VMEM((128, KEY_PAD), f32),
+            VMEM((384, length), bf16),
+            VMEM((384, width), f32),
+            VMEM((8, width), f32),
             VMEM(cube + (3 * r, width), bf16),
             VMEM(cube + (16, 128), f32),
         ]
         + scatter_bufs(nb, way, (rows2, quarter), bf16) * 4
-        + scatter_bufs(nb, way, (3 * r, half), bf16)
-        + scatter_bufs(nb, way, (3 * r, quarter), bf16) * 2
-        + scatter_bufs(nb, way, (16, 128), f32)
-        + [dma((8,) + links)] * 2
-        + [dma((turns, 6)), dma((3,)), dma((seqs * (length // 512),)), dma((2,))],
+        + scatter_bufs(nb, way, (3 * r, 128), bf16) * 3
+        + scatter_bufs(nb, short(way), (3 * r, 128), bf16)
+        + scatter_bufs(nb, short(way), (16, 128), f32)
+        + [dma((9,) + links)] * 2
+        + [dma((turns, 6)), dma((2 + seqs,)), dma((seqs * (length // 512),)), dma((2,))],
         compiler_params=pltpu.CompilerParams(
             collective_id=1, has_side_effects=True, vmem_limit_bytes=62 * 2**20
         ),

time: 185 us -> 175 us (0.946)
  Pallas kernels: 184 us -> 174 us
    pallas_call x1, Pallas kernels: 68.8 us -> 61.9 us  [pull_call(): pl.pallas_call(functools.partial(pull_kernel, count, sub, mem_rows, r, fr...]
    pallas_call x1, Pallas kernels: 61.3 us -> 58 us  [attend_call(): pl.pallas_call(functools.partial(attend_kernel, count, sub, mem_rows), ou...]
where the time goes in v4:
time: 175 us
  Pallas kernels  174 us (99%)
    pallas_call x1, Pallas kernels, pull_call(): pl.pallas_call(functools.partial(pull_kernel, count, sub, mem_rows, r, fr...  61.9 us
    pallas_call x1, Pallas kernels, attend_call(): pl.pallas_call(functools.partial(attend_kernel, count, sub, mem_rows), ou...  58 us
    pallas_call x1, Pallas kernels, feed_call(): pl.pallas_call(functools.partial(feed_kernel, r, fr, seqs * tiles), grid=...  50.2 us
    pallas_call x1, Pallas kernels, results_call(): pl.pallas_call(functools.partial(results_kernel, r, fr, mem_rows), out_sh...  3.85 us

profile of v4, /device:TPU:0, one launch (start us, length us, event | category | flops | bytes accessed | tf_op | source)
XLA Modules:
  0.0 174.9 jit_solution(1273756555771310757)
XLA Ops:
  0.7 58.0 %attend.1 = (bf16[2,4,128,1024]{3,2,1,0:T(8,128)(2,1)}, bf16[2,4,128,1056]{3,2,1,0:T(8,128)(2,1)}, bf16[2,4,1056,128]{3,2,1,0:T(8,128)(2,1)}, bf16[2,8,64,1024]{...) custom-call(s32[2]{0:T(128)} %len_ref.1, ...), custom_call_target="tpu_custom_call" | custom-call | tf_op jit(solution)/shard_map/attend/pallas_call | solution.py:492
  58.7 50.2 %feed.1 = (bf16[2,1024,512]{2,1,0:T(8,128)(2,1)}, f32[2,1024,512]{2,1,0:T(8,128)}, bf16[2,4,1024,128]{3,2,1,0:T(8,128)(2,1)}, bf16[32,144,512]{2,1,0:T(8,128)(2,...) custom-call(bf16[2,1024,512]{2,1,0:T(8,128)(2,1)} %x_any.3, bf16[2,512,1024]{2,1,0:T(8,128)(2,1)} %bitcast.23, ...), custom_call_target="tpu_custom_call" | custom-call | tf_op jit(solution)/shard_map/feed/pallas_call | solution.py:690
  108.9 61.9 %pull.1 = (bf16[2,1024,512]{2,1,0:T(8,128)(2,1)}, f32[192,512]{1,0:T(8,128)}, f32[16,128]{1,0:T(8,128)}) custom-call(bf16[2,1024,512]{2,1,0:T(8,128)(2,1)} %x_any.3, bf16[32,512]{1,0:T(8,128)(2,1)} %get-tuple-element.60.mem_ref, bf16[2,4,128,1024]{3,2,1,0:T(8,128)(2,1)} %get-tuple-element.61.q_any, bf16[2,4,128,1056]{3,2,1,0:T(8,128)(2,1)} %get-tuple-element.62.k_any, ...), custom_call_target="tpu_custom_call" | custom-call | tf_op jit(solution)/shard_map/pull/pallas_call | solution.py:1022
  170.8 3.8 %results.1 = (bf16[2,1024,512]{2,1,0:T(8,128)(2,1)}, f32[16,512]{1,0:T(8,128)}, f32[16,512]{1,0:T(8,128)}, f32[16,512]{1,0:T(8,128)}, f32[16,512]{1,0:T(8,128)},...) custom-call(bf16[2,1024,512]{2,1,0:T(8,128)(2,1)} %get-tuple-element, ...), custom_call_target="tpu_custom_call" | custom-call | tf_op jit(solution)/shard_map/results/pallas_call | solution.py:1095

commit v5 on v4

--- a/solution.py
+++ b/solution.py
@@ -163,20 +163,14 @@
     return bufs
 
 
-def attend_kernel(
-    count, sub, mem_rows,
-    len_ref, x_any, wq_ref, wk_ref, wv_ref, wo_ref, wu_ref, wd_ref, memt_ref, ub_ref, *rest,
+def attend_part(
+    cube, mem_rows,
+    len_ref, x_any, wq_ref, wk_ref, wv_ref, wo_ref, wu_ref, wd_ref, memt_ref, ub_ref, vec_refs,
+    x_ref, q_o, k_o, v_o, att_o, inv_o, g1, g2, gs, vec_o, ub_o, mem_o, prob_any,
+    qt_o, ksel, vt_s, score_a, score_b, prob_s, top_a, top_b, flat_s, wide_s,
+    local, x_sem, prob_sem, send1, recv1, send2, recv2, send3, recv3,
 ):
-    vec_refs, rest = rest[:8], rest[8:]
-    (
-    q_any, k_any, v_any, att_any, inv_any, g1_any, prob_any, g2, vec_o, ub_o, mem_o,
-    x_ref, q_o, k_o, v_o, att_o, inv_o, g1,
-    qt_o, gs, ksel, vt_s, score_a, score_b, prob_s, top_a, top_b,
-    flat_s, wide_s,
-    local, x_sem, out_sem, head_sem, prob_sem, send1, recv1, send2, recv2, send3, recv3,
-    ) = rest
-    cube = Cube(count, sub)
-    nb = cube.nb
+    nb, count = cube.nb, cube.count
     seqs, length, width = x_ref.shape
     keys = v_o.shape[2]
     mem_pad = keys - length
@@ -213,7 +207,7 @@
     ]
     for move in moves:
         move.start()
-    cube.barrier(ways)
+    cube.barrier([*ways, short(list(reversed(ways[0])))])
 
     every_row = slice(None)
 
@@ -349,8 +343,6 @@
     arrived(3)
     advance(0, 1)
     advance(1, 1)
-    g1_out = pltpu.make_async_copy(g1, g1_any, out_sem.at[0])
-    g1_out.start()
 
     @pl.loop(0, seqs * tiles)
     def _(i):
@@ -410,23 +402,8 @@
             prob_s.at[slot], prob_any.at[s, h, i % per_head], prob_sem.at[slot]
         )
 
-    outs = [
-        pltpu.make_async_copy(src, dst, out_sem.at[1 + n])
-        for n, (src, dst) in enumerate(((q_o, q_any), (k_o, k_any), (v_o, v_any)))
-    ]
-    for out in outs:
-        out.start()
     turn(None, None, (0, score_a, top_a))
     turns = blocks // 2
-    heads_a_turn = max(1, 2 // per_head)
-
-    def head_outs(j):
-        s, h = j // HEADS, j % HEADS
-        return [
-            pltpu.make_async_copy(att_o.at[s, h], att_any.at[s, h], head_sem.at[j, 0]),
-            pltpu.make_async_copy(inv_o.at[s, h], inv_any.at[s, h], head_sem.at[j, 1]),
-        ]
-
     plan = ((2, 0, 2), (2, 1, 2), (3, 2, 1), (3, 3, 1), (9, 0, 3), (9, 1, 3), (9, 2, 2), (9, 3, 2))
     plan += ((15, 2, 3), (15, 3, 3))
 
@@ -448,90 +425,12 @@
         turn(2 * j, (score_a, top_a, (odd, 0)), (2 * j + 1, score_b, top_b))
         then = jnp.minimum(2 * j + 2, blocks - 1)
         turn(2 * j + 1, (score_b, top_b, (odd, 1)), (then, score_a, top_a))
-        for k in range(heads_a_turn):
-            for out in head_outs(j * heads_a_turn + k):
-                out.start()
 
     for c in range(chunks):
         advance(c, steps)
     for j in range(max(0, turns - 2), turns):
         for k in range(2):
             prob_out(2 * j + k, (j % 2, k)).wait()
-    for out in outs + [g1_out]:
-        out.wait()
-
-    @pl.loop(0, seqs * HEADS)
-    def _(j):
-        for out in head_outs(j):
-            out.wait()
-
-
-def attend_call(count, sub, lengths, x, wq, wk, wv, wo, wu, wd, memt, ub, vecs, mem_rows):
-    seqs, length, width = x.shape
-    r, ff, fr = wq.shape[0], wu.shape[1], wd.shape[0]
-    rows2 = r + (ff // width) * r + fr
-    keys = length + KEY_PAD
-    nb = count.bit_length() - 1
-    cube = (2,) * nb
-    way = routes(nb)[0]
-    links = (len(way), most(way))
-    block = min(512, length)
-    pairs = HEADS // 2
-    shape = jax.ShapeDtypeStruct
-    vm = pl.BlockSpec(memory_space=VMEM)
-    hbm = pl.BlockSpec(memory_space=pl.ANY)
-    dma = pltpu.SemaphoreType.DMA
-    kept = (
-        shape((seqs, pairs, 128, length), bf16),
-        shape((seqs, pairs, 128, keys), bf16),
-        shape((seqs, pairs, keys, 128), bf16),
-        shape((seqs, HEADS, HEAD_DIM, length), bf16),
-        shape((seqs, HEADS, 1, length), f32),
-        shape(cube + (3 * r, width), bf16),
-    )
-    return pl.pallas_call(
-        functools.partial(attend_kernel, count, sub, mem_rows),
-        out_shape=kept
-        + (
-            shape((seqs, HEADS, length // block, keys, block), bf16),
-            shape(cube + (rows2, width), bf16),
-            shape((8, width), f32),
-            shape((1, ff), f32),
-            shape((KEY_PAD, width), bf16),
-        ),
-        in_specs=[pl.BlockSpec(memory_space=pltpu.SMEM), hbm] + [vm] * 16,
-        out_specs=[hbm] * 8 + [vm] * 3,
-        scratch_shapes=[VMEM(x.shape, bf16)]
-        + [VMEM(a.shape, a.dtype) for a in kept]
-        + [
-            VMEM((seqs, HEADS, 128, length), bf16),
-            VMEM(cube + (16, 128), bf16),
-            VMEM((seqs, HEADS, keys, 128), bf16),
-            VMEM((seqs, HEADS, 80, keys), bf16),
-            VMEM((keys, block), f32),
-            VMEM((keys, block), f32),
-            VMEM((2, 2, keys, block), bf16),
-            VMEM((1, block), f32),
-            VMEM((1, block), f32),
-            VMEM((16, 128), f32),
-            VMEM((128, 128), f32),
-            dma((2 + ff // width,)),
-            dma,
-            dma((4,)),
-            dma((seqs * HEADS, 2)),
-            dma((2, 2)),
-            dma((6,) + links),
-            dma((6,) + links),
-            dma((4,) + links),
-            dma((4,) + links),
-            dma(links),
-            dma(links),
-        ],
-        compiler_params=pltpu.CompilerParams(
-            collective_id=0, has_side_effects=True, vmem_limit_bytes=60 * 2**20
-        ),
-        name="attend",
-    )(lengths, x, wq, wk, wv, wo, wu, wd, memt, ub, *vecs)
 
 
 def norm_forward(value, gain, shift):
@@ -550,194 +449,159 @@
     )
 
 
-def feed_kernel(
-    r, fr, steps,
-    x_ref, att_ref, dy_ref, g2, vec, ub,
-    out_o, res_o, datt_o, part_o, gvec, gub,
-    act_s, slope_s, low_s, outer_s, branch_s, gwo, gwu, gwd,
+def tile_copy(i, rows, source, target, sem):
+    tiles = source.shape[1] // rows
+    s, start = i // tiles, (i % tiles) * rows
+    own = pl.ds(start if isinstance(i, int) else pl.multiple_of(start, rows), rows)
+    return pltpu.make_async_copy(source.at[s, own], target.at[s, own], sem.at[i])
+
+
+def feed_part(
+    cube, r, fr,
+    x_all, att_all, dy_all, g2, vec, ub, out_all, out_any, res_all, datt_all, gvec, gub,
+    act_s, slope_s, low_s, outer_s, branch_s, gwo, gwu, gwd, out_sem,
 ):
-    i = pl.program_id(0)
-    rows, width = x_ref.shape[1:]
-    count = g2.shape[0]
-    cols = g2.shape[1] // r - 1 - fr // r
-    per = width // fr
-
-    @pl.when(i == 0)
-    def _():
-        for ref in (gwo, gwu, gwd, gvec, gub):
-            ref[...] = jnp.zeros_like(ref)
+    nb = cube.nb
+    rows, width = low_s.shape
+    length = x_all.shape[1]
+    tiles = length // rows
+    steps = x_all.shape[0] * tiles
+    cols = g2.shape[-2] // r - 1 - fr // r
+    high = cols.bit_length() - 1
+    half = rows // 2
+    every = (slice(None),) * nb
+
+    for ref in (gwo, gwu, gwd, gvec, gub):
+        ref[...] = jnp.zeros_like(ref)
 
     bo, ga, sa, bd, gb, sb = [vec[j : j + 1, :] for j in range(2, 8)]
 
     def wo():
-        return g2[:, 0:r, :].reshape(width, width)
+        return g2[every + (slice(0, r), slice(None))].reshape(width, width)
 
     def wu(c):
-        return g2[:, r + c * r : r + c * r + r, :].reshape(width, width)
+        return g2[every + (slice(r + c * r, r + c * r + r), slice(None))].reshape(width, width)
 
     def wd(c):
-        return g2[c * per : (c + 1) * per, r + cols * r :, :].reshape(width, width)
-
-    class Part:
-        def __init__(self, at):
-            self.at = at
-
-        def enter(self):
-            branch = dg(att_ref[0, :, self.at], wo(), TN)
-            value = x_ref[0, self.at, :].astype(f32) + branch + bo
-            hidden, self.normed, self.inverse = norm_forward(value, ga, sa)
-            self.low = hidden.astype(bf16)
-            low_s[self.at, :] = self.low
-            self.outer = hidden + bd
-
-        def forward(self, c):
-            u = dg(self.low, wu(c), NN) + ub[:, c * width : (c + 1) * width]
-            bend = GELU_A + GELU_B * (u * u)
-            gate = 0.5 + 0.5 * jnp.tanh(u * bend)
-            act = u * gate
-            low = act.astype(bf16)
-            act_s[c][self.at, :] = low
-            slope = gate + act * (1.0 - gate) * (6.0 * bend - 4.0 * GELU_A)
-            slope_s[c][self.at, :] = slope.astype(bf16)
-            self.outer = self.outer + dg(low, wd(c), NN)
-
-        def turn(self):
-            out, normed, inverse = norm_forward(self.outer, gb, sb)
-            out_o[0, self.at, :] = out.astype(bf16)
-            dy = dy_ref[0, self.at, :].astype(f32)
-            gvec[6:7, :] += col_sum(dy * normed)
-            gvec[7:8, :] += col_sum(dy)
-            self.d_hidden = norm_backward(dy, normed, inverse, gb)
-            gvec[5:6, :] += col_sum(self.d_hidden)
-            self.d_outer = self.d_hidden.astype(bf16)
-            outer_s[self.at, :] = self.d_outer
-
-        def backward(self, c):
-            d_act = dg(self.d_outer, wd(c), NT)
-            d_inner = d_act * slope_s[c][self.at, :].astype(f32)
-            gub[:, c * width : (c + 1) * width] += col_sum(d_inner)
-            low = d_inner.astype(bf16)
-            slope_s[c][self.at, :] = low
-            self.d_hidden = self.d_hidden + dg(low, wu(c), NT)
-
-        def leave(self):
-            gvec[3:4, :] += col_sum(self.d_hidden * self.normed)
-            gvec[4:5, :] += col_sum(self.d_hidden)
-            d_res1 = norm_backward(self.d_hidden, self.normed, self.inverse, ga)
-            res_o[0, self.at, :] = d_res1
-            gvec[2:3, :] += col_sum(d_res1)
-            d_branch = d_res1.astype(bf16)
-            branch_s[self.at, :] = d_branch
-            d_att = dg(d_branch, wo(), NT).astype(bf16)
-            for p in range(width // 128):
-                datt_o[0, p, self.at, :] = d_att[:, 128 * p : 128 * p + 128]
-
-    half = rows // 2
-    a, b = Part(slice(0, half)), Part(slice(half, rows))
-    a.enter()
-    b.enter()
+        top = tuple((c >> k) & 1 for k in range(high - 1, -1, -1))
+        rest = every[high:] + (slice(r + cols * r, None), slice(None))
+        return g2[top + rest].reshape(width, width)
+
+    def feed_tile(seq, base):
+        tile = pl.ds(pl.multiple_of(base, rows), rows)
+        class Part:
+            def __init__(self, low):
+                self.at = slice(low, low + half)
+                self.all = pl.ds(pl.multiple_of(base + low, half), half)
+
+            def enter(self):
+                branch = dg(att_all[seq, :, :, self.all].reshape(width, half), wo(), TN)
+                value = x_all[seq, self.all, :].astype(f32) + branch + bo
+                hidden, self.normed, self.inverse = norm_forward(value, ga, sa)
+                self.low = hidden.astype(bf16)
+                low_s[self.at, :] = self.low
+                self.outer = hidden + bd
+
+            def forward(self, c):
+                u = dg(self.low, wu(c), NN) + ub[:, c * width : (c + 1) * width]
+                bend = GELU_A + GELU_B * (u * u)
+                gate = 0.5 + 0.5 * jnp.tanh(u * bend)
+                act = u * gate
+                low = act.astype(bf16)
+                act_s[c][self.at, :] = low
+                slope = gate + act * (1.0 - gate) * (6.0 * bend - 4.0 * GELU_A)
+                slope_s[c][self.at, :] = slope.astype(bf16)
+                self.outer = self.outer + dg(low, wd(c), NN)
+
+            def turn(self):
+                out, normed, inverse = norm_forward(self.outer, gb, sb)
+                out_all[seq, self.all, :] = out.astype(bf16)
+                dy = dy_all[seq, self.all, :].astype(f32)
+                gvec[6:7, :] += col_sum(dy * normed)
+                gvec[7:8, :] += col_sum(dy)
+                self.d_hidden = norm_backward(dy, normed, inverse, gb)
+                gvec[5:6, :] += col_sum(self.d_hidden)
+                self.d_outer = self.d_hidden.astype(bf16)
+                outer_s[self.at, :] = self.d_outer
+
+            def backward(self, c):
+                d_act = dg(self.d_outer, wd(c), NT)
+                d_inner = d_act * slope_s[c][self.at, :].astype(f32)
+                gub[:, c * width : (c + 1) * width] += col_sum(d_inner)
+                low = d_inner.astype(bf16)
+                slope_s[c][self.at, :] = low
+                self.d_hidden = self.d_hidden + dg(low, wu(c), NT)
+
+            def leave(self):
+                gvec[3:4, :] += col_sum(self.d_hidden * self.normed)
+                gvec[4:5, :] += col_sum(self.d_hidden)
+                d_res1 = norm_backward(self.d_hidden, self.normed, self.inverse, ga)
+                res_all[seq, self.all, :] = d_res1
+                gvec[2:3, :] += col_sum(d_res1)
+                d_branch = d_res1.astype(bf16)
+                branch_s[self.at, :] = d_branch
+                d_att = dg(d_branch, wo(), NT).astype(bf16)
+                for p in range(width // 128):
+                    datt_all[seq, p, self.all, :] = d_att[:, 128 * p : 128 * p + 128]
+
+        a, b = Part(0), Part(half)
+        a.enter()
+        b.enter()
+        for c in range(cols):
+            a.forward(c)
+        b.forward(0)
+        a.turn()
+        for c in range(1, cols):
+            b.forward(c)
+        a.backward(0)
+        b.turn()
+        for c in range(1, cols):
+            a.backward(c)
+        b.backward(0)
+        a.leave()
+        for c in range(1, cols):
+            b.backward(c)
+        for c in range(cols):
+            at = slice(c * width, (c + 1) * width)
+            gwd[at, :] += dg(act_s[c][...], outer_s[...], TN)
+            gwu[:, at] += dg(low_s[...], slope_s[c][...], TN)
+            if c == 0:
+                b.leave()
+        gwo[...] += dg(att_all[seq, :, :, tile].reshape(width, rows), branch_s[...], NN)
+
+    @pl.loop(0, steps)
+    def _(i):
+        feed_tile(i // tiles, (i % tiles) * rows)
+        tile_copy(i, rows, out_all, out_any, out_sem).start()
+
+    g2[every + (slice(0, r), slice(None))] = gwo[...].astype(bf16).reshape((2,) * nb + (r, width))
     for c in range(cols):
-        a.forward(c)
-    b.forward(0)
-    a.turn()
-    for c in range(1, cols):
-        b.forward(c)
-    a.backward(0)
-    b.turn()
-    for c in range(1, cols):
-        a.backward(c)
-    b.backward(0)
-    a.leave()
-    for c in range(1, cols):
-        b.backward(c)
-    for c in range(cols):
-        at = slice(c * width, (c + 1) * width)
-        gwd[at, :] += dg(act_s[c][...], outer_s[...], TN)
-        gwu[:, at] += dg(low_s[...], slope_s[c][...], TN)
-        if c == 0:
-            b.leave()
-    gwo[...] += dg(att_ref[0], branch_s[...], NN)
-
-    @pl.when(i == steps - 1)
-    def _():
-        part_o[:, 0:r, :] = gwo[...].astype(bf16).reshape(count, r, width)
-        for c in range(cols):
-            part_o[:, r + c * r : r + c * r + r, :] = (
-                gwu[:, c * width : (c + 1) * width].astype(bf16).reshape(count, r, width)
-            )
-        part_o[:, r + cols * r :, :] = gwd[...].astype(bf16).reshape(count, fr, width)
-
-
-def feed_call(x, att, dy, g2, vec, ub, r, fr):
-    seqs, length, width = x.shape
-    ff = ub.shape[1]
-    tile = min(512, length)
-    tiles = length // tile
-    shape = jax.ShapeDtypeStruct
-    rows = pl.BlockSpec((1, tile, width), lambda i: (i // tiles, i % tiles, 0))
-
-    def full(a):
-        return pl.BlockSpec(a.shape, lambda i: (0,) * len(a.shape))
-
-    outs = (
-        shape((seqs, length, width), bf16),
-        shape((seqs, length, width), f32),
-        shape((seqs, width // 128, length, 128), bf16),
-        shape(g2.shape, bf16),
-        shape((8, width), f32),
-        shape((1, ff), f32),
+        g2[every + (slice(r + c * r, r + c * r + r), slice(None))] = (
+            gwu[:, c * width : (c + 1) * width].astype(bf16).reshape((2,) * nb + (r, width))
+        )
+    g2[every + (slice(r + cols * r, None), slice(None))] = (
+        gwd[...].astype(bf16).reshape((2,) * nb + (fr, width))
     )
-    return pl.pallas_call(
-        functools.partial(feed_kernel, r, fr, seqs * tiles),
-        grid=(seqs * tiles,),
-        out_shape=outs,
-        in_specs=[
-            rows,
-            pl.BlockSpec((1, width, tile), lambda i: (i // tiles, 0, i % tiles)),
-            rows,
-            full(g2),
-            full(vec),
-            full(ub),
-        ],
-        out_specs=[
-            rows,
-            rows,
-            pl.BlockSpec((1, width // 128, tile, 128), lambda i: (i // tiles, 0, i % tiles, 0)),
-        ]
-        + [full(a) for a in outs[3:]],
-        scratch_shapes=[
-            [VMEM((tile, width), bf16)] * (ff // width),
-            [VMEM((tile, width), bf16)] * (ff // width),
-            VMEM((tile, width), bf16),
-            VMEM((tile, width), bf16),
-            VMEM((tile, width), bf16),
-            VMEM((width, width), f32),
-            VMEM((width, ff), f32),
-            VMEM((ff, width), f32),
-        ],
-        compiler_params=pltpu.CompilerParams(vmem_limit_bytes=60 * 2**20),
-        name="feed",
-    )(x, att, dy, g2, vec, ub)
-
-
-def pull_kernel(
-    count, sub, mem_rows, r, fr,
-    x_any, mem_ref, q_any, k_any, v_any, att_any, inv_any, prob_any, da_any, res_any, g1_any, part1,
-    gvec_ref, gub_ref,
-    dx_any, sums_o, small_o,
-    x_ref, q_ref, k_ref, v_ref, att_ref, inv_ref, da_ref, res_ref, g1, dx_o,
-    prob_s, vsel, dot_s, d_a, d_b, pt_s, dt_s, dq_s, dk_s, dv_s, dqt, dkt, dvt, dkm, dvm, turned, terms,
-    vec_s, part2, small_s, *rest,
+
+
+def prob_load(j, seqs, prob_any, prob_s, prob_sem):
+    p, s = j // seqs, j % seqs
+    return pltpu.make_async_copy(
+        prob_any.at[s, pl.ds(2 * p, 2)], prob_s.at[j % 2], prob_sem.at[j % 2]
+    )
+
+
+def pull_part(
+    cube, mem_rows, r, fr,
+    x_ref, mem_ref, q_ref, k_ref, v_ref, att_ref, inv_ref, prob_any, da_ref, res_ref, g1, part1,
+    gvec_ref, gub_ref, dx_any, sums_o, small_o, prob_s,
+    vsel, dot_s, d_a, d_b, pt_s, dt_s, dq_s, dk_s, dv_s, dqt, dkt, dvt, dkm, dvm, turned, terms,
+    vec_s, part2, small_s, bufs, send, recv, out_sem, prob_sem,
 ):
-    cube = Cube(count, sub)
-    nb = cube.nb
+    nb, count = cube.nb, cube.count
     ways = [list(reversed(route)) for route in routes(nb)]
     steps = len(ways[0])
     brief = short(ways[0])
-    sizes = [steps] * 7 + [len(brief)] * 2
-    ends = [sum(sizes[: k + 1]) for k in range(len(sizes))]
-    bufs = [rest[end - size : end] for size, end in zip(sizes, ends, strict=True)]
-    send, recv, load_sem, late_sem, out_sem, prob_sem = rest[ends[-1] :]
     seqs, length, width = x_ref.shape
     keys = v_ref.shape[2]
     ff = gub_ref.shape[1]
@@ -770,43 +634,9 @@
             if step < part.steps - 1:
                 part.add(step)
 
-    def loads(j):
-        p, s = j // seqs, j % seqs
-        own = ((q_any, q_ref), (k_any, k_ref), (v_any, v_ref), (da_any, da_ref))
-        out = [
-            pltpu.make_async_copy(a.at[s, p], b.at[s, p], load_sem.at[j, n])
-            for n, (a, b) in enumerate(own)
-        ]
-        both = pl.ds(2 * p, 2)
-        return out + [
-            pltpu.make_async_copy(a.at[s, both], b.at[s, both], load_sem.at[j, 4 + n])
-            for n, (a, b) in enumerate(((att_any, att_ref), (inv_any, inv_ref)))
-        ]
-
-    def prob_load(j):
-        p, s = j // seqs, j % seqs
-        return pltpu.make_async_copy(
-            prob_any.at[s, pl.ds(2 * p, 2)], prob_s.at[j % 2], prob_sem.at[j % 2]
-        )
-
-    late = [
-        pltpu.make_async_copy(a, b, late_sem.at[n])
-        for n, (a, b) in enumerate(((g1_any, g1), (res_any, res_ref)))
-    ]
-
-    def x_load(s):
-        return pltpu.make_async_copy(x_any.at[s], x_ref.at[s], late_sem.at[2 + s])
-
-    prob_load(0).start()
-
-    @pl.loop(0, seqs * pairs)
-    def _(j):
-        for load in loads(j):
-            load.start()
-
-    for load in [x_load(s) for s in range(seqs)] + late:
-        load.start()
-    cube.barrier(ways + [brief])
+    def load(j):
+        return prob_load(j, seqs, prob_any, prob_s, prob_sem)
+
     start(feeds, 0)
 
     lane = lax.broadcasted_iota(jnp.int32, (1, 128), 1)
@@ -911,17 +741,9 @@
     def _(j):
         @pl.when(j + 1 < turns)
         def _():
-            prob_load(j + 1).start()
-
-        for load in loads(j) + [prob_load(j)]:
-            load.wait()
-
-        for s in range(seqs):
-
-            @pl.when(j == s)
-            def _():
-                x_load(s).wait()
-
+            load(j + 1).start()
+
+        load(j).wait()
         plan = ((1, feeds, 0), (3, feeds[:2], 1), (4, feeds[2:], 1), (5, feeds[:2], 2))
         plan += ((6, feeds[2:], 2), (2, heads[:1], -1), (4, heads[1:2], -1), (6, heads[2:3], -1))
         plan += ((5, heads[:2], 0), (6, heads[:2], 1), (7, heads[:2], 2), (7, heads[2:3], 0))
@@ -936,8 +758,6 @@
         pair(j)
 
     start(heads[3:], 0)
-    for load in late:
-        load.wait()
     tails = [jnp.concatenate([ref[s, tail, :] for s in range(seqs)], 0) for ref in (dk_s, dv_s)]
     both = dg(tails[0], weight(1), NT) + dg(tails[1], weight(2), NT)
     gmem = sum(both[s * (keys - length) : (s + 1) * (keys - length), :] for s in range(seqs))
@@ -967,8 +787,8 @@
         s, rows = i // tiles, pl.ds((i % tiles) * tile, tile)
         dx = res_ref[s, rows, :] + dg(dq_s[s, rows, :], weight(0), NT) * scale
         dx = dx + dg(dk_s[s, rows, :], weight(1), NT) + dg(dv_s[s, rows, :], weight(2), NT)
-        dx_o[s, rows, :] = dx.astype(bf16)
-        out = pltpu.make_async_copy(dx_o.at[s, rows], dx_any.at[s, rows], out_sem.at[i])
+        x_ref[s, rows, :] = dx.astype(bf16)
+        out = pltpu.make_async_copy(x_ref.at[s, rows], dx_any.at[s, rows], out_sem.at[i])
         out.start()
         return out
 
@@ -1004,70 +824,198 @@
         out.wait()
 
 
-def pull_call(count, sub, mem_rows, r, fr, x, mem, q, k, v, att, inv, prob, da, res, g1, part1, gvec, gub):
+def layer_kernel(
+    count, sub, mem_rows, r, fr, layout,
+    len_ref, x_any, dy_any, wq_ref, wk_ref, wv_ref, wo_ref, wu_ref, wd_ref, memt_ref, ub_ref, *rest,
+):
+    vec_refs, rest = rest[:8], rest[8:]
+    (out_any, dx_any, sums_o, small_o, prob_any), rest = rest[:5], rest[5:]
+    (x_ref, q_o, k_o, v_o, att_o, inv_o, g1, g2, gs, vec_o, ub_o, mem_o, gvec, gub), rest = rest[:14], rest[14:]
+    (bufs, sems1, feed_sem, dy_sem, load_sem, sems3) = rest
+    cube = Cube(count, sub)
+    early, late, feed, pull = layout
+    dy_load = []
+
+    def attend(*scoped):
+        attend_part(
+            cube, mem_rows,
+            len_ref, x_any, wq_ref, wk_ref, wv_ref, wo_ref, wu_ref, wd_ref, memt_ref, ub_ref,
+            vec_refs,
+            x_ref, q_o, k_o, v_o, att_o, inv_o, g1, g2, gs, vec_o, ub_o, mem_o, prob_any,
+            *scoped, *sems1,
+        )
+
+    pl.run_scoped(attend, *early)
+
+    def others(out_s, res_s, datt_s, part2, small_s, prob_s):
+        seqs = x_ref.shape[0]
+        prob_load(0, seqs, prob_any, prob_s, load_sem).start()
+
+        def forward(dy_s, *scoped):
+            load = pltpu.make_async_copy(dy_any, dy_s, dy_sem)
+            load.start()
+            load.wait()
+            feed_part(
+                cube, r, fr,
+                x_ref, att_o, dy_s, g2, vec_o, ub_o, out_s, out_any, res_s, datt_s, gvec, gub,
+                *scoped, feed_sem,
+            )
+
+        pl.run_scoped(forward, *feed)
+
+        def backward(*scoped):
+            pull_part(
+                cube, mem_rows, r, fr,
+                x_ref, mem_o, q_o, k_o, v_o, att_o, inv_o, prob_any, datt_s, res_s, g1, g2,
+                gvec, gub, dx_any, sums_o, small_o, prob_s,
+                *scoped, part2, small_s, bufs, *sems3, load_sem,
+            )
+
+        pl.run_scoped(backward, *pull)
+        tile = feed[3].shape[0]
+        for i in range(feed_sem.shape[0]):
+            tile_copy(i, tile, out_s, out_any, feed_sem).wait()
+
+    pl.run_scoped(others, *late)
+
+
+def layer_call(count, sub, mem_rows, lengths, x, dy, wq, wk, wv, wo, wu, wd, memt, ub, vecs):
     seqs, length, width = x.shape
-    keys = v.shape[2]
-    rows2 = part1.shape[-2]
+    r, ff, fr = wq.shape[0], wu.shape[1], wd.shape[0]
+    rows2 = r + (ff // width) * r + fr
+    keys = length + KEY_PAD
     nb = count.bit_length() - 1
     cube = (2,) * nb
-    way = list(reversed(routes(nb)[0]))
+    ways = routes(nb)
+    way = list(reversed(ways[0]))
     links = (len(way), most(way))
-    block = prob.shape[4]
+    wide = (len(way), max(most(way), most(short(way))))
+    block = min(512, length)
+    tile = min(512, length)
+    pairs = HEADS // 2
     quarter = width // 4
-    turns = seqs * (HEADS // 2)
     shape = jax.ShapeDtypeStruct
     vm = pl.BlockSpec(memory_space=VMEM)
     hbm = pl.BlockSpec(memory_space=pl.ANY)
     dma = pltpu.SemaphoreType.DMA
+    early = (
+        VMEM((seqs, HEADS, 128, length), bf16),
+        VMEM((seqs, HEADS, keys, 128), bf16),
+        VMEM((seqs, HEADS, 80, keys), bf16),
+        VMEM((keys, block), f32),
+        VMEM((keys, block), f32),
+        VMEM((2, 2, keys, block), bf16),
+        VMEM((1, block), f32),
+        VMEM((1, block), f32),
+        VMEM((16, 128), f32),
+        VMEM((128, 128), f32),
+    )
+    late = (
+        VMEM(x.shape, bf16),
+        VMEM(x.shape, f32),
+        VMEM((seqs, pairs, length, 128), bf16),
+        VMEM(cube + (3 * r, width), bf16),
+        VMEM(cube + (16, 128), f32),
+        VMEM((2, 2, length // block, keys, block), bf16),
+    )
+    feed = (
+        VMEM(x.shape, bf16),
+        [VMEM((tile, width), bf16)] * (ff // width),
+        [VMEM((tile, width), bf16)] * (ff // width),
+        VMEM((tile, width), bf16),
+        VMEM((tile, width), bf16),
+        VMEM((tile, width), bf16),
+        VMEM((width, width), f32),
+        VMEM((width, ff), f32),
+        VMEM((ff, width), f32),
+    )
+    pull = (
+        VMEM((2, keys, 128), bf16),
+        VMEM((2, 128, length), bf16),
+        VMEM((keys, block), bf16),
+        VMEM((keys, block), bf16),
+        VMEM((2, block, length), bf16),
+        VMEM((2, block, length), bf16),
+        VMEM((seqs, length, width), bf16),
+        VMEM((seqs, keys, width), bf16),
+        VMEM((seqs, keys, width), bf16),
+        VMEM((128, length), f32),
+        VMEM((128, length), f32),
+        VMEM((128, length), f32),
+        VMEM((128, KEY_PAD), f32),
+        VMEM((128, KEY_PAD), f32),
+        VMEM((384, length), bf16),
+        VMEM((384, width), f32),
+        VMEM((8, width), f32),
+    )
+    bufs = [scatter_bufs(nb, way, (rows2, quarter), bf16) for _ in range(4)]
+    bufs += [scatter_bufs(nb, way, (3 * r, 128), bf16) for _ in range(3)]
+    bufs += [scatter_bufs(nb, short(way), (3 * r, 128), bf16)]
+    bufs += [scatter_bufs(nb, short(way), (16, 128), f32)]
     return pl.pallas_call(
-        functools.partial(pull_kernel, count, sub, mem_rows, r, fr),
+        functools.partial(layer_kernel, count, sub, mem_rows, r, fr, (early, late, feed, pull)),
         out_shape=(
-            shape((seqs, length, width), bf16),
+            shape(x.shape, bf16),
+            shape(x.shape, bf16),
             shape((3 * r + rows2, width), f32),
             shape((16, 128), f32),
+            shape((seqs, HEADS, length // block, keys, block), bf16),
         ),
-        in_specs=[hbm, vm] + [hbm] * 9 + [vm] * 3,
-        out_specs=[hbm, vm, vm],
-        scratch_shapes=[VMEM(a.shape, a.dtype) for a in (x, q, k, v, att, inv, da, res, g1, x)]
-        + [
-            VMEM((2, 2) + prob.shape[2:], bf16),
-            VMEM((2, keys, 128), bf16),
-            VMEM((2, 128, length), bf16),
-            VMEM((keys, block), bf16),
-            VMEM((keys, block), bf16),
-            VMEM((2, block, length), bf16),
-            VMEM((2, block, length), bf16),
-            VMEM((seqs, length, width), bf16),
-            VMEM((seqs, keys, width), bf16),
-            VMEM((seqs, keys, width), bf16),
-            VMEM((128, length), f32),
-            VMEM((128, length), f32),
-            VMEM((128, length), f32),
-            VMEM((128, KEY_PAD), f32),
-            VMEM((128, KEY_PAD), f32),
-            VMEM((384, length), bf16),
-            VMEM((384, width), f32),
+        in_specs=[pl.BlockSpec(memory_space=pltpu.SMEM), hbm, hbm] + [vm] * 16,
+        out_specs=[hbm, hbm, vm, vm, hbm],
+        scratch_shapes=[
+            VMEM(x.shape, bf16),
+            VMEM((seqs, pairs, 128, length), bf16),
+            VMEM((seqs, pairs, 128, keys), bf16),
+            VMEM((seqs, pairs, keys, 128), bf16),
+            VMEM((seqs, HEADS, HEAD_DIM, length), bf16),
+            VMEM((seqs, HEADS, 1, length), f32),
+            VMEM(cube + (3 * r, width), bf16),
+            VMEM(cube + (rows2, width), bf16),
+            VMEM(cube + (16, 128), bf16),
             VMEM((8, width), f32),
-            VMEM(cube + (3 * r, width), bf16),
-            VMEM(cube + (16, 128), f32),
-        ]
-        + scatter_bufs(nb, way, (rows2, quarter), bf16) * 4
-        + scatter_bufs(nb, way, (3 * r, 128), bf16) * 3
-        + scatter_bufs(nb, short(way), (3 * r, 128), bf16)
-        + scatter_bufs(nb, short(way), (16, 128), f32)
-        + [dma((9,) + links)] * 2
-        + [dma((turns, 6)), dma((2 + seqs,)), dma((seqs * (length // 512),)), dma((2,))],
+            VMEM((1, ff), f32),
+            VMEM((KEY_PAD, width), bf16),
+            VMEM((8, width), f32),
+            VMEM((1, ff), f32),
+            bufs,
+            [
+                dma((2 + ff // width,)),
+                dma,
+                dma((2, 2)),
+                dma((6,) + links),
+                dma((6,) + links),
+                dma((4,) + links),
+                dma((4,) + links),
+                dma(links),
+                dma(links),
+            ],
+            dma((seqs * (length // tile),)),
+            dma,
+            dma((2,)),
+            [dma((9,) + wide), dma((9,) + wide), dma((seqs * (length // 512),))],
+        ],
         compiler_params=pltpu.CompilerParams(
-            collective_id=1, has_side_effects=True, vmem_limit_bytes=62 * 2**20
+            collective_id=0, has_side_effects=True, vmem_limit_bytes=63 * 2**20
         ),
-        name="pull",
-    )(x, mem, q, k, v, att, inv, prob, da, res, g1, part1, gvec, gub)
-
-
-def results_kernel(r, fr, mem_rows, dx_ref, sums, small, dx_o, *outs):
-    outs, sem = outs[:-1], outs[-1]
-    move = pltpu.make_async_copy(dx_ref, dx_o, sem)
-    move.start()
+        name="layer",
+    )(lengths, x, dy, wq, wk, wv, wo, wu, wd, memt, ub, *vecs)
+
+
+def results_kernel(r, fr, mem_rows, out_any, dx_any, sums, small, out_o, dx_o, *outs):
+    outs, (hold, load_sem, save_sem) = outs[:-3], outs[-3:]
+    seqs, length = out_any.shape[:2]
+    cut = length // 2
+    jobs = []
+    for n, (src, dst) in enumerate(((out_any, out_o), (dx_any, dx_o))):
+        for s in range(seqs):
+            for c in range(length // cut):
+                at = (s, slice(c * cut, (c + 1) * cut))
+                k = len(jobs)
+                load = pltpu.make_async_copy(src.at[at], hold.at[k], load_sem.at[k])
+                jobs.append((load, pltpu.make_async_copy(hold.at[k], dst.at[at], save_sem.at[k])))
+    for load, _ in jobs:
+        load.start()
     gq, gk, gv, go, gu, gd, gm, gb = outs[:8]
     vecs = outs[8:]
     width = gq.shape[1]
@@ -1083,23 +1031,36 @@
     for n, ref in enumerate(vecs):
         ref[...] = turned[VEC + n : VEC + n + 1, 0:r]
     gb[...] = value[0:1, 64 : 64 + fr]
-    move.wait()
-
-
-def results_call(r, fr, mem_rows, ff, dx, sums, small):
+    for load, save in jobs:
+        load.wait()
+        save.start()
+    for _, save in jobs:
+        save.wait()
+
+
+def results_call(r, fr, mem_rows, ff, out, dx, sums, small):
     width = sums.shape[1]
+    seqs, length = dx.shape[:2]
     shape = jax.ShapeDtypeStruct
     vm = pl.BlockSpec(memory_space=VMEM)
     hbm = pl.BlockSpec(memory_space=pl.ANY)
-    mats = [(r, width)] * 4 + [(r, ff), (fr, width), (r, mem_rows), (1, fr)] + [(1, r)] * 8
+    mats = [(r, width)] * 4 + [(r, ff), (fr, width), (mem_rows, r), (1, fr)] + [(1, r)] * 8
+    mats[6] = (r, mem_rows)
+    jobs = 4 * seqs
     return pl.pallas_call(
         functools.partial(results_kernel, r, fr, mem_rows),
-        out_shape=(shape(dx.shape, dx.dtype),) + tuple(shape(m, f32) for m in mats),
-        in_specs=[vm, vm, vm],
-        out_specs=[hbm] + [vm] * len(mats),
-        scratch_shapes=[pltpu.SemaphoreType.DMA],
+        out_shape=(shape(out.shape, out.dtype), shape(dx.shape, dx.dtype))
+        + tuple(shape(m, f32) for m in mats),
+        in_specs=[hbm, hbm, vm, vm],
+        out_specs=[hbm, hbm] + [vm] * len(mats),
+        scratch_shapes=[
+            VMEM((jobs, length // 2, width), bf16),
+            pltpu.SemaphoreType.DMA((jobs,)),
+            pltpu.SemaphoreType.DMA((jobs,)),
+        ],
+        compiler_params=pltpu.CompilerParams(vmem_limit_bytes=60 * 2**20),
         name="results",
-    )(dx, sums, small)
+    )(out, dx, sums, small)
 
 
 DIMS = (1, 0, 0, 0, 0, 0, 0, 0, 0, 0, 0, 0, 0, 0, 0, 0)
@@ -1121,26 +1082,12 @@
     mem_rows = memory.shape[0]
 
     vecs = [a.reshape(1, r) for a in (bq, bv, bo, ga, sa, bd, gb, sb)]
-    q, k, v, att, inv, g1, prob, g2, vec, ub, mem = attend_call(
-        count, sub, lengths, inputs, wq, wk, wv, wo, wu, wd, memory.T, bu.reshape(1, fr), vecs, mem_rows
+    out, dx, sums, tiny, _ = layer_call(
+        count, sub, mem_rows, lengths, inputs, cotangent, wq, wk, wv, wo, wu, wd, memory.T,
+        bu.reshape(1, fr), vecs,
     )
-    seqs, length = inputs.shape[:2]
-    layer_out, res, datt, part1, gvec, gub = feed_call(
-        inputs,
-        att.reshape(seqs, width, length),
-        cotangent,
-        g2.reshape((count,) + g2.shape[-2:]),
-        vec,
-        ub,
-        r,
-        fr,
-    )
-    dx, sums, tiny = pull_call(
-        count, sub, mem_rows, r, fr, inputs, mem, q, k, v, att, inv, prob, datt, res, g1,
-        part1.reshape(g2.shape), gvec, gub,
-    )
-    dx, gwq, gwk, gwv, gwo, gwu, gwd, gmem, gbu, *vecs = results_call(
-        r, fr, mem_rows, wu.shape[1], dx, sums, tiny
+    layer_out, dx, gwq, gwk, gwv, gwo, gwu, gwd, gmem, gbu, *vecs = results_call(
+        r, fr, mem_rows, wu.shape[1], out, dx, sums, tiny
     )
     gmem = gmem.T
     gbu = gbu.reshape(fr)

time: 175 us -> 166 us (0.949)
  Pallas kernels: 174 us -> 165 us
    pallas_call x3 -> x1, Pallas kernels: 170 us -> 160 us  [layer_call(): pl.pallas_call(functools.partial(layer_kernel, count, sub, mem_rows, r, f...]
where the time goes in v5:
time: 166 us
  Pallas kernels  165 us (99%)
    pallas_call x1, Pallas kernels, layer_call(): pl.pallas_call(functools.partial(layer_kernel, count, sub, mem_rows, r, f...  160 us
    pallas_call x1, Pallas kernels, results_call(): pl.pallas_call(functools.partial(results_kernel, r, fr, mem_rows), out_sh...  5.37 us

profile of v5, /device:TPU:0, one launch (start us, length us, event | category | flops | bytes accessed | tf_op | source)
XLA Modules:
  0.0 166.2 jit_solution(4138677124772043044)
XLA Ops:
  0.7 160.0 %layer.1 = (bf16[2,1024,512]{2,1,0:T(8,128)(2,1)}, bf16[2,1024,512]{2,1,0:T(8,128)(2,1)}, f32[192,512]{1,0:T(8,128)}, f32[16,128]{1,0:T(8,128)}, bf16[2,8,2,1056,512]{4,3,2,1,0:T(8,128)(2,1)}) custom-call(s32[2]{0:T(128)} %len_ref.1, bf16[2,1024,512]{2,1,0:T(8,128)(2,1)} %x_any.1, bf16[2,1024,512]{2,1,0:T(8,128)(2,1)} %dy_any.1, bf16[16,512]{1,0:T(8,128)(2,1)} %wq_ref.1, ...), custom_call_target="tpu_custom_call" | custom-call | tf_op jit(solution)/shard_map/layer/pallas_call | solution.py:955
  160.6 5.4 %results.1 = (bf16[2,1024,512]{2,1,0:T(8,128)(2,1)}, bf16[2,1024,512]{2,1,0:T(8,128)(2,1)}, f32[16,512]{1,0:T(8,128)}, f32[16,512]{1,0:T(8,128)}, f32[16,512]{1,...) custom-call(bf16[2,1024,512]{2,1,0:T(8,128)(2,1)} %get-tuple-element, ...), custom_call_target="tpu_custom_call" | custom-call | tf_op jit(solution)/shard_map/results/pallas_call | solution.py:1050

commit v6 on v5

--- a/solution.py
+++ b/solution.py
@@ -51,12 +51,12 @@
             to = to + (1 - 2 * self.bits[b]) * (2**b * self.sub)
         return (to,)
 
-    def barrier(self, routes):
+    def greet(self, routes):
         groups = sorted({flips for route in routes for group in route for flips in masks(group)})
         sem = pltpu.get_barrier_semaphore()
         for flips in groups:
             pl.semaphore_signal(sem, inc=1, device_id=self.partner(flips), device_id_type=MESH)
-        pl.semaphore_wait(sem, len(groups))
+        return len(groups)
 
     def own(self):
         return tuple(self.bits[b] for b in self.msb_first)
@@ -164,7 +164,7 @@
 
 
 def attend_part(
-    cube, mem_rows,
+    cube, mem_rows, greeted,
     len_ref, x_any, wq_ref, wk_ref, wv_ref, wo_ref, wu_ref, wd_ref, memt_ref, ub_ref, vec_refs,
     x_ref, q_o, k_o, v_o, att_o, inv_o, g1, g2, gs, vec_o, ub_o, mem_o, prob_any,
     qt_o, ksel, vt_s, score_a, score_b, prob_s, top_a, top_b, flat_s, wide_s,
@@ -186,8 +186,14 @@
     whole = (slice(None), slice(None))
     x_load = pltpu.make_async_copy(x_any, x_ref, x_sem)
     x_load.start()
-    for j, ref in enumerate((wq_ref, wk_ref, wv_ref)):
-        g1[own + (slice(j * r, j * r + r), slice(None))] = ref[...]
+    near = [
+        pltpu.make_async_copy(
+            ref, g1.at[own + (slice(j * r, j * r + r), slice(None))], local.at[2 + cols + j]
+        )
+        for j, ref in enumerate((wq_ref, wk_ref, wv_ref))
+    ]
+    for move in near:
+        move.start()
     wide_s[...] = jnp.zeros_like(wide_s)
     flat_s[...] = jnp.zeros_like(flat_s)
     for j, ref in enumerate(vec_refs):
@@ -207,7 +213,9 @@
     ]
     for move in moves:
         move.start()
-    cube.barrier([*ways, short(list(reversed(ways[0])))])
+    for move in near:
+        move.wait()
+    pl.semaphore_wait(pltpu.get_barrier_semaphore(), greeted)
 
     every_row = slice(None)
 
@@ -245,22 +253,22 @@
             copy.start()
     for move in moves:
         move.wait()
-    for step in range(1, steps):
-        for copies in sets:
-            for copy in copies(step - 1):
-                copy.wait()
-            for copy in copies(step):
+    def follow(n, step):
+        for copy in sets[n](step - 1):
+            copy.wait()
+        if step < steps:
+            for copy in sets[n](step):
                 copy.start()
+
+    for step in range(1, steps - 1):
+        for n in range(len(sets)):
+            follow(n, step)
         if step == 1:
             for c in range(chunks):
                 advance(c, 0)
-
-    def arrived(n):
-        for copy in sets[n](steps - 1):
-            copy.wait()
-
-    arrived(0)
-    arrived(1)
+    for step in (steps - 1, steps):
+        follow(0, step)
+        follow(1, step)
     x_load.wait()
 
     lane = lax.broadcasted_iota(jnp.int32, (1, 128), 1)
@@ -309,6 +317,7 @@
     for s in range(seqs):
         for h in range(HEADS):
             vt_s[s, h, 64:80, :] = ones
+    follow(2, steps - 1)
     mem = mem_o[...]
     mem_keys = dg(mem, weight(1), NN)
     mem_row = lax.broadcasted_iota(jnp.int32, (mem_pad, 1), 0)
@@ -330,7 +339,8 @@
         bias = jnp.where(row < len_ref[s], 0.0, HIDE)
         put_keys(s, rows, dg(x_ref[s, rows, :], weight(1), NN), bias)
 
-    arrived(2)
+    follow(3, steps - 1)
+    follow(2, steps)
     mem_values = dg(mem, weight(2), NN) + bv
     for s in range(seqs):
         put_values(s, slice(length, keys), mem_values)
@@ -340,7 +350,7 @@
         s, start, rows = place_rows(i)
         put_values(s, rows, dg(x_ref[s, rows, :], weight(2), NN) + bv)
 
-    arrived(3)
+    follow(3, steps)
     advance(0, 1)
     advance(1, 1)
 
@@ -458,7 +468,7 @@
 
 def feed_part(
     cube, r, fr,
-    x_all, att_all, dy_all, g2, vec, ub, out_all, out_any, res_all, datt_all, gvec, gub,
+    x_all, att_all, both_all, g2, vec, ub, out_any, res_all, datt_all, gvec, gub,
     act_s, slope_s, low_s, outer_s, branch_s, gwo, gwu, gwd, out_sem,
 ):
     nb = cube.nb
@@ -515,8 +525,8 @@
 
             def turn(self):
                 out, normed, inverse = norm_forward(self.outer, gb, sb)
-                out_all[seq, self.all, :] = out.astype(bf16)
-                dy = dy_all[seq, self.all, :].astype(f32)
+                dy = both_all[seq, self.all, :].astype(f32)
+                both_all[seq, self.all, :] = out.astype(bf16)
                 gvec[6:7, :] += col_sum(dy * normed)
                 gvec[7:8, :] += col_sum(dy)
                 self.d_hidden = norm_backward(dy, normed, inverse, gb)
@@ -572,7 +582,7 @@
     @pl.loop(0, steps)
     def _(i):
         feed_tile(i // tiles, (i % tiles) * rows)
-        tile_copy(i, rows, out_all, out_any, out_sem).start()
+        tile_copy(i, rows, both_all, out_any, out_sem).start()
 
     g2[every + (slice(0, r), slice(None))] = gwo[...].astype(bf16).reshape((2,) * nb + (r, width))
     for c in range(cols):
@@ -779,6 +789,8 @@
         up = jnp.broadcast_to(gub_ref[:, i * fr - off : i * fr - off + 128], (8, 128))
         up = pltpu.roll(up, (64 - off) % 128, 1)
         small_s[at + (slice(0, 1), slice(64, 64 + fr))] = up[0:1, 64 : 64 + fr]
+    finish(heads[3:], 0)
+    start(heads[3:], 1)
     start([smalls], 0)
     tile = 512
     tiles = length // tile
@@ -797,27 +809,36 @@
 
     todo = list(range(seqs * tiles))
     outs = []
-    group = heads[3:] + [smalls]
-    for step in range(len(brief)):
+
+    def some():
         if todo:
             outs.append(inputs(todo.pop(0)))
-        finish(group, step)
-        if step + 1 < len(brief):
-            start(group, step + 1)
-        if step == 0:
-            finish(heads[2:3], 1)
-            start(heads[2:3], 2)
-            finish(feeds, steps - 1)
-            for part in feeds:
-                total(part, 3 * r, sums_o.shape[0])
-        if step == 1:
-            finish(heads[2:3], 2)
-            start(heads[2:3], 3)
-            finish(heads[:2], steps - 1)
+
+    def follow(part, step):
+        finish([part], step)
+        if step + 1 < part.steps:
+            start([part], step + 1)
+
+    follow(heads[2], 1)
+    some()
+    follow(smalls, 0)
+    finish(feeds, steps - 1)
+    for part in feeds:
+        total(part, 3 * r, sums_o.shape[0])
+    for step in range(1, len(brief) - 1):
+        follow(heads[3], step)
+        some()
+        follow(smalls, step)
+    follow(heads[2], 2)
+    some()
+    finish(heads[:2], steps - 1)
+    for part in heads[:2]:
+        total(part, 0, 3 * r)
     for i in todo:
         outs.append(inputs(i))
-    finish(heads[2:3], 3)
-    for part in heads:
+    finish(heads[2:3], steps - 1)
+    finish([heads[3], smalls], len(brief) - 1)
+    for part in heads[2:]:
         total(part, 0, 3 * r)
     small_o[...] = smalls.total(smalls.steps - 1)
     for out in outs:
@@ -830,15 +851,19 @@
 ):
     vec_refs, rest = rest[:8], rest[8:]
     (out_any, dx_any, sums_o, small_o, prob_any), rest = rest[:5], rest[5:]
-    (x_ref, q_o, k_o, v_o, att_o, inv_o, g1, g2, gs, vec_o, ub_o, mem_o, gvec, gub), rest = rest[:14], rest[14:]
+    held, rest = rest[:15], rest[15:]
+    (x_ref, dy_ref, q_o, k_o, v_o, att_o, inv_o, g1, g2, gs, vec_o, ub_o, mem_o, gvec, gub) = held
     (bufs, sems1, feed_sem, dy_sem, load_sem, sems3) = rest
     cube = Cube(count, sub)
     early, late, feed, pull = layout
-    dy_load = []
+    ways = routes(cube.nb)
+    greeted = cube.greet([*ways, short(list(reversed(ways[0])))])
+    dy_load = pltpu.make_async_copy(dy_any, dy_ref, dy_sem)
+    dy_load.start()
 
     def attend(*scoped):
         attend_part(
-            cube, mem_rows,
+            cube, mem_rows, greeted,
             len_ref, x_any, wq_ref, wk_ref, wv_ref, wo_ref, wu_ref, wd_ref, memt_ref, ub_ref,
             vec_refs,
             x_ref, q_o, k_o, v_o, att_o, inv_o, g1, g2, gs, vec_o, ub_o, mem_o, prob_any,
@@ -847,17 +872,15 @@
 
     pl.run_scoped(attend, *early)
 
-    def others(out_s, res_s, datt_s, part2, small_s, prob_s):
+    def others(res_s, datt_s, part2, small_s, prob_s):
         seqs = x_ref.shape[0]
         prob_load(0, seqs, prob_any, prob_s, load_sem).start()
 
-        def forward(dy_s, *scoped):
-            load = pltpu.make_async_copy(dy_any, dy_s, dy_sem)
-            load.start()
-            load.wait()
+        def forward(*scoped):
+            dy_load.wait()
             feed_part(
                 cube, r, fr,
-                x_ref, att_o, dy_s, g2, vec_o, ub_o, out_s, out_any, res_s, datt_s, gvec, gub,
+                x_ref, att_o, dy_ref, g2, vec_o, ub_o, out_any, res_s, datt_s, gvec, gub,
                 *scoped, feed_sem,
             )
 
@@ -872,9 +895,9 @@
             )
 
         pl.run_scoped(backward, *pull)
-        tile = feed[3].shape[0]
+        tile = feed[2].shape[0]
         for i in range(feed_sem.shape[0]):
-            tile_copy(i, tile, out_s, out_any, feed_sem).wait()
+            tile_copy(i, tile, dy_ref, out_any, feed_sem).wait()
 
     pl.run_scoped(others, *late)
 
@@ -911,7 +934,6 @@
         VMEM((128, 128), f32),
     )
     late = (
-        VMEM(x.shape, bf16),
         VMEM(x.shape, f32),
         VMEM((seqs, pairs, length, 128), bf16),
         VMEM(cube + (3 * r, width), bf16),
@@ -919,7 +941,6 @@
         VMEM((2, 2, length // block, keys, block), bf16),
     )
     feed = (
-        VMEM(x.shape, bf16),
         [VMEM((tile, width), bf16)] * (ff // width),
         [VMEM((tile, width), bf16)] * (ff // width),
         VMEM((tile, width), bf16),
@@ -961,9 +982,10 @@
             shape((16, 128), f32),
             shape((seqs, HEADS, length // block, keys, block), bf16),
         ),
-        in_specs=[pl.BlockSpec(memory_space=pltpu.SMEM), hbm, hbm] + [vm] * 16,
+        in_specs=[pl.BlockSpec(memory_space=pltpu.SMEM)] + [hbm] * 8 + [vm] * 10,
         out_specs=[hbm, hbm, vm, vm, hbm],
         scratch_shapes=[
+            VMEM(x.shape, bf16),
             VMEM(x.shape, bf16),
             VMEM((seqs, pairs, 128, length), bf16),
             VMEM((seqs, pairs, 128, keys), bf16),
@@ -980,7 +1002,7 @@
             VMEM((1, ff), f32),
             bufs,
             [
-                dma((2 + ff // width,)),
+                dma((5 + ff // width,)),
                 dma,
                 dma((2, 2)),
                 dma((6,) + links),
@@ -1002,22 +1024,31 @@
     )(lengths, x, dy, wq, wk, wv, wo, wu, wd, memt, ub, *vecs)
 
 
-def results_kernel(r, fr, mem_rows, out_any, dx_any, sums, small, out_o, dx_o, *outs):
-    outs, (hold, load_sem, save_sem) = outs[:-3], outs[-3:]
-    seqs, length = out_any.shape[:2]
-    cut = length // 2
+def results_kernel(r, fr, mem_rows, out_any, dx_any, sums_any, small_any, out_o, dx_o, *rest):
+    outs, (sums, small, hold, first_sem, load_sem, save_sem, *kept, kept_sem) = rest[:16], rest[16:]
+    length = out_any.shape[1]
+    pieces = hold.shape[0] // (2 * out_any.shape[0])
+    cut = length // pieces
+    firsts = [
+        pltpu.make_async_copy(a, b, first_sem.at[n])
+        for n, (a, b) in enumerate(((sums_any, sums), (small_any, small)))
+    ]
+    for move in firsts:
+        move.start()
     jobs = []
-    for n, (src, dst) in enumerate(((out_any, out_o), (dx_any, dx_o))):
-        for s in range(seqs):
-            for c in range(length // cut):
+    for src, dst in ((out_any, out_o), (dx_any, dx_o)):
+        for s in range(out_any.shape[0]):
+            for c in range(pieces):
                 at = (s, slice(c * cut, (c + 1) * cut))
                 k = len(jobs)
                 load = pltpu.make_async_copy(src.at[at], hold.at[k], load_sem.at[k])
                 jobs.append((load, pltpu.make_async_copy(hold.at[k], dst.at[at], save_sem.at[k])))
     for load, _ in jobs:
         load.start()
-    gq, gk, gv, go, gu, gd, gm, gb = outs[:8]
-    vecs = outs[8:]
+    for move in firsts:
+        move.wait()
+    gq, gk, gv, go, gu, gd, gm, gb = kept[:8]
+    vecs = kept[8:]
     width = gq.shape[1]
     cols = gu.shape[1] // width
     for n, ref in enumerate((gq, gk, gv, go)):
@@ -1031,10 +1062,16 @@
     for n, ref in enumerate(vecs):
         ref[...] = turned[VEC + n : VEC + n + 1, 0:r]
     gb[...] = value[0:1, 64 : 64 + fr]
+    saves = [
+        pltpu.make_async_copy(a, b, kept_sem.at[n])
+        for n, (a, b) in enumerate(zip(kept, outs, strict=True))
+    ]
+    for save in saves:
+        save.start()
     for load, save in jobs:
         load.wait()
         save.start()
-    for _, save in jobs:
+    for save in saves + [save for _, save in jobs]:
         save.wait()
 
 
@@ -1042,21 +1079,25 @@
     width = sums.shape[1]
     seqs, length = dx.shape[:2]
     shape = jax.ShapeDtypeStruct
-    vm = pl.BlockSpec(memory_space=VMEM)
     hbm = pl.BlockSpec(memory_space=pl.ANY)
-    mats = [(r, width)] * 4 + [(r, ff), (fr, width), (mem_rows, r), (1, fr)] + [(1, r)] * 8
-    mats[6] = (r, mem_rows)
-    jobs = 4 * seqs
+    dma = pltpu.SemaphoreType.DMA
+    mats = [(r, width)] * 4 + [(r, ff), (fr, width), (r, mem_rows), (1, fr)] + [(1, r)] * 8
+    jobs = 8 * seqs
     return pl.pallas_call(
         functools.partial(results_kernel, r, fr, mem_rows),
         out_shape=(shape(out.shape, out.dtype), shape(dx.shape, dx.dtype))
         + tuple(shape(m, f32) for m in mats),
-        in_specs=[hbm, hbm, vm, vm],
-        out_specs=[hbm, hbm] + [vm] * len(mats),
+        in_specs=[hbm] * 4,
+        out_specs=[hbm] * (2 + len(mats)),
         scratch_shapes=[
-            VMEM((jobs, length // 2, width), bf16),
-            pltpu.SemaphoreType.DMA((jobs,)),
-            pltpu.SemaphoreType.DMA((jobs,)),
+            VMEM(sums.shape, f32),
+            VMEM(small.shape, f32),
+            VMEM((jobs, 2 * seqs * length // jobs, width), bf16),
+            dma((2,)),
+            dma((jobs,)),
+            dma((jobs,)),
+            *[VMEM(m, f32) for m in mats],
+            dma((len(mats),)),
         ],
         compiler_params=pltpu.CompilerParams(vmem_limit_bytes=60 * 2**20),
         name="results",

time: 166 us -> 161 us (0.970)
  Pallas kernels: 165 us -> 160 us
    pallas_call x1, Pallas kernels: 160 us -> 155 us  [layer_call(): pl.pallas_call(functools.partial(layer_kernel, count, sub, mem_rows, r, f...]
where the time goes in v6:
time: 161 us
  Pallas kernels  160 us (99%)
    pallas_call x1, Pallas kernels, layer_call(): pl.pallas_call(functools.partial(layer_kernel, count, sub, mem_rows, r, f...  155 us
    pallas_call x1, Pallas kernels, results_call(): pl.pallas_call(functools.partial(results_kernel, r, fr, mem_rows), out_sh...  4.72 us

profile of v6, /device:TPU:0, one launch (start us, length us, event | category | flops | bytes accessed | tf_op | source)
XLA Modules:
  0.0 160.5 jit_solution(15861095819625165464)
XLA Ops:
  0.7 155.0 %layer.1 = (bf16[2,1024,512]{2,1,0:T(8,128)(2,1)}, bf16[2,1024,512]{2,1,0:T(8,128)(2,1)}, f32[192,512]{1,0:T(8,128)}, f32[16,128]{1,0:T(8,128)}, bf16[2,8,2,1056,512]{4,3,2,1,0:T(8,128)(2,1)}) custom-call(s32[2]{0:T(128)} %len_ref.1, bf16[2,1024,512]{2,1,0:T(8,128)(2,1)} %x_any.1, bf16[2,1024,512]{2,1,0:T(8,128)(2,1)} %dy_any.1, bf16[16,512]{1,0:T(8,128)(2,1)} %wq_ref.1, ...), custom_call_target="tpu_custom_call" | custom-call | tf_op jit(solution)/shard_map/layer/pallas_call | solution.py:976
  155.6 4.7 %results.1 = (bf16[2,1024,512]{2,1,0:T(8,128)(2,1)}, bf16[2,1024,512]{2,1,0:T(8,128)(2,1)}, f32[16,512]{1,0:T(8,128)}, f32[16,512]{1,0:T(8,128)}, f32[16,512]{1,...) custom-call(bf16[2,1024,512]{2,1,0:T(8,128)(2,1)} %get-tuple-element, ...), custom_call_target="tpu_custom_call" | custom-call | tf_op jit(solution)/shard_map/results/pallas_call | solution.py:1086
